TPU v7x, 256 devices: a whole 4x4x8 slice. The times are simulated.
256 devices in a mesh: visit: 16 (over y, x_lo, core), row: 16 (over z, x_hi).
Axes of the slice: x: 4 (x_hi: 2, x_lo: 2; x = x_hi * 2 + x_lo), y: 4, z: 8, core: 2. Of those that a mesh axis runs over, the one named last changes fastest.
Arguments:
- science: float32 [16, 512, 4096], P('visit', 'row'), may hold values from -8 to 8
- basis_kernels: float32 [9, 21, 21], replicated, may hold values from -0.25 to 0.25
- basis_coeffs: float32 [16, 9], P('visit'), may hold values from -2 to 2
- row_starts: int32 [16, 512], P('visit', 'row'), may hold values from -7 to 1
- row_taps: float32 [16, 8, 512], P('visit', None, 'row'), may hold values from -0.2 to 0.45
- col_offsets: int32 [16], P('visit'), may hold values from 0 to 511
- col_starts: int32 [16, 4096], P('visit'), may hold values from -3 to -2
- col_taps: float32 [16, 8, 4096], P('visit'), may hold values from -0.2 to 0.45
- visit_weights: float32 [16], P('visit'), may hold values from 0.25 to 4
- clip_masks: int32 [16, 512, 4096], P('visit', 'row'), may hold values 0 or 1
- decorrelation: float32 [16, 21, 21], P('visit'), may hold values from -0.25 to 0.25
Outputs:
- decorrelated: float32 [16, 512, 4096], P('visit', 'row')
- template: float32 [512, 4096], P('row', 'visit')
Inputs may be any that keep to these rules, and one draw needn't show every extreme that they name: Row i of a visit reads matched rows i + row_starts[v, i] to i + row_starts[v, i] + 7.
All inputs are finite; a program needn't handle non-finite values. No bound on the sum of `clip_masks` on one device may be relied on, other than what follows from the above.
Results may differ from a plain program's by a relative error of at most 0.0003.
Values sent between devices are 32-bit elements; how exact they have to be, the bound alone decides.
No kernel may reach another device: no remote copies, remote signals or barrier semaphores. Data moves between devices by JAX's collectives and lax.ppermute only.
A program may use at most 64 MiB of HBM per device.

v0:
```python
import jax
import jax.numpy as jnp
from jax import lax
from jax.experimental import pallas as pl
from jax.experimental.pallas import tpu as pltpu
from jax.sharding import PartitionSpec as P

KS = 21
HALF = KS // 2
TAPS = 8
ROWS = 32
COLS = 4096
BAND = 80
BASE = 24
LEAD = 6
CHUNK = 1024
BLOCK = 256
GROUP = 3
STEPS = KS // GROUP
FRAME = COLS + 128
LEFT = 640
F32 = jnp.float32
BF16 = jnp.bfloat16
VMEM_LIMIT = 48 * 1024 * 1024

VM = pl.BlockSpec(memory_space=pltpu.VMEM)
SM = pl.BlockSpec(memory_space=pltpu.SMEM)


def call(kernel, outs, ins, scratch=(), cost=None):
    return pl.pallas_call(
        kernel,
        out_shape=outs,
        in_specs=ins,
        out_specs=jax.tree.map(lambda _: VM, outs),
        scratch_shapes=list(scratch),
        compiler_params=pltpu.CompilerParams(vmem_limit_bytes=VMEM_LIMIT),
        cost_estimate=cost,
    )


def sds(*shape, dtype=F32):
    return jax.ShapeDtypeStruct(shape, dtype)


def pack_kernel(source_ref, up_ref, down_ref, x_ref, sem):
    fetch = pltpu.make_async_copy(source_ref, x_ref, sem)
    fetch.start()
    fetch.wait()
    for q in range(4):
        cols = pl.ds(q * CHUNK, CHUNK)
        down_ref[16 * q : 16 * q + 16, :] = x_ref[16:32, cols]
        up_ref[16 * q : 16 * q + 16, :] = x_ref[0:16, cols]
        down_ref[64 + q : 65 + q, :] = x_ref[15:16, cols]
        down_ref[68 + q : 69 + q, :] = jnp.zeros((1, CHUNK), F32)
        up_ref[64 + q : 65 + q, :] = x_ref[16:17, cols]
        up_ref[68 + q : 69 + q, :] = x_ref[17:18, cols]


def split_bands(values):
    lanes = lax.broadcasted_iota(jnp.int32, values.shape, 1)
    high = values.astype(BF16).astype(F32)
    return jnp.where(lanes < 2 * BAND, high, values - high).astype(BF16)


def bands_kernel(k1_ref, k2_ref, mix_ref, a1_ref, a2_ref):
    mix = mix_ref[...]
    for lag in range(KS):
        first = jnp.broadcast_to(k1_ref[lag : lag + 1, :], (48, 256))
        first = pltpu.roll(first, 0, 1, stride=1, stride_axis=0)
        merged = jnp.dot(
            mix, first, precision=lax.Precision.HIGHEST, preferred_element_type=F32
        )
        step, part = lag // GROUP, lag % GROUP
        rows, lanes = pl.ds(ROWS * step, ROWS), pl.ds(256 * part, 256)
        a1_ref[rows, lanes] = split_bands(merged)
        second = jnp.broadcast_to(k2_ref[lag : lag + 1, :], (ROWS, 256))
        second = pltpu.roll(second, 8, 1, stride=1, stride_axis=0)
        a2_ref[rows, lanes] = split_bands(second)


def coverage(starts, offset, q):
    column = lax.broadcasted_iota(jnp.int32, starts.shape, 1) + q * CHUNK
    actual = column - offset + starts
    return ((actual >= 0) & (actual <= COLS - TAPS)).astype(F32)


def put_blocks(ref, values, place_ref, q):
    core = place_ref[1]
    pair = place_ref[2]
    for j in range(4):
        ref[(j % 2) ^ core, (j // 2) ^ pair, q] = values[:, j * BLOCK : (j + 1) * BLOCK]


def share_kernel(place_ref, weight_ref, mask_ref, starts_ref, share_ref):
    for q in range(4):
        cols = pl.ds(q * CHUNK, CHUNK)
        covered = coverage(starts_ref[:, cols], place_ref[0], q)
        share = weight_ref[0] * mask_ref[:, cols].astype(F32) * covered
        put_blocks(share_ref, share, place_ref, q)


def put_rows(frame_ref, row, values, valid=None):
    count = values.shape[0]
    if valid is not None:
        values = jnp.where(valid, values, 0.0)
    framed = jnp.concatenate([values, jnp.zeros((count, 128), F32)], axis=1)
    frame_ref[row : row + count, :] = pltpu.roll(framed, HALF, 1)


def wide(ref, rows):
    return jnp.concatenate([ref[rows * q : rows * (q + 1), :] for q in range(4)], axis=1)


def thin(ref, at):
    return jnp.concatenate([ref[at + q : at + q + 1, :] for q in range(4)], axis=1)


def split_rows(frame_ref, halves_ref):
    frame = frame_ref[...]
    for part in range(GROUP):
        moved = pltpu.roll(frame, FRAME - part, 1) if part else frame
        high = moved.astype(BF16)
        at = 256 * part
        halves_ref[at : at + BAND, :] = high
        halves_ref[at + BAND : at + 2 * BAND, :] = (moved - high.astype(F32)).astype(BF16)
        halves_ref[at + 2 * BAND : at + 3 * BAND, :] = high
        halves_ref[at + 3 * BAND : at + 256, :] = jnp.zeros((256 - 3 * BAND, FRAME), BF16)


def correlate_chunk(band_ref, halves_ref, q):
    width = CHUNK + 128
    lags = jnp.dot(
        band_ref[...],
        halves_ref[:, q * CHUNK : q * CHUNK + width],
        preferred_element_type=F32,
    )
    total = lags[0:ROWS, :CHUNK]
    for step in range(1, STEPS):
        moved = pltpu.roll(lags[ROWS * step : ROWS * (step + 1), :], width - GROUP * step, 1)
        total = total + moved[:, :CHUNK]
    return total


def warp_kernel(
    place_ref,
    weight_ref,
    own_ref,
    above_ref,
    below_ref,
    band_ref,
    starts_ref,
    taps_ref,
    mask_ref,
    after_ref,
    warped_ref,
    weighted_ref,
    frame_ref,
    halves_ref,
    source_ref,
):
    band = place_ref[3]
    has_above, has_below = band > 0, band < 15
    put_rows(frame_ref, BASE, own_ref[...])
    put_rows(frame_ref, BASE - 16, wide(above_ref, 16), has_above)
    put_rows(frame_ref, BASE + ROWS, wide(below_ref, 16), has_below)
    frame_ref[0:8, :] = jnp.zeros((8, FRAME), F32)
    frame_ref[BAND - 8 : BAND, :] = jnp.zeros((8, FRAME), F32)
    put_rows(frame_ref, BASE - 17, thin(above_ref, 64), has_above)
    put_rows(frame_ref, BASE + 48, thin(below_ref, 64), has_below)
    put_rows(frame_ref, BASE + 49, thin(below_ref, 68), has_below)
    split_rows(frame_ref, halves_ref)

    source_ref[:, 0:LEFT] = jnp.zeros((ROWS, LEFT), F32)
    source_ref[:, LEFT + COLS : LEFT + COLS + 128] = jnp.zeros((ROWS, 128), F32)
    for q in range(4):
        source_ref[:, LEFT + q * CHUNK : LEFT + (q + 1) * CHUNK] = correlate_chunk(
            band_ref, halves_ref, q
        )

    offset = place_ref[0]
    first = LEFT - 3 - offset
    aligned = first // 128
    rest = first - aligned * 128
    width = CHUNK + 256
    for q in range(4):
        cols = pl.ds(q * CHUNK, CHUNK)
        at = pl.multiple_of((aligned + q * (CHUNK // 128)) * 128, 128)
        moved = pltpu.roll(source_ref[:, pl.ds(at, width)], width - rest, 1)
        starts = starts_ref[:, cols]
        early = starts == -3
        taps = [taps_ref[t : t + 1, cols] for t in range(TAPS)]
        zero = jnp.zeros_like(taps[0])
        total = None
        for lag in range(TAPS + 1):
            tap = jnp.where(
                early, taps[lag] if lag < TAPS else zero, taps[lag - 1] if lag else zero
            )
            part = moved if lag == 0 else pltpu.roll(moved, width - lag, 1)
            term = tap * part[:, :CHUNK]
            total = term if total is None else total + term
        warped_ref[:, cols] = total
        share = weight_ref[0] * mask_ref[:, cols].astype(F32) * coverage(starts, offset, q)
        put_blocks(weighted_ref, share * total, place_ref, q)


def differ_kernel(place_ref, own_ref, mine_ref, other_ref, diff_ref, up_ref, down_ref):
    core = place_ref[1]
    pair = place_ref[2]
    for b in range(16):
        cols = pl.ds(b * BLOCK, BLOCK)
        at = ((b // 2) % 2) ^ pair
        coadd = jnp.where(core == b % 2, mine_ref[at, b // 4], other_ref[at, b // 4])
        diff_ref[:, cols] = own_ref[:, cols] - coadd
    for q in range(4):
        cols = pl.ds(q * CHUNK, CHUNK)
        down_ref[8 * q : 8 * q + 8, :] = diff_ref[24:32, cols]
        up_ref[8 * q : 8 * q + 8, :] = diff_ref[0:8, cols]
        for extra in range(2):
            at = 32 + 4 * extra + q
            down_ref[at : at + 1, :] = diff_ref[22 + extra : 23 + extra, cols]
            up_ref[at : at + 1, :] = diff_ref[8 + extra : 9 + extra, cols]


def clean_kernel(
    place_ref, own_ref, above_ref, below_ref, band_ref, out_ref, frame_ref, halves_ref
):
    band = place_ref[3]
    has_above, has_below = band > 0, band < 15
    frame_ref[0:16, :] = jnp.zeros((16, FRAME), F32)
    frame_ref[BAND - 16 : BAND, :] = jnp.zeros((16, FRAME), F32)
    put_rows(frame_ref, BASE, own_ref[...])
    put_rows(frame_ref, BASE - 8, wide(above_ref, 8), has_above)
    put_rows(frame_ref, BASE + ROWS, wide(below_ref, 8), has_below)
    for extra in range(2):
        put_rows(frame_ref, BASE - 10 + extra, thin(above_ref, 32 + 4 * extra), has_above)
        put_rows(frame_ref, BASE + 40 + extra, thin(below_ref, 32 + 4 * extra), has_below)
    split_rows(frame_ref, halves_ref)
    for q in range(4):
        out_ref[:, q * CHUNK : (q + 1) * CHUNK] = correlate_chunk(band_ref, halves_ref, q)


def three_places(kernel):
    span = jnp.pad(kernel.T, ((0, 3), (LEAD, BAND - LEAD - KS)))
    return jnp.pad(jnp.concatenate([span] * 3, axis=1), ((0, 0), (0, 256 - 3 * BAND)))


def swap(values, step):
    return lax.ppermute(values, "visit", [(i, i ^ step) for i in range(16)])


RING_A = [(i, (i // 4 ^ 1) * 4 + i % 4) for i in range(16)]
RING_B = [(i, (3 - i // 4) * 4 + i % 4) for i in range(16)]


def over_y(part):
    part = part + lax.ppermute(part, "visit", RING_A)
    return part + lax.ppermute(part, "visit", RING_B)


def over_visits(blocks):
    half = blocks[0] + swap(blocks[1], 1)
    return over_y(half[0] + swap(half[1], 2))


def to_next(values):
    return lax.ppermute(values, "row", [(i, (i + 1) % 16) for i in range(16)])


def to_previous(values):
    return lax.ppermute(values, "row", [((i + 1) % 16, i) for i in range(16)])


def on_device(
    science,
    basis_kernels,
    basis_coeffs,
    row_starts,
    row_taps,
    col_offsets,
    col_starts,
    col_taps,
    visit_weights,
    clip_masks,
    decorrelation,
):
    pixels = science[0]
    visit = lax.axis_index("visit")
    band = lax.axis_index("row")
    band_at = band * ROWS
    place = jnp.stack([col_offsets[0], visit % 2, (visit // 2) % 2, band]).astype(jnp.int32)

    up, down = call(
        pack_kernel,
        (sds(72, CHUNK), sds(72, CHUNK)),
        [pl.BlockSpec(memory_space=pl.ANY)],
        [pltpu.VMEM((ROWS, COLS), F32), pltpu.SemaphoreType.DMA],
    )(pixels)
    above = to_next(down)
    below = to_previous(up)

    kernel = jnp.einsum(
        "b,bij->ij", basis_coeffs[0], basis_kernels, precision=lax.Precision.HIGHEST
    )
    matched_row = jnp.arange(48, dtype=jnp.int32)[None, :] - 8
    tap_at = matched_row - (jnp.arange(ROWS, dtype=jnp.int32) + row_starts[0])[:, None]
    inside = (matched_row + band_at >= 0) & (matched_row + band_at < 16 * ROWS)
    hits = tap_at[None] == jnp.arange(TAPS, dtype=jnp.int32)[:, None, None]
    mix = jnp.sum(jnp.where(hits & inside[None], row_taps[0][:, :, None], 0.0), axis=0)
    first_bands, second_bands = call(
        bands_kernel, (sds(STEPS * ROWS, GROUP * 256, dtype=BF16),) * 2, [VM] * 3
    )(three_places(kernel), three_places(decorrelation[0]), mix)

    shares = call(share_kernel, sds(2, 2, 4, ROWS, BLOCK), [SM, SM, VM, VM])(
        place, visit_weights, clip_masks[0], col_starts
    )
    shares = over_y(shares[0] + swap(shares[1], 1))
    denominator = jnp.maximum(shares[0] + swap(shares[1], 2), 1.0)

    frames = [
        pltpu.VMEM((BAND, FRAME), F32),
        pltpu.VMEM((GROUP * 256, FRAME), BF16),
    ]
    warped, weighted = call(
        warp_kernel,
        (sds(ROWS, COLS), sds(2, 2, 4, ROWS, BLOCK)),
        [SM, SM] + [VM] * 7 + [pl.BlockSpec(memory_space=pl.ANY)],
        frames + [pltpu.VMEM((ROWS, LEFT + COLS + 128), F32)],
    )(
        place,
        visit_weights,
        pixels,
        above,
        below,
        first_bands,
        col_starts,
        col_taps[0],
        clip_masks[0],
        shares,
    )
    weighted, denominator = lax.optimization_barrier((weighted, denominator))
    coadd = over_visits(weighted) / denominator
    template = lax.dynamic_index_in_dim(coadd, visit // 4, 0, keepdims=False)
    mine = jnp.stack([coadd, swap(coadd, 2)])
    other = swap(mine, 1)
    difference, up, down = call(
        differ_kernel,
        (sds(ROWS, COLS), sds(40, CHUNK), sds(40, CHUNK)),
        [SM] + [VM] * 3,
    )(place, warped, mine, other)
    cleaned = call(clean_kernel, sds(ROWS, COLS), [SM] + [VM] * 4, frames)(
        place, difference, to_next(down), to_previous(up), second_bands
    )
    return cleaned[None], template


def solution(mesh):
    return jax.shard_map(
        on_device,
        mesh=mesh,
        in_specs=(
            P("visit", "row", None),
            P(),
            P("visit", None),
            P("visit", "row"),
            P("visit", None, "row"),
            P("visit"),
            P("visit", None),
            P("visit", None, None),
            P("visit"),
            P("visit", "row", None),
            P("visit", None, None),
        ),
        out_specs=(P("visit", "row", None), P("row", "visit")),
        check_vma=False,
    )
```

profile of v0, /device:TPU:1, one launch (start us, length us, event | category | flops | bytes accessed | tf_op | source)
XLA Modules:
  0.0 79.1 jit_solution(14801790916332918445)
XLA Ops:
  0.6 0.0 copy-start
  2.0 0.1 pad_add_fusion.place_ref
  2.1 1.0 %copy-done.1 = s32[1,32,4096]{2,1,0:T(8,128)S(1)} copy-done((s32[1,32,4096]{2,1,0:T(8,128)S(1)}, s32[1,32,4096]{2,1,0:T(8,128)}, u32[]{:S(2)}) %copy-start.1) | copy-done | bytes 524312
  3.1 0.7 shard_map.124
  3.8 0.0 copy-start.3
  3.8 3.3 %collective-permute-start.2 = (f32[2,4,32,256]{3,2,1,0:T(8,128)S(1)}, f32[2,4,32,256]{3,2,1,0:T(8,128)S(1)}, u32[]{:S(2)}, u32[]{:S(2)}) collective-permute-start(f32[2,4,32,256]{3,2,1,0:T(8,128)S(1)} %slice_bitcast_fusion), channel_id=1, source_target_pairs={{0,16},{16,0},{32,48},{48,32},{64,80},{80,64},{96,112},{112,96},{1... | collective-permute-start | bytes 786440 | tf_op jit(solution)/shard_map/ppermute | solution.py:249
  7.2 0.1 shard_map.122
  7.3 1.3 %collective-permute-start = (f32[72,1024]{1,0:T(8,128)S(1)}, f32[72,1024]{1,0:T(8,128)S(1)}, u32[]{:S(2)}, u32[]{:S(2)}) collective-permute-start(f32[72,1024]{1,0:T(8,128)S(1)} %get-tuple-element.13), channel_id=1, source_target_pairs={{0,1},{1,2},{2,3},{3,4},{4,5},{5,6},{6,7},{7,8},{8,9},{9,10},{10,1... | collective-permute-start | bytes 884744 | tf_op jit(solution)/shard_map/ppermute | solution.py:267
  8.6 5.4 %collective-permute-start.1 = (f32[72,1024]{1,0:T(8,128)S(1)}, f32[72,1024]{1,0:T(8,128)S(1)}, u32[]{:S(2)}, u32[]{:S(2)}) collective-permute-start(f32[72,1024]{1,0:T(8,128)S(1)} %get-tuple-element.14), channel_id=1, source_target_pairs={{1,0},{2,1},{3,2},{4,3},{5,4},{6,5},{7,6},{8,7},{9,8},{10,9},{11,1... | collective-permute-start | bytes 884744 | tf_op jit(solution)/shard_map/ppermute | solution.py:271
  14.0 0.1 copy.14
  14.1 0.2 fusion.1
  14.3 0.1 copy.16
  14.4 0.1 pad.16
  14.5 0.1 pad.14
  14.6 0.0 collective-permute-done.2
  14.6 0.0 copy-start.9
  14.6 1.4 %collective-permute-start.3 = (f32[2,4,32,256]{3,2,1,0:T(8,128)S(1)}, f32[2,4,32,256]{3,2,1,0:T(8,128)S(1)}, u32[]{:S(2)}, u32[]{:S(2)}) collective-permute-start(f32[2,4,32,256]{3,2,1,0:T(8,128)S(1)} %fusion), channel_id=1, source_target_pairs={{0,64},{16,80},{32,96},{48,112},{64,0},{80,16},{96,32},{112,48},{1... | collective-permute-start | bytes 786440 | tf_op jit(solution)/shard_map/ppermute | solution.py:257
  16.0 0.1 select_maximum_fusion
  16.1 5.4 %collective-permute-done.3 = f32[2,4,32,256]{3,2,1,0:T(8,128)S(1)} collective-permute-done((f32[2,4,32,256]{3,2,1,0:T(8,128)S(1)}, f32[2,4,32,256]{3,2,1,0:T(8,128)S(1)}, u32[]{:S(2)}, u32[]{:S(2)}) %collective-permute-start.3) | collective-permute-done | bytes 262176 | tf_op jit(solution)/shard_map/ppermute | solution.py:257
  21.6 2.8 %collective-permute-start.4 = (f32[2,4,32,256]{3,2,1,0:T(8,128)S(1)}, f32[2,4,32,256]{3,2,1,0:T(8,128)S(1)}, u32[]{:S(2)}, u32[]{:S(2)}) collective-permute-start(f32[2,4,32,256]{3,2,1,0:T(8,128)S(1)} %add.83), channel_id=1, source_target_pairs={{0,192},{16,208},{32,224},{48,240},{64,128},{80,144},{96,160},{112... | collective-permute-start | bytes 786440 | tf_op jit(solution)/shard_map/ppermute | solution.py:258
  24.4 0.1 broadcast_subtract_fusion
  24.5 4.5 %collective-permute-done.4 = f32[2,4,32,256]{3,2,1,0:T(8,128)S(1)} collective-permute-done((f32[2,4,32,256]{3,2,1,0:T(8,128)S(1)}, f32[2,4,32,256]{3,2,1,0:T(8,128)S(1)}, u32[]{:S(2)}, u32[]{:S(2)}) %collective-permute-start.4) | collective-permute-done | bytes 262176 | tf_op jit(solution)/shard_map/ppermute | solution.py:258
  29.0 0.0 copy-start.7
  29.0 0.0 copy-start.4
  29.1 0.4 collective-permute-start.5
  29.5 0.2 copy-done.7
  29.7 0.1 select_reduce_fusion.mix_ref
  29.8 0.8 %shard_map.123 = (bf16[224,768]{1,0:T(8,128)(2,1)S(1)}, bf16[224,768]{1,0:T(8,128)(2,1)S(1)}) custom-call(f32[24,256]{1,0:T(8,128)S(1)} %get-tuple-element.25.k1_ref, f32[24,256]{1,0:T(8,128)S(1)} %get-tuple-element.24.k2_ref, f32[32,48]{1,0:T(8,128)S(1)} %select_reduce_fusion.mix_ref), custom_call_target="tpu_custom_call" | custom-call | tf_op jit(solution)/shard_map/pallas_call | solution.py:310
  30.7 5.3 %shard_map.125 = (f32[32,4096]{1,0:T(8,128)S(1)}, f32[2,2,4,32,256]{4,3,2,1,0:T(8,128)S(1)}) custom-call(s32[4]{0:T(128)S(1)} %pad_add_fusion.place_ref, f32[1]{0:T(128)S(6)} %copy.20.weight_ref, f32[32,4096]{1,0:T(8,128)S(1)} %bitcast.52, f32[72,1024]{1,0:T(8,128)S(1)} %collective-permute-done.above_ref, f32[72,1024]{1,0:T(8,128)S(1)} %collective-permute-done.1.below_ref, ...), custom_call_target="tpu_custom_call" | custom-call | tf_op jit(solution)/shard_map/pallas_call | solution.py:324
  36.0 2.9 %collective-permute-start.6 = (f32[2,4,32,256]{3,2,1,0:T(8,128)S(1)}, f32[2,4,32,256]{3,2,1,0:T(8,128)S(1)}, u32[]{:S(2)}, u32[]{:S(2)}) collective-permute-start(f32[2,4,32,256]{3,2,1,0:T(8,128)S(1)} %slice_bitcast_fusion.2), channel_id=1, source_target_pairs={{0,16},{16,0},{32,48},{48,32},{64,80},{80,64},{96,112},{112,96},{1... | collective-permute-start | bytes 786440 | tf_op jit(solution)/shard_map/ppermute | solution.py:249
  38.9 1.2 %collective-permute-done.6 = f32[2,4,32,256]{3,2,1,0:T(8,128)S(1)} collective-permute-done((f32[2,4,32,256]{3,2,1,0:T(8,128)S(1)}, f32[2,4,32,256]{3,2,1,0:T(8,128)S(1)}, u32[]{:S(2)}, u32[]{:S(2)}) %collective-permute-start.6) | collective-permute-done | bytes 262176 | tf_op jit(solution)/shard_map/ppermute | solution.py:249
  40.1 1.2 %collective-permute-start.7 = (f32[4,32,256]{2,1,0:T(8,128)S(1)}, f32[4,32,256]{2,1,0:T(8,128)S(1)}, u32[]{:S(2)}, u32[]{:S(2)}) collective-permute-start(f32[4,32,256]{2,1,0:T(8,128)S(1)} %slice_bitcast_fusion.3), channel_id=1, source_target_pairs={{0,32},{16,48},{32,0},{48,16},{64,96},{80,112},{96,64},{112,80},{1... | collective-permute-start | bytes 393224 | tf_op jit(solution)/shard_map/ppermute | solution.py:249
  41.3 3.6 %collective-permute-done.7 = f32[4,32,256]{2,1,0:T(8,128)S(1)} collective-permute-done((f32[4,32,256]{2,1,0:T(8,128)S(1)}, f32[4,32,256]{2,1,0:T(8,128)S(1)}, u32[]{:S(2)}, u32[]{:S(2)}) %collective-permute-start.7) | collective-permute-done | bytes 131104 | tf_op jit(solution)/shard_map/ppermute | solution.py:249
  44.9 0.1 collective-permute-start.8
  45.0 3.8 %collective-permute-done.8 = f32[4,32,256]{2,1,0:T(8,128)S(1)} collective-permute-done((f32[4,32,256]{2,1,0:T(8,128)S(1)}, f32[4,32,256]{2,1,0:T(8,128)S(1)}, u32[]{:S(2)}, u32[]{:S(2)}) %collective-permute-start.8) | collective-permute-done | bytes 131104 | tf_op jit(solution)/shard_map/ppermute | solution.py:257
  48.8 2.9 %collective-permute-start.9 = (f32[4,32,256]{2,1,0:T(8,128)S(1)}, f32[4,32,256]{2,1,0:T(8,128)S(1)}, u32[]{:S(2)}, u32[]{:S(2)}) collective-permute-start(f32[4,32,256]{2,1,0:T(8,128)S(1)} %add.88), channel_id=1, source_target_pairs={{0,192},{16,208},{32,224},{48,240},{64,128},{80,144},{96,160},{112... | collective-permute-start | bytes 393224 | tf_op jit(solution)/shard_map/ppermute | solution.py:258
  51.8 2.4 %collective-permute-done.9 = f32[4,32,256]{2,1,0:T(8,128)S(1)} collective-permute-done((f32[4,32,256]{2,1,0:T(8,128)S(1)}, f32[4,32,256]{2,1,0:T(8,128)S(1)}, u32[]{:S(2)}, u32[]{:S(2)}) %collective-permute-start.9) | collective-permute-done | bytes 131104 | tf_op jit(solution)/shard_map/ppermute | solution.py:258
  54.2 1.2 %collective-permute-start.10 = (f32[4,32,256]{2,1,0:T(8,128)S(1)}, f32[4,32,256]{2,1,0:T(8,128)S(1)}, u32[]{:S(2)}, u32[]{:S(2)}) collective-permute-start(f32[4,32,256]{2,1,0:T(8,128)S(1)} %add_divide_fusion), channel_id=1, source_target_pairs={{0,32},{16,48},{32,0},{48,16},{64,96},{80,112},{96,64},{112,80},{1... | collective-permute-start | bytes 393224 | tf_op jit(solution)/shard_map/ppermute | solution.py:249
  55.4 2.7 %collective-permute-done.10 = f32[4,32,256]{2,1,0:T(8,128)S(1)} collective-permute-done((f32[4,32,256]{2,1,0:T(8,128)S(1)}, f32[4,32,256]{2,1,0:T(8,128)S(1)}, u32[]{:S(2)}, u32[]{:S(2)}) %collective-permute-start.10) | collective-permute-done | bytes 131104 | tf_op jit(solution)/shard_map/ppermute | solution.py:249
  58.1 4.7 %collective-permute-start.11 = (f32[2,4,32,256]{3,2,1,0:T(8,128)S(1)}, f32[2,4,32,256]{3,2,1,0:T(8,128)S(1)}, u32[]{:S(2)}, u32[]{:S(2)}) collective-permute-start(f32[2,4,32,256]{3,2,1,0:T(8,128)S(1)} %pad_maximum_fusion.mine_ref), channel_id=1, source_target_pairs={{0,16},{16,0},{32,48},{48,32},{64,80},{80,64},{96,112},{112,96},{1... | collective-permute-start | bytes 786440 | tf_op jit(solution)/shard_map/ppermute | solution.py:249
  62.8 1.2 %collective-permute-done.11.other_ref = f32[2,4,32,256]{3,2,1,0:T(8,128)S(1)} collective-permute-done((f32[2,4,32,256]{3,2,1,0:T(8,128)S(1)}, f32[2,4,32,256]{3,2,1,0:T(8,128)S(1)}, u32[]{:S(2)}, u32[]{:S(2)}) %collective-permute-start.11) | collective-permute-done | bytes 262176 | tf_op jit(solution)/shard_map/ppermute | solution.py:249
  64.0 0.6 shard_map.126
  64.6 0.1 collective-permute-start.12
  64.7 5.1 %collective-permute-start.13 = (f32[40,1024]{1,0:T(8,128)S(1)}, f32[40,1024]{1,0:T(8,128)S(1)}, u32[]{:S(2)}, u32[]{:S(2)}) collective-permute-start(f32[40,1024]{1,0:T(8,128)S(1)} %get-tuple-element.22), channel_id=1, source_target_pairs={{1,0},{2,1},{3,2},{4,3},{5,4},{6,5},{7,6},{8,7},{9,8},{10,9},{11,1... | collective-permute-start | bytes 491528 | tf_op jit(solution)/shard_map/ppermute | solution.py:271
  69.8 0.6 dynamic-slice_bitcast_fusion
  70.4 3.4 %collective-permute-done.12.above_ref = f32[40,1024]{1,0:T(8,128)S(1)} collective-permute-done((f32[40,1024]{1,0:T(8,128)S(1)}, f32[40,1024]{1,0:T(8,128)S(1)}, u32[]{:S(2)}, u32[]{:S(2)}) %collective-permute-start.12) | collective-permute-done | bytes 163872 | tf_op jit(solution)/shard_map/ppermute | solution.py:267
  73.8 1.5 %collective-permute-done.13.below_ref = f32[40,1024]{1,0:T(8,128)S(1)} collective-permute-done((f32[40,1024]{1,0:T(8,128)S(1)}, f32[40,1024]{1,0:T(8,128)S(1)}, u32[]{:S(2)}, u32[]{:S(2)}) %collective-permute-start.13) | collective-permute-done | bytes 163872 | tf_op jit(solution)/shard_map/ppermute | solution.py:271
  75.2 3.9 %shard_map.127 = f32[32,4096]{1,0:T(8,128)} custom-call(s32[4]{0:T(128)S(1)} %pad_add_fusion.place_ref, f32[32,4096]{1,0:T(8,128)S(1)} %get-tuple-element.20.own_ref, f32[40,1024]{1,0:T(8,128)S(1)} %collective-permute-done.12.above_ref, f32[40,1024]{1,0:T(8,128)S(1)} %collective-permute-done.13.below_ref, bf16[224,768]{1,0:T(8,128)(2,1)S(1)} %get-tuple-element.23.band_ref), custom_call_target="tpu_custom_call" | custom-call | tf_op jit(solution)/shard_map/pallas_call | solution.py:351
  (32 shorter events, 0.4 us)
Async XLA Ops:
  0.6 13.5 %copy-start = (f32[9,21,21]{2,1,0:T(8,128)S(1)}, f32[9,21,21]{2,1,0:T(8,128)}, u32[]{:S(2)}) copy-start(f32[9,21,21]{2,1,0:T(8,128)} %param.12) | copy-start | bytes 47632
  0.7 1.4 %copy-start.5 = (s32[1,4096]{1,0:T(1,128)S(1)}, s32[1,4096]{1,0:T(1,128)}, u32[]{:S(2)}) copy-start(s32[1,4096]{1,0:T(1,128)} %starts_ref.3) | copy-start | bytes 49156
  2.1 1.0 %copy-start.1 = (s32[1,32,4096]{2,1,0:T(8,128)S(1)}, s32[1,32,4096]{2,1,0:T(8,128)}, u32[]{:S(2)}) copy-start(s32[1,32,4096]{2,1,0:T(8,128)} %param.20) | copy-start | bytes 1572868
  3.8 3.4 %copy-start.3 = (f32[1,32,4096]{2,1,0:T(8,128)S(1)}, f32[1,32,4096]{2,1,0:T(8,128)}, u32[]{:S(2)}) copy-start(f32[1,32,4096]{2,1,0:T(8,128)} %param.11) | copy-start | bytes 1572868
  3.8 10.7 %collective-permute-start.2 = (f32[2,4,32,256]{3,2,1,0:T(8,128)S(1)}, f32[2,4,32,256]{3,2,1,0:T(8,128)S(1)}, u32[]{:S(2)}, u32[]{:S(2)}) collective-permute-start(f32[2,4,32,256]{3,2,1,0:T(8,128)S(1)} %slice_bitcast_fusion), channel_id=1, source_target_pairs={{0,16},{16,0},{32,48},{48,32},{64,80},{80,64},{96,112},{112,96},{1... | collective-permute-start | bytes 786440 | tf_op jit(solution)/shard_map/ppermute | solution.py:249
  7.2 6.8 %copy-start.6 = (f32[1,21,21]{2,0,1:T(1,128)S(1)}, f32[1,21,21]{2,0,1:T(1,128)}, u32[]{:S(2)}) copy-start(f32[1,21,21]{2,0,1:T(1,128)} %param.21) | copy-start | bytes 5296
  7.3 23.4 %collective-permute-start = (f32[72,1024]{1,0:T(8,128)S(1)}, f32[72,1024]{1,0:T(8,128)S(1)}, u32[]{:S(2)}, u32[]{:S(2)}) collective-permute-start(f32[72,1024]{1,0:T(8,128)S(1)} %get-tuple-element.13), channel_id=1, source_target_pairs={{0,1},{1,2},{2,3},{3,4},{4,5},{5,6},{6,7},{7,8},{8,9},{9,10},{10,1... | collective-permute-start | bytes 884744 | tf_op jit(solution)/shard_map/ppermute | solution.py:267
  8.6 5.5 %copy-start.8 = (f32[1,9]{1,0:T(1,128)S(1)}, f32[1,9]{1,0:T(1,128)}, u32[]{:S(2)}) copy-start(f32[1,9]{1,0:T(1,128)} %param.13) | copy-start | bytes 112
  8.6 22.0 %collective-permute-start.1 = (f32[72,1024]{1,0:T(8,128)S(1)}, f32[72,1024]{1,0:T(8,128)S(1)}, u32[]{:S(2)}, u32[]{:S(2)}) collective-permute-start(f32[72,1024]{1,0:T(8,128)S(1)} %get-tuple-element.14), channel_id=1, source_target_pairs={{1,0},{2,1},{3,2},{4,3},{5,4},{6,5},{7,6},{8,7},{9,8},{10,9},{11,1... | collective-permute-start | bytes 884744 | tf_op jit(solution)/shard_map/ppermute | solution.py:271
  14.6 1.5 %copy-start.9 = (s32[1,32]{1,0:T(1,128)S(1)}, s32[1,32]{1,0:T(1,128)}, u32[]{:S(2)}) copy-start(s32[1,32]{1,0:T(1,128)} %param.14) | copy-start | bytes 388
  14.6 6.9 %collective-permute-start.3 = (f32[2,4,32,256]{3,2,1,0:T(8,128)S(1)}, f32[2,4,32,256]{3,2,1,0:T(8,128)S(1)}, u32[]{:S(2)}, u32[]{:S(2)}) collective-permute-start(f32[2,4,32,256]{3,2,1,0:T(8,128)S(1)} %fusion), channel_id=1, source_target_pairs={{0,64},{16,80},{32,96},{48,112},{64,0},{80,16},{96,32},{112,48},{1... | collective-permute-start | bytes 786440 | tf_op jit(solution)/shard_map/ppermute | solution.py:257
  21.6 7.4 %collective-permute-start.4 = (f32[2,4,32,256]{3,2,1,0:T(8,128)S(1)}, f32[2,4,32,256]{3,2,1,0:T(8,128)S(1)}, u32[]{:S(2)}, u32[]{:S(2)}) collective-permute-start(f32[2,4,32,256]{3,2,1,0:T(8,128)S(1)} %add.83), channel_id=1, source_target_pairs={{0,192},{16,208},{32,224},{48,240},{64,128},{80,144},{96,160},{112... | collective-permute-start | bytes 786440 | tf_op jit(solution)/shard_map/ppermute | solution.py:258
  24.5 6.1 %copy-start.2 = (s32[1,32,4096]{2,1,0:T(8,128)S(1)}, s32[1,32,4096]{2,1,0:T(8,128)}, u32[]{:S(2)}) copy-start(s32[1,32,4096]{2,1,0:T(8,128)} %param.20) | copy-start | bytes 1572868
  29.0 0.7 copy-start.7
  29.0 1.6 %copy-start.4 = (f32[1,8,4096]{2,1,0:T(8,128)S(1)}, f32[1,8,4096]{2,1,0:T(8,128)}, u32[]{:S(2)}) copy-start(f32[1,8,4096]{2,1,0:T(8,128)} %param.18) | copy-start | bytes 393220
  29.1 6.9 %collective-permute-start.5 = (f32[4,32,256]{2,1,0:T(8,128)S(1)}, f32[4,32,256]{2,1,0:T(8,128)S(1)}, u32[]{:S(2)}, u32[]{:S(2)}) collective-permute-start(f32[4,32,256]{2,1,0:T(8,128)S(1)} %slice_bitcast_fusion.5), channel_id=1, source_target_pairs={{0,32},{16,48},{32,0},{48,16},{64,96},{80,112},{96,64},{112,80},{1... | collective-permute-start | bytes 393224 | tf_op jit(solution)/shard_map/ppermute | solution.py:249
  36.0 4.0 %collective-permute-start.6 = (f32[2,4,32,256]{3,2,1,0:T(8,128)S(1)}, f32[2,4,32,256]{3,2,1,0:T(8,128)S(1)}, u32[]{:S(2)}, u32[]{:S(2)}) collective-permute-start(f32[2,4,32,256]{3,2,1,0:T(8,128)S(1)} %slice_bitcast_fusion.2), channel_id=1, source_target_pairs={{0,16},{16,0},{32,48},{48,32},{64,80},{80,64},{96,112},{112,96},{1... | collective-permute-start | bytes 786440 | tf_op jit(solution)/shard_map/ppermute | solution.py:249
  40.1 4.8 %collective-permute-start.7 = (f32[4,32,256]{2,1,0:T(8,128)S(1)}, f32[4,32,256]{2,1,0:T(8,128)S(1)}, u32[]{:S(2)}, u32[]{:S(2)}) collective-permute-start(f32[4,32,256]{2,1,0:T(8,128)S(1)} %slice_bitcast_fusion.3), channel_id=1, source_target_pairs={{0,32},{16,48},{32,0},{48,16},{64,96},{80,112},{96,64},{112,80},{1... | collective-permute-start | bytes 393224 | tf_op jit(solution)/shard_map/ppermute | solution.py:249
  44.9 3.9 %collective-permute-start.8 = (f32[4,32,256]{2,1,0:T(8,128)S(1)}, f32[4,32,256]{2,1,0:T(8,128)S(1)}, u32[]{:S(2)}, u32[]{:S(2)}) collective-permute-start(f32[4,32,256]{2,1,0:T(8,128)S(1)} %fusion.3), channel_id=1, source_target_pairs={{0,64},{16,80},{32,96},{48,112},{64,0},{80,16},{96,32},{112,48},{1... | collective-permute-start | bytes 393224 | tf_op jit(solution)/shard_map/ppermute | solution.py:257
  48.8 5.3 %collective-permute-start.9 = (f32[4,32,256]{2,1,0:T(8,128)S(1)}, f32[4,32,256]{2,1,0:T(8,128)S(1)}, u32[]{:S(2)}, u32[]{:S(2)}) collective-permute-start(f32[4,32,256]{2,1,0:T(8,128)S(1)} %add.88), channel_id=1, source_target_pairs={{0,192},{16,208},{32,224},{48,240},{64,128},{80,144},{96,160},{112... | collective-permute-start | bytes 393224 | tf_op jit(solution)/shard_map/ppermute | solution.py:258
  54.2 3.9 %collective-permute-start.10 = (f32[4,32,256]{2,1,0:T(8,128)S(1)}, f32[4,32,256]{2,1,0:T(8,128)S(1)}, u32[]{:S(2)}, u32[]{:S(2)}) collective-permute-start(f32[4,32,256]{2,1,0:T(8,128)S(1)} %add_divide_fusion), channel_id=1, source_target_pairs={{0,32},{16,48},{32,0},{48,16},{64,96},{80,112},{96,64},{112,80},{1... | collective-permute-start | bytes 393224 | tf_op jit(solution)/shard_map/ppermute | solution.py:249
  58.1 5.9 %collective-permute-start.11 = (f32[2,4,32,256]{3,2,1,0:T(8,128)S(1)}, f32[2,4,32,256]{3,2,1,0:T(8,128)S(1)}, u32[]{:S(2)}, u32[]{:S(2)}) collective-permute-start(f32[2,4,32,256]{3,2,1,0:T(8,128)S(1)} %pad_maximum_fusion.mine_ref), channel_id=1, source_target_pairs={{0,16},{16,0},{32,48},{48,32},{64,80},{80,64},{96,112},{112,96},{1... | collective-permute-start | bytes 786440 | tf_op jit(solution)/shard_map/ppermute | solution.py:249
  64.6 9.1 %collective-permute-start.12 = (f32[40,1024]{1,0:T(8,128)S(1)}, f32[40,1024]{1,0:T(8,128)S(1)}, u32[]{:S(2)}, u32[]{:S(2)}) collective-permute-start(f32[40,1024]{1,0:T(8,128)S(1)} %get-tuple-element.21), channel_id=1, source_target_pairs={{0,1},{1,2},{2,3},{3,4},{4,5},{5,6},{6,7},{7,8},{8,9},{9,10},{10,1... | collective-permute-start | bytes 491528 | tf_op jit(solution)/shard_map/ppermute | solution.py:267
  64.7 10.5 %collective-permute-start.13 = (f32[40,1024]{1,0:T(8,128)S(1)}, f32[40,1024]{1,0:T(8,128)S(1)}, u32[]{:S(2)}, u32[]{:S(2)}) collective-permute-start(f32[40,1024]{1,0:T(8,128)S(1)} %get-tuple-element.22), channel_id=1, source_target_pairs={{1,0},{2,1},{3,2},{4,3},{5,4},{6,5},{7,6},{8,7},{9,8},{10,9},{11,1... | collective-permute-start | bytes 491528 | tf_op jit(solution)/shard_map/ppermute | solution.py:271
where the time goes:
time: 79.4 us; the launch traced here: 79.1 us
  starting transfers between devices  32.9 us (41%)
  waiting for transfers between devices  29.5 us (37%)
  Pallas kernels  11.4 us (14%)
  local copies, waits for them, and re-layouts  2.34 us (3%)
  between operations  2.25 us (3%)
    ppermute x6, starting transfers between devices, swap(): return lax.ppermute(values, 'visit', [(i, i ^ step) for i in range(16)])  13.8 us
    ppermute x2, starting transfers between devices, to_previous(): return lax.ppermute(values, 'row', [((i + 1) % 16, i) for i in range(16)])  10.5 us
    ppermute x2, waiting for transfers between devices, over_y(): part = part + lax.ppermute(part, 'visit', RING_A)  9.25 us
    ppermute x6, waiting for transfers between devices, swap(): return lax.ppermute(values, 'visit', [(i, i ^ step) for i in range(16)])  8.57 us
    ppermute x2, waiting for transfers between devices, over_y(): return part + lax.ppermute(part, 'visit', RING_B)  6.81 us
    ppermute x2, starting transfers between devices, over_y(): return part + lax.ppermute(part, 'visit', RING_B)  5.76 us
    pallas_call x1, Pallas kernels, on_device(): call(warp_kernel, (sds(ROWS, COLS), sds(2, 2, 4, ROWS, BLOCK)), [SM, SM]...  5.27 us
    pallas_call x1, Pallas kernels, on_device(): call(clean_kernel, sds(ROWS, COLS), [SM] + [VM] * 4, frames)  3.91 us
  transfers between devices with their start and end apart: 14, of which 10 were waited for; matrix products, arithmetic and copies ran while one was open for 2% of the time, Pallas kernels for 8%

commit v1 on v0

v1 whole, which is shorter than its diff:
```python
import jax
import jax.numpy as jnp
from jax import lax
from jax.experimental import pallas as pl
from jax.experimental.pallas import tpu as pltpu
from jax.sharding import PartitionSpec as P

KS = 21
HALF = KS // 2
TAPS = 8
ROWS = 32
COLS = 4096
SPAN = 40
SLOT = 128
BASE = 24
LEAD = 6
CHUNK = 1024
BLOCK = 256
GROUP = 4
STEPS = 6
FRAME = COLS + 128
LEFT = 640
F32 = jnp.float32
BF16 = jnp.bfloat16
VMEM_LIMIT = 16 * 1024 * 1024

VM = pl.BlockSpec(memory_space=pltpu.VMEM)
SM = pl.BlockSpec(memory_space=pltpu.SMEM)


def call(kernel, outs, ins, scratch=(), cost=None):
    return pl.pallas_call(
        kernel,
        out_shape=outs,
        in_specs=ins,
        out_specs=jax.tree.map(lambda _: VM, outs),
        scratch_shapes=list(scratch),
        compiler_params=pltpu.CompilerParams(vmem_limit_bytes=VMEM_LIMIT),
        cost_estimate=cost,
    )


def sds(*shape, dtype=F32):
    return jax.ShapeDtypeStruct(shape, dtype)


def pack_kernel(x_ref, up_ref, down_ref):
    for q in range(4):
        cols = pl.ds(q * CHUNK, CHUNK)
        down_ref[16 * q : 16 * q + 16, :] = x_ref[16:32, cols]
        up_ref[16 * q : 16 * q + 16, :] = x_ref[0:16, cols]
        down_ref[64 + q : 65 + q, :] = x_ref[15:16, cols]
        down_ref[68 + q : 69 + q, :] = jnp.zeros((1, CHUNK), F32)
        up_ref[64 + q : 65 + q, :] = x_ref[16:17, cols]
        up_ref[68 + q : 69 + q, :] = x_ref[17:18, cols]


def between(values, low, high, shift):
    lanes = lax.broadcasted_iota(jnp.int32, values.shape, 1)
    return pltpu.roll(jnp.where((lanes >= low) & (lanes < high), values, 0.0), shift % SLOT, 1)


def put_bands(ref, values):
    lanes = lax.broadcasted_iota(jnp.int32, values.shape, 1)
    spans = values + pltpu.roll(values, SPAN, 1) + pltpu.roll(values, 2 * SPAN, 1)
    high = spans.astype(BF16).astype(F32)
    parts = jnp.where(lanes < 2 * SPAN, high, spans - high).astype(BF16)
    for lag in range(GROUP * STEPS):
        rows = pl.ds(ROWS * (lag // GROUP), ROWS)
        slot = pl.ds(SLOT * (lag % GROUP), SLOT)
        ref[rows, slot] = parts[ROWS * lag : ROWS * (lag + 1)]


def put_both(own_ref, edge_ref, values):
    put_bands(own_ref, between(values, BASE, BASE + ROWS, -BASE))
    edge = between(values, BASE - 16, BASE, 16 - BASE)
    edge = edge + between(values, BASE + ROWS, BASE + ROWS + 18, 16 - BASE - ROWS)
    put_bands(edge_ref, edge + between(values, BASE - 17, BASE - 16, 39 - (BASE - 17)))


def skewed(ref, lag, rows, shift):
    values = jnp.broadcast_to(ref[lag : lag + 1, :], (rows, SLOT))
    return pltpu.roll(values, shift, 1, stride=1, stride_axis=0)


def bands_kernel(k1_ref, k2_ref, mix_ref, own1_ref, edge1_ref, own2_ref, edge2_ref):
    first = jnp.concatenate([skewed(k1_ref, lag, 48, 0) for lag in range(24)], axis=1)
    merged = jnp.dot(
        mix_ref[...], first, precision=lax.Precision.HIGHEST, preferred_element_type=F32
    )
    slots = [merged[:, SLOT * lag : SLOT * (lag + 1)] for lag in range(24)]
    put_both(own1_ref, edge1_ref, jnp.concatenate(slots, axis=0))
    slots = [skewed(k2_ref, lag, ROWS, 8) for lag in range(24)]
    put_both(own2_ref, edge2_ref, jnp.concatenate(slots, axis=0))


def coverage(starts, offset, q):
    column = lax.broadcasted_iota(jnp.int32, starts.shape, 1) + q * CHUNK
    actual = column - offset + starts
    return ((actual >= 0) & (actual <= COLS - TAPS)).astype(F32)


def put_blocks(ref, values, row, place_ref, q):
    for j in range(4):
        at = (j % 2) ^ place_ref[1], 2 * q + j // 2, pl.ds(row, ROWS)
        ref[at] = values[:, j * BLOCK : (j + 1) * BLOCK]


def clear(frame_ref, row):
    frame_ref[:, COLS:FRAME] = jnp.zeros((SPAN, FRAME - COLS), F32)
    frame_ref[row:SPAN, 0:COLS] = jnp.zeros((SPAN - row, COLS), F32)


def put_wide(frame_ref, row, ref, rows, valid):
    for q in range(4):
        values = jnp.where(valid, ref[rows * q : rows * (q + 1), :], 0.0)
        frame_ref[row : row + rows, q * CHUNK : (q + 1) * CHUNK] = values


def put_thin(frame_ref, row, ref, at, valid):
    for q in range(4):
        values = jnp.where(valid, ref[at + q : at + q + 1, :], 0.0)
        frame_ref[row : row + 1, q * CHUNK : (q + 1) * CHUNK] = values


def split_rows(frame_ref, halves_ref):
    frame = frame_ref[...]
    padding = jnp.zeros((SLOT - 3 * SPAN, FRAME), F32)
    for part in range(GROUP):
        moved = pltpu.roll(frame, HALF - part, 1)
        high = moved.astype(BF16).astype(F32)
        spans = jnp.concatenate([high, moved - high, high, padding], axis=0)
        halves_ref[SLOT * part : SLOT * (part + 1), :] = spans.astype(BF16)


def correlate_chunk(band_ref, halves_ref, q):
    width = CHUNK + 128
    lags = jnp.dot(
        band_ref[...],
        halves_ref[:, q * CHUNK : q * CHUNK + width],
        preferred_element_type=F32,
    )
    total = lags[0:ROWS, :CHUNK]
    for step in range(1, STEPS):
        moved = pltpu.roll(lags[ROWS * step : ROWS * (step + 1), :], width - GROUP * step, 1)
        total = total + moved[:, :CHUNK]
    return total


def own_kernel(own_ref, band_ref, out_ref, frame_ref, halves_ref):
    clear(frame_ref, ROWS)
    frame_ref[0:ROWS, 0:COLS] = own_ref[...]
    split_rows(frame_ref, halves_ref)
    for q in range(4):
        out_ref[:, q * CHUNK : (q + 1) * CHUNK] = correlate_chunk(band_ref, halves_ref, q)


def warp_kernel(
    place_ref,
    weight_ref,
    own_ref,
    above_ref,
    below_ref,
    band_ref,
    starts_ref,
    taps_ref,
    mask_ref,
    warped_ref,
    weighted_ref,
    frame_ref,
    halves_ref,
    source_ref,
):
    band = place_ref[2]
    has_above, has_below = band > 0, band < 15
    clear(frame_ref, 32)
    put_wide(frame_ref, 0, above_ref, 16, has_above)
    put_wide(frame_ref, 16, below_ref, 16, has_below)
    put_thin(frame_ref, 32, below_ref, 64, has_below)
    put_thin(frame_ref, 33, below_ref, 68, has_below)
    put_thin(frame_ref, 39, above_ref, 64, has_above)
    split_rows(frame_ref, halves_ref)

    source_ref[:, 0:LEFT] = jnp.zeros((ROWS, LEFT), F32)
    source_ref[:, LEFT + COLS : LEFT + COLS + 128] = jnp.zeros((ROWS, 128), F32)
    for q in range(4):
        edges = correlate_chunk(band_ref, halves_ref, q)
        source_ref[:, LEFT + q * CHUNK : LEFT + (q + 1) * CHUNK] = (
            own_ref[:, q * CHUNK : (q + 1) * CHUNK] + edges
        )

    offset = place_ref[0]
    first = LEFT - 3 - offset
    aligned = first // 128
    rest = first - aligned * 128
    width = CHUNK + 256
    for q in range(4):
        cols = pl.ds(q * CHUNK, CHUNK)
        at = pl.multiple_of((aligned + q * (CHUNK // 128)) * 128, 128)
        moved = pltpu.roll(source_ref[:, pl.ds(at, width)], width - rest, 1)
        starts = starts_ref[:, cols]
        early = starts == -3
        taps = [taps_ref[t : t + 1, cols] for t in range(TAPS)]
        zero = jnp.zeros_like(taps[0])
        total = None
        for lag in range(TAPS + 1):
            tap = jnp.where(
                early, taps[lag] if lag < TAPS else zero, taps[lag - 1] if lag else zero
            )
            part = moved if lag == 0 else pltpu.roll(moved, width - lag, 1)
            term = tap * part[:, :CHUNK]
            total = term if total is None else total + term
        warped_ref[:, cols] = total
        share = weight_ref[0] * mask_ref[:, cols].astype(F32) * coverage(starts, offset, q)
        put_blocks(weighted_ref, share * total, 0, place_ref, q)
        put_blocks(weighted_ref, share, ROWS, place_ref, q)


def differ_kernel(
    place_ref,
    own_ref,
    mine_ref,
    other_ref,
    diff_ref,
    up_ref,
    down_ref,
):
    core = place_ref[1]
    for b in range(16):
        cols = pl.ds(b * BLOCK, BLOCK)
        coadd = jnp.where(core == b % 2, mine_ref[b // 2], other_ref[b // 2])
        diff_ref[:, cols] = own_ref[:, cols] - coadd
    for q in range(4):
        cols = pl.ds(q * CHUNK, CHUNK)
        down_ref[8 * q : 8 * q + 8, :] = diff_ref[24:32, cols]
        up_ref[8 * q : 8 * q + 8, :] = diff_ref[0:8, cols]
        for extra in range(2):
            at = 32 + 4 * extra + q
            down_ref[at : at + 1, :] = diff_ref[22 + extra : 23 + extra, cols]
            up_ref[at : at + 1, :] = diff_ref[8 + extra : 9 + extra, cols]


def clean_kernel(
    place_ref,
    own_ref,
    above_ref,
    below_ref,
    coadd_ref,
    band_ref,
    out_ref,
    template_ref,
    frame_ref,
    halves_ref,
):
    template_ref[...] = coadd_ref[...]
    band = place_ref[2]
    has_above, has_below = band > 0, band < 15
    clear(frame_ref, 0)
    put_wide(frame_ref, 8, above_ref, 8, has_above)
    put_wide(frame_ref, 16, below_ref, 8, has_below)
    for extra in range(2):
        put_thin(frame_ref, 6 + extra, above_ref, 32 + 4 * extra, has_above)
        put_thin(frame_ref, 24 + extra, below_ref, 32 + 4 * extra, has_below)
    split_rows(frame_ref, halves_ref)
    for q in range(4):
        cols = pl.ds(q * CHUNK, CHUNK)
        out_ref[:, cols] = own_ref[:, cols] + correlate_chunk(band_ref, halves_ref, q)


def by_lag(kernel):
    return jnp.pad(kernel.T, ((0, 3), (LEAD, SLOT - LEAD - KS)))


def swap(values, step):
    return lax.ppermute(values, "visit", [(i, i ^ step) for i in range(16)])


def over_chips(blocks):
    return lax.all_to_all(
        blocks,
        "visit",
        split_axis=0,
        concat_axis=0,
        axis_index_groups=[list(range(core, 16, 2)) for core in range(2)],
        tiled=True,
    )


def to_next(values):
    return lax.ppermute(values, "row", [(i, (i + 1) % 16) for i in range(16)])


def to_previous(values):
    return lax.ppermute(values, "row", [((i + 1) % 16, i) for i in range(16)])


def on_device(
    science,
    basis_kernels,
    basis_coeffs,
    row_starts,
    row_taps,
    col_offsets,
    col_starts,
    col_taps,
    visit_weights,
    clip_masks,
    decorrelation,
):
    pixels = science[0]
    visit = lax.axis_index("visit")
    band = lax.axis_index("row")
    band_at = band * ROWS
    place = jnp.stack([col_offsets[0], visit % 2, band]).astype(jnp.int32)

    up, down = call(pack_kernel, (sds(72, CHUNK), sds(72, CHUNK)), [VM])(pixels)
    above = to_next(down)
    below = to_previous(up)

    kernel = jnp.einsum(
        "b,bij->ij", basis_coeffs[0], basis_kernels, precision=lax.Precision.HIGHEST
    )
    matched_row = jnp.arange(48, dtype=jnp.int32)[None, :] - 8
    tap_at = matched_row - (jnp.arange(ROWS, dtype=jnp.int32) + row_starts[0])[:, None]
    inside = (matched_row + band_at >= 0) & (matched_row + band_at < 16 * ROWS)
    hits = tap_at[None] == jnp.arange(TAPS, dtype=jnp.int32)[:, None, None]
    mix = jnp.sum(jnp.where(hits & inside[None], row_taps[0][:, :, None], 0.0), axis=0)
    own_first, edge_first, own_second, edge_second = call(
        bands_kernel, (sds(STEPS * ROWS, GROUP * SLOT, dtype=BF16),) * 4, [VM] * 3
    )(by_lag(kernel), by_lag(decorrelation[0]), mix)

    frames = [
        pltpu.VMEM((SPAN, FRAME), F32),
        pltpu.VMEM((GROUP * SLOT, FRAME), BF16),
    ]
    own_part = call(own_kernel, sds(ROWS, COLS), [VM] * 2, frames)(pixels, own_first)
    warped, weighted = call(
        warp_kernel,
        (sds(ROWS, COLS), sds(2, 8, 2 * ROWS, BLOCK)),
        [SM, SM] + [VM] * 7,
        frames + [pltpu.VMEM((ROWS, LEFT + COLS + 128), F32)],
    )(
        place,
        visit_weights,
        own_part,
        above,
        below,
        edge_first,
        col_starts,
        col_taps[0],
        clip_masks[0],
    )
    half = weighted[0] + swap(weighted[1], 1)
    total = jnp.sum(over_chips(half), axis=0)
    coadd = total[:ROWS] / jnp.maximum(total[ROWS:], 1.0)
    mine = over_chips(jnp.broadcast_to(coadd[None], (8, ROWS, BLOCK)))
    other = swap(mine, 1)
    difference, up, down = call(
        differ_kernel,
        (sds(ROWS, COLS), sds(40, CHUNK), sds(40, CHUNK)),
        [SM] + [VM] * 3,
    )(place, warped, mine, other)
    above, below = to_next(down), to_previous(up)
    own_part = call(own_kernel, sds(ROWS, COLS), [VM] * 2, frames)(difference, own_second)
    cleaned, template = call(
        clean_kernel, (sds(ROWS, COLS), sds(ROWS, BLOCK)), [SM] + [VM] * 5, frames
    )(place, own_part, above, below, coadd, edge_second)
    return cleaned[None], template


def solution(mesh):
    return jax.shard_map(
        on_device,
        mesh=mesh,
        in_specs=(
            P("visit", "row", None),
            P(),
            P("visit", None),
            P("visit", "row"),
            P("visit", None, "row"),
            P("visit"),
            P("visit", None),
            P("visit", None, None),
            P("visit"),
            P("visit", "row", None),
            P("visit", None, None),
        ),
        out_specs=(P("visit", "row", None), P("row", "visit")),
        check_vma=False,
    )
```

time: 79.4 us -> 71.8 us (0.904)
  the two profiles are of different devices: /device:TPU:1 before, /device:TPU:102 now
where the time goes in v1:
time: 71.8 us; the launch traced here: 71.5 us
  blocking collectives  24.8 us (35%)
  waiting for transfers between devices  16.1 us (22%)
  Pallas kernels  14.8 us (21%)
  starting transfers between devices  9.74 us (14%)
  local copies, waits for them, and re-layouts  3.35 us (5%)
  between operations  2.15 us (3%)
    all_to_all x2, blocking collectives, over_chips(): lax.all_to_all(blocks, 'visit', split_axis=0, concat_axis=0, axis_index_g...  24.8 us
    ppermute x2, starting transfers between devices, to_next(): return lax.ppermute(values, 'row', [(i, (i + 1) % 16) for i in range(16)])  9.64 us
    ppermute x2, waiting for transfers between devices, to_next(): return lax.ppermute(values, 'row', [(i, (i + 1) % 16) for i in range(16)])  6.86 us
    ppermute x2, waiting for transfers between devices, to_previous(): return lax.ppermute(values, 'row', [((i + 1) % 16, i) for i in range(16)])  5.77 us
    pallas_call x1, Pallas kernels, on_device(): call(warp_kernel, (sds(ROWS, COLS), sds(2, 8, 2 * ROWS, BLOCK)), [SM, SM]...  4.57 us
    ppermute x2, waiting for transfers between devices, swap(): return lax.ppermute(values, 'visit', [(i, i ^ step) for i in range(16)])  3.43 us
    pallas_call x1, Pallas kernels, on_device(): call(clean_kernel, (sds(ROWS, COLS), sds(ROWS, BLOCK)), [SM] + [VM] * 5,...  3.18 us
    unnamed x21, local copies, waits for them, and re-layouts  3.04 us
  transfers between devices with their start and end apart: 6, of which 5 were waited for; matrix products, arithmetic and copies ran while one was open for 1% of the time, Pallas kernels for 8%

profile of v1, /device:TPU:102, one launch (start us, length us, event | category | flops | bytes accessed | tf_op | source)
XLA Modules:
  0.0 71.5 jit_solution(2167622701511998429)
XLA Ops:
  0.6 0.0 copy-start
  0.6 0.0 copy-start.1
  0.7 1.1 %copy-done.1 = f32[1,32,4096]{2,1,0:T(8,128)S(1)} copy-done((f32[1,32,4096]{2,1,0:T(8,128)S(1)}, f32[1,32,4096]{2,1,0:T(8,128)}, u32[]{:S(2)}) %copy-start.1) | copy-done | bytes 524312
  1.7 0.8 %shard_map.124 = (f32[72,1024]{1,0:T(8,128)S(1)}, f32[72,1024]{1,0:T(8,128)}) custom-call(f32[32,4096]{1,0:T(8,128)S(1)} %bitcast.24), custom_call_target="tpu_custom_call" | custom-call | tf_op jit(solution)/shard_map/pallas_call | solution.py:316
  2.5 4.0 %collective-permute-start = (f32[72,1024]{1,0:T(8,128)}, f32[72,1024]{1,0:T(8,128)S(1)}, u32[]{:S(2)}, u32[]{:S(2)}) collective-permute-start(f32[72,1024]{1,0:T(8,128)} %get-tuple-element.16), channel_id=1, source_target_pairs={{0,1},{1,2},{2,3},{3,4},{4,5},{5,6},{6,7},{7,8},{8,9},{9,10},{10,1... | collective-permute-start | bytes 884744 | tf_op jit(solution)/shard_map/ppermute | solution.py:290
  6.5 0.0 collective-permute-start.1
  7.1 0.0 copy-start.9
  7.8 0.0 copy-done.9
  7.8 0.0 copy-start.8
  7.8 0.0 copy-done
  7.8 0.6 copy-done.8
  8.5 0.2 fusion
  8.7 0.0 copy-start.6
  8.7 0.1 copy.16
  8.8 0.6 copy-done.6
  9.4 0.1 copy.14
  9.5 0.1 pad.7.k1_ref
  9.5 0.1 pad.8.k2_ref
  9.6 0.1 broadcast_subtract_fusion
  9.7 0.6 copy-done.7
  10.3 0.1 select_reduce_fusion.mix_ref
  10.4 2.1 %shard_map.122 = (bf16[192,512]{1,0:T(8,128)(2,1)S(1)}, bf16[192,512]{1,0:T(8,128)(2,1)S(1)}, bf16[192,512]{1,0:T(8,128)(2,1)S(1)}, bf16[192,512]{1,0:T(8,128)(2,1)S(1)}) custom-call(f32[24,128]{1,0:T(8,128)S(1)} %pad.7.k1_ref, f32[24,128]{1,0:T(8,128)S(1)} %pad.8.k2_ref, f32[32,48]{1,0:T(8,128)S(1)} %select_reduce_fusion.mix_ref), custom_call_target="tpu_custom_call" | custom-call | tf_op jit(solution)/shard_map/pallas_call | solution.py:328
  12.5 0.0 copy-done.2
  12.5 0.0 copy-start.3
  12.5 0.0 copy-start.4
  12.5 0.0 copy-start.5
  12.6 1.8 %shard_map.123.own_ref = f32[32,4096]{1,0:T(8,128)S(1)} custom-call(f32[32,4096]{1,0:T(8,128)S(1)} %bitcast.25, bf16[192,512]{1,0:T(8,128)(2,1)S(1)} %get-tuple-element.15.band_ref), custom_call_target="tpu_custom_call" | custom-call | tf_op jit(solution)/shard_map/pallas_call | solution.py:336
  14.3 0.1 pad_add_fusion.place_ref
  14.4 4.9 %collective-permute-done.above_ref = f32[72,1024]{1,0:T(8,128)S(1)} collective-permute-done((f32[72,1024]{1,0:T(8,128)}, f32[72,1024]{1,0:T(8,128)S(1)}, u32[]{:S(2)}, u32[]{:S(2)}) %collective-permute-start) | collective-permute-done | bytes 294944 | tf_op jit(solution)/shard_map/ppermute | solution.py:290
  19.3 0.0 collective-permute-done.1.below_ref
  19.3 0.0 copy-done.3
  19.3 0.0 copy-done.4
  19.3 0.0 copy-done.5
  19.3 4.6 %shard_map.125 = (f32[32,4096]{1,0:T(8,128)S(1)}, f32[2,8,64,256]{3,2,1,0:T(8,128)S(1)}) custom-call(s32[3]{0:T(128)S(1)} %pad_add_fusion.place_ref, f32[1]{0:T(128)S(6)} %copy.20.weight_ref, f32[32,4096]{1,0:T(8,128)S(1)} %shard_map.123.own_ref, f32[72,1024]{1,0:T(8,128)S(1)} %collective-permute-done.above_ref, ...), custom_call_target="tpu_custom_call" | custom-call | tf_op jit(solution)/shard_map/pallas_call | solution.py:337
  23.9 0.1 collective-permute-start.2
  24.0 1.9 %collective-permute-done.2 = f32[8,64,256]{2,1,0:T(8,128)S(1)} collective-permute-done((f32[8,64,256]{2,1,0:T(8,128)S(1)}, f32[8,64,256]{2,1,0:T(8,128)S(1)}, u32[]{:S(2)}, u32[]{:S(2)}) %collective-permute-start.2) | collective-permute-done | bytes 524320 | tf_op jit(solution)/shard_map/ppermute | solution.py:275
  25.9 0.1 bitcast_add_fusion
  26.0 15.0 %all_to_all.10 = f32[8,64,256]{2,1,0:T(8,128)S(1)} all-to-all(f32[8,64,256]{2,1,0:T(8,128)S(1)} %bitcast_add_fusion), channel_id=1, replica_groups={{0,32,64,96,128,160,192,224},{16,48,80,112,144,176,208,240},{1,33,65,97..., dimensions={0} | all-to-all | bytes 1048576 | tf_op jit(solution)/shard_map/all_to_all | solution.py:279
  41.1 9.8 %all_to_all.11.mine_ref = f32[8,32,256]{2,1,0:T(8,128)S(1)} all-to-all(f32[8,32,256]{2,1,0:T(8,128)S(1)} %broadcast_in_dim.31), channel_id=1, replica_groups={{0,32,64,96,128,160,192,224},{16,48,80,112,144,176,208,240},{1,33,65,97..., dimensions={0} | all-to-all | bytes 524288 | tf_op jit(solution)/shard_map/all_to_all | solution.py:279
  50.9 0.0 collective-permute-start.3
  50.9 1.5 %collective-permute-done.3.other_ref = f32[8,32,256]{2,1,0:T(8,128)S(1)} collective-permute-done((f32[8,32,256]{2,1,0:T(8,128)S(1)}, f32[8,32,256]{2,1,0:T(8,128)S(1)}, u32[]{:S(2)}, u32[]{:S(2)}) %collective-permute-start.3) | collective-permute-done | bytes 262176 | tf_op jit(solution)/shard_map/ppermute | solution.py:275
  52.4 0.6 shard_map.126
  53.0 5.7 %collective-permute-start.4 = (f32[40,1024]{1,0:T(8,128)S(1)}, f32[40,1024]{1,0:T(8,128)S(1)}, u32[]{:S(2)}, u32[]{:S(2)}) collective-permute-start(f32[40,1024]{1,0:T(8,128)S(1)} %get-tuple-element.23), channel_id=1, source_target_pairs={{0,1},{1,2},{2,3},{3,4},{4,5},{5,6},{6,7},{7,8},{8,9},{9,10},{10,1... | collective-permute-start | bytes 491528 | tf_op jit(solution)/shard_map/ppermute | solution.py:290
  58.7 0.0 collective-permute-start.5
  58.7 1.8 %shard_map.127.own_ref = f32[32,4096]{1,0:T(8,128)S(1)} custom-call(f32[32,4096]{1,0:T(8,128)S(1)} %get-tuple-element.21.own_ref, bf16[192,512]{1,0:T(8,128)(2,1)S(1)} %get-tuple-element.22.band_ref), custom_call_target="tpu_custom_call" | custom-call | tf_op jit(solution)/shard_map/pallas_call | solution.py:364
  60.5 2.0 %collective-permute-done.4.above_ref = f32[40,1024]{1,0:T(8,128)S(1)} collective-permute-done((f32[40,1024]{1,0:T(8,128)S(1)}, f32[40,1024]{1,0:T(8,128)S(1)}, u32[]{:S(2)}, u32[]{:S(2)}) %collective-permute-start.4) | collective-permute-done | bytes 163872 | tf_op jit(solution)/shard_map/ppermute | solution.py:290
  62.5 5.8 %collective-permute-done.5.below_ref = f32[40,1024]{1,0:T(8,128)S(1)} collective-permute-done((f32[40,1024]{1,0:T(8,128)S(1)}, f32[40,1024]{1,0:T(8,128)S(1)}, u32[]{:S(2)}, u32[]{:S(2)}) %collective-permute-start.5) | collective-permute-done | bytes 163872 | tf_op jit(solution)/shard_map/ppermute | solution.py:294
  68.3 3.2 %shard_map.128 = (f32[32,4096]{1,0:T(8,128)}, f32[32,256]{1,0:T(8,128)}) custom-call(s32[3]{0:T(128)S(1)} %pad_add_fusion.place_ref, f32[32,4096]{1,0:T(8,128)S(1)} %shard_map.127.own_ref, f32[40,1024]{1,0:T(8,128)S(1)} %collective-permute-done.4.above_ref, f32[40,1024]{1,0:T(8,128)S(1)} %collective-permute-done.5.below_ref, f32[32,256]{1,0:T(8,128)S(1)} %fusion.3.coadd_ref, ...), custom_call_target="tpu_custom_call" | custom-call | tf_op jit(solution)/shard_map/pallas_call | solution.py:365
  (9 shorter events, 0.1 us)
Async XLA Ops:
  0.6 7.2 %copy-start = (f32[9,21,21]{2,1,0:T(8,128)S(1)}, f32[9,21,21]{2,1,0:T(8,128)}, u32[]{:S(2)}) copy-start(f32[9,21,21]{2,1,0:T(8,128)} %param.12) | copy-start | bytes 47632
  0.6 1.1 %copy-start.1 = (f32[1,32,4096]{2,1,0:T(8,128)S(1)}, f32[1,32,4096]{2,1,0:T(8,128)}, u32[]{:S(2)}) copy-start(f32[1,32,4096]{2,1,0:T(8,128)} %param.11) | copy-start | bytes 1572868
  1.7 10.8 %copy-start.2 = (f32[1,32,4096]{2,1,0:T(8,128)S(1)}, f32[1,32,4096]{2,1,0:T(8,128)}, u32[]{:S(2)}) copy-start(f32[1,32,4096]{2,1,0:T(8,128)} %param.11) | copy-start | bytes 1572868
  2.5 16.8 %collective-permute-start = (f32[72,1024]{1,0:T(8,128)}, f32[72,1024]{1,0:T(8,128)S(1)}, u32[]{:S(2)}, u32[]{:S(2)}) collective-permute-start(f32[72,1024]{1,0:T(8,128)} %get-tuple-element.16), channel_id=1, source_target_pairs={{0,1},{1,2},{2,3},{3,4},{4,5},{5,6},{6,7},{7,8},{8,9},{9,10},{10,1... | collective-permute-start | bytes 884744 | tf_op jit(solution)/shard_map/ppermute | solution.py:290
  6.5 12.8 %collective-permute-start.1 = (f32[72,1024]{1,0:T(8,128)S(1)}, f32[72,1024]{1,0:T(8,128)S(1)}, u32[]{:S(2)}, u32[]{:S(2)}) collective-permute-start(f32[72,1024]{1,0:T(8,128)S(1)} %get-tuple-element.17), channel_id=1, source_target_pairs={{1,0},{2,1},{3,2},{4,3},{5,4},{6,5},{7,6},{8,7},{9,8},{10,9},{11,1... | collective-permute-start | bytes 884744 | tf_op jit(solution)/shard_map/ppermute | solution.py:294
  7.1 0.7 copy-start.9
  7.8 0.7 copy-start.8
  8.7 0.7 copy-start.6
  9.6 0.7 copy-start.7
  12.5 6.7 %copy-start.3 = (s32[1,32,4096]{2,1,0:T(8,128)S(1)}, s32[1,32,4096]{2,1,0:T(8,128)}, u32[]{:S(2)}) copy-start(s32[1,32,4096]{2,1,0:T(8,128)} %param.20) | copy-start | bytes 1572868
  12.5 6.7 %copy-start.4 = (f32[1,8,4096]{2,1,0:T(8,128)S(1)}, f32[1,8,4096]{2,1,0:T(8,128)}, u32[]{:S(2)}) copy-start(f32[1,8,4096]{2,1,0:T(8,128)} %param.18) | copy-start | bytes 393220
  12.5 6.7 %copy-start.5 = (s32[1,4096]{1,0:T(1,128)S(1)}, s32[1,4096]{1,0:T(1,128)}, u32[]{:S(2)}) copy-start(s32[1,4096]{1,0:T(1,128)} %starts_ref.1) | copy-start | bytes 49156
  23.9 2.0 %collective-permute-start.2 = (f32[8,64,256]{2,1,0:T(8,128)S(1)}, f32[8,64,256]{2,1,0:T(8,128)S(1)}, u32[]{:S(2)}, u32[]{:S(2)}) collective-permute-start(f32[8,64,256]{2,1,0:T(8,128)S(1)} %slice_bitcast_fusion), channel_id=1, source_target_pairs={{0,16},{16,0},{32,48},{48,32},{64,80},{80,64},{96,112},{112,96},{1... | collective-permute-start | bytes 1572872 | tf_op jit(solution)/shard_map/ppermute | solution.py:275
  50.9 1.5 %collective-permute-start.3 = (f32[8,32,256]{2,1,0:T(8,128)S(1)}, f32[8,32,256]{2,1,0:T(8,128)S(1)}, u32[]{:S(2)}, u32[]{:S(2)}) collective-permute-start(f32[8,32,256]{2,1,0:T(8,128)S(1)} %all_to_all.11.mine_ref), channel_id=1, source_target_pairs={{0,16},{16,0},{32,48},{48,32},{64,80},{80,64},{96,112},{112,96},{1... | collective-permute-start | bytes 786440 | tf_op jit(solution)/shard_map/ppermute | solution.py:275
  53.0 9.5 %collective-permute-start.4 = (f32[40,1024]{1,0:T(8,128)S(1)}, f32[40,1024]{1,0:T(8,128)S(1)}, u32[]{:S(2)}, u32[]{:S(2)}) collective-permute-start(f32[40,1024]{1,0:T(8,128)S(1)} %get-tuple-element.23), channel_id=1, source_target_pairs={{0,1},{1,2},{2,3},{3,4},{4,5},{5,6},{6,7},{7,8},{8,9},{9,10},{10,1... | collective-permute-start | bytes 491528 | tf_op jit(solution)/shard_map/ppermute | solution.py:290
  58.7 9.6 %collective-permute-start.5 = (f32[40,1024]{1,0:T(8,128)S(1)}, f32[40,1024]{1,0:T(8,128)S(1)}, u32[]{:S(2)}, u32[]{:S(2)}) collective-permute-start(f32[40,1024]{1,0:T(8,128)S(1)} %get-tuple-element.24), channel_id=1, source_target_pairs={{1,0},{2,1},{3,2},{4,3},{5,4},{6,5},{7,6},{8,7},{9,8},{10,9},{11,1... | collective-permute-start | bytes 491528 | tf_op jit(solution)/shard_map/ppermute | solution.py:294

commit v2 on v1

--- a/solution.py
+++ b/solution.py
@@ -18,6 +18,9 @@
 BLOCK = 256
 GROUP = 4
 STEPS = 6
+THIN = 16
+THIN_GROUP = 5
+THIN_STEPS = 5
 FRAME = COLS + 128
 LEFT = 640
 F32 = jnp.float32
@@ -28,15 +31,18 @@
 SM = pl.BlockSpec(memory_space=pltpu.SMEM)
 
 
-def call(kernel, outs, ins, scratch=(), cost=None):
+ANY = pl.BlockSpec(memory_space=pl.ANY)
+
+
+def call(kernel, outs, ins, scratch=(), places=None, aliases=None):
     return pl.pallas_call(
         kernel,
         out_shape=outs,
         in_specs=ins,
-        out_specs=jax.tree.map(lambda _: VM, outs),
+        out_specs=jax.tree.map(lambda _: VM, outs) if places is None else places,
         scratch_shapes=list(scratch),
+        input_output_aliases=aliases or {},
         compiler_params=pltpu.CompilerParams(vmem_limit_bytes=VMEM_LIMIT),
-        cost_estimate=cost,
     )
 
 
@@ -44,13 +50,18 @@
     return jax.ShapeDtypeStruct(shape, dtype)
 
 
-def pack_kernel(x_ref, up_ref, down_ref):
+def down_kernel(x_ref, down_ref):
     for q in range(4):
         cols = pl.ds(q * CHUNK, CHUNK)
         down_ref[16 * q : 16 * q + 16, :] = x_ref[16:32, cols]
-        up_ref[16 * q : 16 * q + 16, :] = x_ref[0:16, cols]
         down_ref[64 + q : 65 + q, :] = x_ref[15:16, cols]
         down_ref[68 + q : 69 + q, :] = jnp.zeros((1, CHUNK), F32)
+
+
+def up_kernel(x_ref, up_ref):
+    for q in range(4):
+        cols = pl.ds(q * CHUNK, CHUNK)
+        up_ref[16 * q : 16 * q + 16, :] = x_ref[0:16, cols]
         up_ref[64 + q : 65 + q, :] = x_ref[16:17, cols]
         up_ref[68 + q : 69 + q, :] = x_ref[17:18, cols]
 
@@ -71,11 +82,32 @@
         ref[rows, slot] = parts[ROWS * lag : ROWS * (lag + 1)]
 
 
-def put_both(own_ref, edge_ref, values):
+def put_thin_bands(ref, values, low, row, valid):
+    lanes = lax.broadcasted_iota(jnp.int32, values.shape, 1)
+    span = jnp.where(valid, between(values, low, low + THIN, -low), 0.0)
+    spans = span + pltpu.roll(span, THIN, 1) + pltpu.roll(span, 2 * THIN, 1)
+    high = spans.astype(BF16).astype(F32)
+    parts = jnp.where(lanes < 2 * THIN, high, spans - high)
+    total = None
+    for part in range(THIN_GROUP):
+        rows = []
+        for step in range(THIN_STEPS):
+            at = ROWS * (THIN_GROUP * step + part) + row
+            known = at < values.shape[0]
+            rows.append(parts[at : at + THIN] if known else jnp.zeros((THIN, SLOT), F32))
+        stacked = jnp.concatenate(rows, axis=0)
+        wide = jnp.concatenate([stacked, jnp.zeros_like(stacked)], axis=1)
+        moved = pltpu.roll(wide, 3 * THIN * part, 1) if part else wide
+        total = moved if total is None else total + moved
+    ref[...] = total.astype(BF16)
+
+
+def put_both(own_ref, edge_ref, values, has_above, has_below):
     put_bands(own_ref, between(values, BASE, BASE + ROWS, -BASE))
-    edge = between(values, BASE - 16, BASE, 16 - BASE)
-    edge = edge + between(values, BASE + ROWS, BASE + ROWS + 18, 16 - BASE - ROWS)
-    put_bands(edge_ref, edge + between(values, BASE - 17, BASE - 16, 39 - (BASE - 17)))
+    above = between(values, BASE - 16, BASE, 16 - BASE)
+    above = above + between(values, BASE - 17, BASE - 16, 39 - (BASE - 17))
+    below = between(values, BASE + ROWS, BASE + ROWS + 18, 16 - BASE - ROWS)
+    put_bands(edge_ref, jnp.where(has_above, above, 0.0) + jnp.where(has_below, below, 0.0))
 
 
 def skewed(ref, lag, rows, shift):
@@ -83,15 +115,21 @@
     return pltpu.roll(values, shift, 1, stride=1, stride_axis=0)
 
 
-def bands_kernel(k1_ref, k2_ref, mix_ref, own1_ref, edge1_ref, own2_ref, edge2_ref):
+def bands_kernel(
+    place_ref, k1_ref, k2_ref, mix_ref, own1_ref, edge1_ref, own2_ref, above2_ref, below2_ref
+):
+    has_above, has_below = place_ref[2] > 0, place_ref[2] < 15
     first = jnp.concatenate([skewed(k1_ref, lag, 48, 0) for lag in range(24)], axis=1)
     merged = jnp.dot(
         mix_ref[...], first, precision=lax.Precision.HIGHEST, preferred_element_type=F32
     )
     slots = [merged[:, SLOT * lag : SLOT * (lag + 1)] for lag in range(24)]
-    put_both(own1_ref, edge1_ref, jnp.concatenate(slots, axis=0))
+    put_both(own1_ref, edge1_ref, jnp.concatenate(slots, axis=0), has_above, has_below)
     slots = [skewed(k2_ref, lag, ROWS, 8) for lag in range(24)]
-    put_both(own2_ref, edge2_ref, jnp.concatenate(slots, axis=0))
+    values = jnp.concatenate(slots, axis=0)
+    put_bands(own2_ref, between(values, BASE, BASE + ROWS, -BASE))
+    put_thin_bands(above2_ref, values, BASE - THIN, 0, has_above)
+    put_thin_bands(below2_ref, values, BASE + ROWS, ROWS - THIN, has_below)
 
 
 def coverage(starts, offset, q):
@@ -107,20 +145,20 @@
 
 
 def clear(frame_ref, row):
-    frame_ref[:, COLS:FRAME] = jnp.zeros((SPAN, FRAME - COLS), F32)
-    frame_ref[row:SPAN, 0:COLS] = jnp.zeros((SPAN - row, COLS), F32)
-
-
-def put_wide(frame_ref, row, ref, rows, valid):
-    for q in range(4):
-        values = jnp.where(valid, ref[rows * q : rows * (q + 1), :], 0.0)
-        frame_ref[row : row + rows, q * CHUNK : (q + 1) * CHUNK] = values
-
-
-def put_thin(frame_ref, row, ref, at, valid):
-    for q in range(4):
-        values = jnp.where(valid, ref[at + q : at + q + 1, :], 0.0)
-        frame_ref[row : row + 1, q * CHUNK : (q + 1) * CHUNK] = values
+    rows = frame_ref.shape[0]
+    frame_ref[:, COLS:FRAME] = jnp.zeros((rows, FRAME - COLS), F32)
+    frame_ref[row:rows, 0:COLS] = jnp.zeros((rows - row, COLS), F32)
+
+
+def put_wide(frame_ref, row, ref, rows):
+    for q in range(4):
+        cols = pl.ds(q * CHUNK, CHUNK)
+        frame_ref[row : row + rows, cols] = ref[rows * q : rows * (q + 1), :]
+
+
+def put_thin(frame_ref, row, ref, at):
+    for q in range(4):
+        frame_ref[row : row + 1, q * CHUNK : (q + 1) * CHUNK] = ref[at + q : at + q + 1, :]
 
 
 def split_rows(frame_ref, halves_ref):
@@ -171,14 +209,12 @@
     halves_ref,
     source_ref,
 ):
-    band = place_ref[2]
-    has_above, has_below = band > 0, band < 15
     clear(frame_ref, 32)
-    put_wide(frame_ref, 0, above_ref, 16, has_above)
-    put_wide(frame_ref, 16, below_ref, 16, has_below)
-    put_thin(frame_ref, 32, below_ref, 64, has_below)
-    put_thin(frame_ref, 33, below_ref, 68, has_below)
-    put_thin(frame_ref, 39, above_ref, 64, has_above)
+    put_wide(frame_ref, 0, above_ref, 16)
+    put_wide(frame_ref, 16, below_ref, 16)
+    put_thin(frame_ref, 32, below_ref, 64)
+    put_thin(frame_ref, 33, below_ref, 68)
+    put_thin(frame_ref, 39, above_ref, 64)
     split_rows(frame_ref, halves_ref)
 
     source_ref[:, 0:LEFT] = jnp.zeros((ROWS, LEFT), F32)
@@ -240,31 +276,75 @@
             up_ref[at : at + 1, :] = diff_ref[8 + extra : 9 + extra, cols]
 
 
-def clean_kernel(
-    place_ref,
+def thin_edges(own_ref, row, band_ref, out_ref, frame_ref, halves_ref, done_ref, sems):
+    frame = frame_ref[...]
+    for part in range(THIN_GROUP):
+        moved = pltpu.roll(frame, HALF - part, 1)
+        high = moved.astype(BF16).astype(F32)
+        spans = jnp.concatenate([high, moved - high, high], axis=0)
+        halves_ref[3 * THIN * part : 3 * THIN * (part + 1), :] = spans.astype(BF16)
+    used = 3 * THIN * THIN_GROUP
+    halves_ref[used:256, :] = jnp.zeros((256 - used, FRAME), BF16)
+    width = CHUNK + 128
+    copies = []
+    for q in range(4):
+        cols = pl.ds(q * CHUNK, CHUNK)
+        lags = jnp.dot(
+            band_ref[...],
+            halves_ref[:, q * CHUNK : q * CHUNK + width],
+            preferred_element_type=F32,
+        )
+        total = own_ref[row : row + THIN, cols] + lags[0:THIN, :CHUNK]
+        for step in range(1, THIN_STEPS):
+            lag = lags[THIN * step : THIN * (step + 1), :]
+            total = total + pltpu.roll(lag, width - THIN_GROUP * step, 1)[:, :CHUNK]
+        done_ref[:, cols] = total
+        copy = pltpu.make_async_copy(
+            done_ref.at[:, cols], out_ref.at[pl.ds(row, THIN), cols], sems.at[q]
+        )
+        copy.start()
+        copies.append(copy)
+    for copy in copies:
+        copy.wait()
+
+
+def above_kernel(
     own_ref,
     above_ref,
-    below_ref,
     coadd_ref,
     band_ref,
     out_ref,
     template_ref,
     frame_ref,
     halves_ref,
+    done_ref,
+    sems,
 ):
     template_ref[...] = coadd_ref[...]
-    band = place_ref[2]
-    has_above, has_below = band > 0, band < 15
     clear(frame_ref, 0)
-    put_wide(frame_ref, 8, above_ref, 8, has_above)
-    put_wide(frame_ref, 16, below_ref, 8, has_below)
+    put_wide(frame_ref, 8, above_ref, 8)
     for extra in range(2):
-        put_thin(frame_ref, 6 + extra, above_ref, 32 + 4 * extra, has_above)
-        put_thin(frame_ref, 24 + extra, below_ref, 32 + 4 * extra, has_below)
-    split_rows(frame_ref, halves_ref)
-    for q in range(4):
-        cols = pl.ds(q * CHUNK, CHUNK)
-        out_ref[:, cols] = own_ref[:, cols] + correlate_chunk(band_ref, halves_ref, q)
+        put_thin(frame_ref, 6 + extra, above_ref, 32 + 4 * extra)
+    thin_edges(own_ref, 0, band_ref, out_ref, frame_ref, halves_ref, done_ref, sems)
+
+
+def below_kernel(
+    own_ref,
+    below_ref,
+    band_ref,
+    begun_ref,
+    out_ref,
+    frame_ref,
+    halves_ref,
+    done_ref,
+    sems,
+):
+    clear(frame_ref, 0)
+    put_wide(frame_ref, 0, below_ref, 8)
+    for extra in range(2):
+        put_thin(frame_ref, 8 + extra, below_ref, 32 + 4 * extra)
+    row = ROWS - THIN
+    thin_edges(own_ref, row, band_ref, out_ref, frame_ref, halves_ref, done_ref, sems)
 
 
 def by_lag(kernel):
@@ -313,9 +393,8 @@
     band_at = band * ROWS
     place = jnp.stack([col_offsets[0], visit % 2, band]).astype(jnp.int32)
 
-    up, down = call(pack_kernel, (sds(72, CHUNK), sds(72, CHUNK)), [VM])(pixels)
-    above = to_next(down)
-    below = to_previous(up)
+    above = to_next(call(down_kernel, sds(72, CHUNK), [VM])(pixels))
+    below = to_previous(call(up_kernel, sds(72, CHUNK), [VM])(pixels))
 
     kernel = jnp.einsum(
         "b,bij->ij", basis_coeffs[0], basis_kernels, precision=lax.Precision.HIGHEST
@@ -325,9 +404,11 @@
     inside = (matched_row + band_at >= 0) & (matched_row + band_at < 16 * ROWS)
     hits = tap_at[None] == jnp.arange(TAPS, dtype=jnp.int32)[:, None, None]
     mix = jnp.sum(jnp.where(hits & inside[None], row_taps[0][:, :, None], 0.0), axis=0)
-    own_first, edge_first, own_second, edge_second = call(
-        bands_kernel, (sds(STEPS * ROWS, GROUP * SLOT, dtype=BF16),) * 4, [VM] * 3
-    )(by_lag(kernel), by_lag(decorrelation[0]), mix)
+    bands = sds(STEPS * ROWS, GROUP * SLOT, dtype=BF16)
+    thin_bands = sds(THIN_STEPS * THIN, 256, dtype=BF16)
+    own_first, edge_first, own_second, above_second, below_second = call(
+        bands_kernel, (bands, bands, bands, thin_bands, thin_bands), [SM] + [VM] * 3
+    )(place, by_lag(kernel), by_lag(decorrelation[0]), mix)
 
     frames = [
         pltpu.VMEM((SPAN, FRAME), F32),
@@ -362,9 +443,22 @@
     )(place, warped, mine, other)
     above, below = to_next(down), to_previous(up)
     own_part = call(own_kernel, sds(ROWS, COLS), [VM] * 2, frames)(difference, own_second)
-    cleaned, template = call(
-        clean_kernel, (sds(ROWS, COLS), sds(ROWS, BLOCK)), [SM] + [VM] * 5, frames
-    )(place, own_part, above, below, coadd, edge_second)
+    thin_frames = [
+        pltpu.VMEM((THIN, FRAME), F32),
+        pltpu.VMEM((256, FRAME), BF16),
+        pltpu.VMEM((THIN, COLS), F32),
+        pltpu.SemaphoreType.DMA((4,)),
+    ]
+    begun, template = call(
+        above_kernel,
+        (sds(ROWS, COLS), sds(ROWS, BLOCK)),
+        [VM] * 4,
+        thin_frames,
+        (ANY, VM),
+    )(own_part, above, coadd, above_second)
+    cleaned = call(
+        below_kernel, sds(ROWS, COLS), [VM] * 3 + [ANY], thin_frames, ANY, {3: 0}
+    )(own_part, below, below_second, begun)
     return cleaned[None], template
 
 

time: 71.8 us -> 70.2 us (0.978)
  the two profiles are of different devices: /device:TPU:102 before, /device:TPU:1 now
where the time goes in v2:
time: 70.2 us; the launch traced here: 69.9 us
  blocking collectives  22.4 us (32%)
  starting transfers between devices  19.6 us (28%)
  Pallas kernels  15.2 us (22%)
  waiting for transfers between devices  5.9 us (8%)
  local copies, waits for them, and re-layouts  3.93 us (6%)
  between operations  2.29 us (3%)
    all_to_all x2, blocking collectives, over_chips(): lax.all_to_all(blocks, 'visit', split_axis=0, concat_axis=0, axis_index_g...  22.4 us
    ppermute x2, starting transfers between devices, to_previous(): return lax.ppermute(values, 'row', [((i + 1) % 16, i) for i in range(16)])  10.9 us
    pallas_call x1, Pallas kernels, on_device(): call(warp_kernel, (sds(ROWS, COLS), sds(2, 8, 2 * ROWS, BLOCK)), [SM, SM]...  4.57 us
    ppermute x2, starting transfers between devices, swap(): return lax.ppermute(values, 'visit', [(i, i ^ step) for i in range(16)])  4.44 us
    ppermute x2, starting transfers between devices, to_next(): return lax.ppermute(values, 'row', [(i, (i + 1) % 16) for i in range(16)])  4.24 us
    unnamed x21, local copies, waits for them, and re-layouts  3.63 us
    ppermute x2, waiting for transfers between devices, swap(): return lax.ppermute(values, 'visit', [(i, i ^ step) for i in range(16)])  2.7 us
    pallas_call x1, Pallas kernels, on_device(): call(bands_kernel, (bands, bands, bands, thin_bands, thin_bands), [SM] +...  2.65 us
  transfers between devices with their start and end apart: 6, of which 4 were waited for; matrix products, arithmetic and copies ran while one was open for 1% of the time, Pallas kernels for 12%

profile of v2, /device:TPU:1, one launch (start us, length us, event | category | flops | bytes accessed | tf_op | source)
XLA Modules:
  0.0 69.9 jit_solution(1567494286068727531)
XLA Ops:
  0.6 0.0 copy-start
  0.6 0.0 copy-start.1
  0.7 1.1 %copy-done.1 = f32[1,32,4096]{2,1,0:T(8,128)S(1)} copy-done((f32[1,32,4096]{2,1,0:T(8,128)S(1)}, f32[1,32,4096]{2,1,0:T(8,128)}, u32[]{:S(2)}) %copy-start.1) | copy-done | bytes 524312
  1.8 0.0 copy-start.2
  1.8 3.7 %collective-permute-start = (f32[72,1024]{1,0:T(8,128)S(1)}, f32[72,1024]{1,0:T(8,128)S(1)}, u32[]{:S(2)}, u32[]{:S(2)}) collective-permute-start(f32[72,1024]{1,0:T(8,128)S(1)} %shard_map.124), channel_id=1, source_target_pairs={{0,1},{1,2},{2,3},{3,4},{4,5},{5,6},{6,7},{7,8},{8,9},{9,10},{10,1... | collective-permute-start | bytes 884744 | tf_op jit(solution)/shard_map/ppermute | solution.py:370
  5.4 5.4 %collective-permute-start.1 = (f32[72,1024]{1,0:T(8,128)S(1)}, f32[72,1024]{1,0:T(8,128)S(1)}, u32[]{:S(2)}, u32[]{:S(2)}) collective-permute-start(f32[72,1024]{1,0:T(8,128)S(1)} %shard_map.125), channel_id=1, source_target_pairs={{1,0},{2,1},{3,2},{4,3},{5,4},{6,5},{7,6},{8,7},{9,8},{10,9},{11,1... | collective-permute-start | bytes 884744 | tf_op jit(solution)/shard_map/ppermute | solution.py:374
  12.1 0.0 copy-start.9
  12.2 0.6 copy-done.9
  12.8 0.0 copy-done
  12.8 0.6 copy-done.8
  13.5 0.2 fusion
  13.7 0.0 copy-start.6
  13.7 0.1 copy.17
  13.8 0.6 copy-done.6
  14.4 0.1 copy.15
  14.5 0.1 pad.7.k1_ref
  14.5 0.1 pad.8.k2_ref
  14.6 0.1 pad_add_fusion.place_ref
  14.7 0.1 broadcast_subtract_fusion
  14.8 0.5 copy-done.7
  15.3 0.1 select_reduce_fusion.mix_ref
  15.4 2.6 %shard_map.122 = (bf16[192,512]{1,0:T(8,128)(2,1)S(1)}, bf16[192,512]{1,0:T(8,128)(2,1)S(1)}, bf16[192,512]{1,0:T(8,128)(2,1)S(1)}, bf16[80,256]{1,0:T(8,128)(2,1)S(1)}, bf16[80,256]{1,0:T(8,128)(2,1)S(1)}) custom-call(s32[3]{0:T(128)S(1)} %pad_add_fusion.place_ref, f32[24,128]{1,0:T(8,128)S(1)} %pad.7.k1_ref, f32[24,128]{1,0:T(8,128)S(1)} %pad.8.k2_ref, ...), custom_call_target="tpu_custom_call" | custom-call | tf_op jit(solution)/shard_map/pallas_call | solution.py:409
  18.1 0.0 copy-done.2
  18.1 0.0 copy-start.3
  18.1 0.0 copy-start.4
  18.1 0.0 copy-start.5
  18.1 1.8 %shard_map.123.own_ref = f32[32,4096]{1,0:T(8,128)S(1)} custom-call(f32[32,4096]{1,0:T(8,128)S(1)} %bitcast.26, bf16[192,512]{1,0:T(8,128)(2,1)S(1)} %get-tuple-element.14.band_ref), custom_call_target="tpu_custom_call" | custom-call | tf_op jit(solution)/shard_map/pallas_call | solution.py:417
  19.9 0.0 collective-permute-done.above_ref
  19.9 1.0 %collective-permute-done.1.below_ref = f32[72,1024]{1,0:T(8,128)S(1)} collective-permute-done((f32[72,1024]{1,0:T(8,128)S(1)}, f32[72,1024]{1,0:T(8,128)S(1)}, u32[]{:S(2)}, u32[]{:S(2)}) %collective-permute-start.1) | collective-permute-done | bytes 294944 | tf_op jit(solution)/shard_map/ppermute | solution.py:374
  20.9 0.0 copy-done.3
  20.9 0.0 copy-done.4
  20.9 0.0 copy-done.5
  20.9 4.6 %shard_map.126 = (f32[32,4096]{1,0:T(8,128)S(1)}, f32[2,8,64,256]{3,2,1,0:T(8,128)S(1)}) custom-call(s32[3]{0:T(128)S(1)} %pad_add_fusion.place_ref, f32[1]{0:T(128)S(6)} %copy.22.weight_ref, f32[32,4096]{1,0:T(8,128)S(1)} %shard_map.123.own_ref, f32[72,1024]{1,0:T(8,128)S(1)} %collective-permute-done.above_ref, ...), custom_call_target="tpu_custom_call" | custom-call | tf_op jit(solution)/shard_map/pallas_call | solution.py:418
  25.5 1.9 %collective-permute-start.2 = (f32[8,64,256]{2,1,0:T(8,128)S(1)}, f32[8,64,256]{2,1,0:T(8,128)S(1)}, u32[]{:S(2)}, u32[]{:S(2)}) collective-permute-start(f32[8,64,256]{2,1,0:T(8,128)S(1)} %slice_bitcast_fusion), channel_id=1, source_target_pairs={{0,16},{16,0},{32,48},{48,32},{64,80},{80,64},{96,112},{112,96},{1... | collective-permute-start | bytes 1572872 | tf_op jit(solution)/shard_map/ppermute | solution.py:355
  27.5 1.5 %collective-permute-done.2 = f32[8,64,256]{2,1,0:T(8,128)S(1)} collective-permute-done((f32[8,64,256]{2,1,0:T(8,128)S(1)}, f32[8,64,256]{2,1,0:T(8,128)S(1)}, u32[]{:S(2)}, u32[]{:S(2)}) %collective-permute-start.2) | collective-permute-done | bytes 524320 | tf_op jit(solution)/shard_map/ppermute | solution.py:355
  29.0 0.1 bitcast_add_fusion
  29.1 13.2 %all_to_all.10 = f32[8,64,256]{2,1,0:T(8,128)S(1)} all-to-all(f32[8,64,256]{2,1,0:T(8,128)S(1)} %bitcast_add_fusion), channel_id=1, replica_groups={{0,32,64,96,128,160,192,224},{16,48,80,112,144,176,208,240},{1,33,65,97..., dimensions={0} | all-to-all | bytes 1048576 | tf_op jit(solution)/shard_map/all_to_all | solution.py:359
  42.4 9.1 %all_to_all.11.mine_ref = f32[8,32,256]{2,1,0:T(8,128)S(1)} all-to-all(f32[8,32,256]{2,1,0:T(8,128)S(1)} %broadcast_in_dim.31), channel_id=1, replica_groups={{0,32,64,96,128,160,192,224},{16,48,80,112,144,176,208,240},{1,33,65,97..., dimensions={0} | all-to-all | bytes 524288 | tf_op jit(solution)/shard_map/all_to_all | solution.py:359
  51.6 2.5 %collective-permute-start.3 = (f32[8,32,256]{2,1,0:T(8,128)S(1)}, f32[8,32,256]{2,1,0:T(8,128)S(1)}, u32[]{:S(2)}, u32[]{:S(2)}) collective-permute-start(f32[8,32,256]{2,1,0:T(8,128)S(1)} %all_to_all.11.mine_ref), channel_id=1, source_target_pairs={{0,16},{16,0},{32,48},{48,32},{64,80},{80,64},{96,112},{112,96},{1... | collective-permute-start | bytes 786440 | tf_op jit(solution)/shard_map/ppermute | solution.py:355
  54.1 1.2 %collective-permute-done.3.other_ref = f32[8,32,256]{2,1,0:T(8,128)S(1)} collective-permute-done((f32[8,32,256]{2,1,0:T(8,128)S(1)}, f32[8,32,256]{2,1,0:T(8,128)S(1)}, u32[]{:S(2)}, u32[]{:S(2)}) %collective-permute-start.3) | collective-permute-done | bytes 262176 | tf_op jit(solution)/shard_map/ppermute | solution.py:355
  55.2 0.6 shard_map.127
  55.9 0.6 collective-permute-start.5
  56.5 5.6 %collective-permute-start.4 = (f32[40,1024]{1,0:T(8,128)S(1)}, f32[40,1024]{1,0:T(8,128)S(1)}, u32[]{:S(2)}, u32[]{:S(2)}) collective-permute-start(f32[40,1024]{1,0:T(8,128)S(1)} %get-tuple-element.20), channel_id=1, source_target_pairs={{1,0},{2,1},{3,2},{4,3},{5,4},{6,5},{7,6},{8,7},{9,8},{10,9},{11,1... | collective-permute-start | bytes 491528 | tf_op jit(solution)/shard_map/ppermute | solution.py:374
  62.0 1.8 %shard_map.128.own_ref = f32[32,4096]{1,0:T(8,128)S(1)} custom-call(f32[32,4096]{1,0:T(8,128)S(1)} %get-tuple-element.18.own_ref, bf16[192,512]{1,0:T(8,128)(2,1)S(1)} %get-tuple-element.19.band_ref), custom_call_target="tpu_custom_call" | custom-call | tf_op jit(solution)/shard_map/pallas_call | solution.py:445
  63.8 2.2 %collective-permute-done.5.above_ref = f32[40,1024]{1,0:T(8,128)S(1)} collective-permute-done((f32[40,1024]{1,0:T(8,128)S(1)}, f32[40,1024]{1,0:T(8,128)S(1)}, u32[]{:S(2)}, u32[]{:S(2)}) %collective-permute-start.5) | collective-permute-done | bytes 163872 | tf_op jit(solution)/shard_map/ppermute | solution.py:370
  66.1 2.1 %shard_map.129 = (f32[32,4096]{1,0:T(8,128)}, f32[32,256]{1,0:T(8,128)}) custom-call(f32[32,4096]{1,0:T(8,128)S(1)} %shard_map.128.own_ref, f32[40,1024]{1,0:T(8,128)S(1)} %collective-permute-done.5.above_ref, f32[32,256]{1,0:T(8,128)S(1)} %fusion.3.coadd_ref, bf16[80,256]{1,0:T(8,128)(2,1)S(1)} %get-tuple-element.23.band_ref), custom_call_target="tpu_custom_call" | custom-call | tf_op jit(solution)/shard_map/pallas_call | solution.py:452
  68.2 0.0 collective-permute-done.4.below_ref
  68.2 1.5 %shard_map.130 = f32[32,4096]{1,0:T(8,128)} custom-call(f32[32,4096]{1,0:T(8,128)S(1)} %shard_map.128.own_ref, f32[40,1024]{1,0:T(8,128)S(1)} %collective-permute-done.4.below_ref, bf16[80,256]{1,0:T(8,128)(2,1)S(1)} %get-tuple-element.21.band_ref, f32[32,4096]{1,0:T(8,128)} %get-tuple-element.24.begun_ref), custom_call_target="tpu_custom_call", output_to_operand_aliasing={{}: (3, {})} | custom-call | tf_op jit(solution)/shard_map/pallas_call | solution.py:459
  (11 shorter events, 0.2 us)
Async XLA Ops:
  0.6 12.2 %copy-start = (f32[9,21,21]{2,1,0:T(8,128)S(1)}, f32[9,21,21]{2,1,0:T(8,128)}, u32[]{:S(2)}) copy-start(f32[9,21,21]{2,1,0:T(8,128)} %param.12) | copy-start | bytes 47632
  0.6 1.1 %copy-start.1 = (f32[1,32,4096]{2,1,0:T(8,128)S(1)}, f32[1,32,4096]{2,1,0:T(8,128)}, u32[]{:S(2)}) copy-start(f32[1,32,4096]{2,1,0:T(8,128)} %param.11) | copy-start | bytes 1572868
  1.8 16.3 %copy-start.2 = (f32[1,32,4096]{2,1,0:T(8,128)S(1)}, f32[1,32,4096]{2,1,0:T(8,128)}, u32[]{:S(2)}) copy-start(f32[1,32,4096]{2,1,0:T(8,128)} %param.11) | copy-start | bytes 1572868
  1.8 18.2 %collective-permute-start = (f32[72,1024]{1,0:T(8,128)S(1)}, f32[72,1024]{1,0:T(8,128)S(1)}, u32[]{:S(2)}, u32[]{:S(2)}) collective-permute-start(f32[72,1024]{1,0:T(8,128)S(1)} %shard_map.124), channel_id=1, source_target_pairs={{0,1},{1,2},{2,3},{3,4},{4,5},{5,6},{6,7},{7,8},{8,9},{9,10},{10,1... | collective-permute-start | bytes 884744 | tf_op jit(solution)/shard_map/ppermute | solution.py:370
  5.4 15.5 %collective-permute-start.1 = (f32[72,1024]{1,0:T(8,128)S(1)}, f32[72,1024]{1,0:T(8,128)S(1)}, u32[]{:S(2)}, u32[]{:S(2)}) collective-permute-start(f32[72,1024]{1,0:T(8,128)S(1)} %shard_map.125), channel_id=1, source_target_pairs={{1,0},{2,1},{3,2},{4,3},{5,4},{6,5},{7,6},{8,7},{9,8},{10,9},{11,1... | collective-permute-start | bytes 884744 | tf_op jit(solution)/shard_map/ppermute | solution.py:374
  12.1 0.7 copy-start.9
  12.8 0.7 copy-start.8
  13.7 0.7 %copy-start.6 = (f32[1,21,21]{2,0,1:T(1,128)S(1)}, f32[1,21,21]{2,0,1:T(1,128)}, u32[]{:S(2)}) copy-start(f32[1,21,21]{2,0,1:T(1,128)} %param.21) | copy-start | bytes 5296
  14.6 0.7 copy-start.7
  18.1 2.8 %copy-start.3 = (s32[1,32,4096]{2,1,0:T(8,128)S(1)}, s32[1,32,4096]{2,1,0:T(8,128)}, u32[]{:S(2)}) copy-start(s32[1,32,4096]{2,1,0:T(8,128)} %param.20) | copy-start | bytes 1572868
  18.1 2.8 %copy-start.4 = (f32[1,8,4096]{2,1,0:T(8,128)S(1)}, f32[1,8,4096]{2,1,0:T(8,128)}, u32[]{:S(2)}) copy-start(f32[1,8,4096]{2,1,0:T(8,128)} %param.18) | copy-start | bytes 393220
  18.1 2.8 %copy-start.5 = (s32[1,4096]{1,0:T(1,128)S(1)}, s32[1,4096]{1,0:T(1,128)}, u32[]{:S(2)}) copy-start(s32[1,4096]{1,0:T(1,128)} %starts_ref.1) | copy-start | bytes 49156
  25.5 3.5 %collective-permute-start.2 = (f32[8,64,256]{2,1,0:T(8,128)S(1)}, f32[8,64,256]{2,1,0:T(8,128)S(1)}, u32[]{:S(2)}, u32[]{:S(2)}) collective-permute-start(f32[8,64,256]{2,1,0:T(8,128)S(1)} %slice_bitcast_fusion), channel_id=1, source_target_pairs={{0,16},{16,0},{32,48},{48,32},{64,80},{80,64},{96,112},{112,96},{1... | collective-permute-start | bytes 1572872 | tf_op jit(solution)/shard_map/ppermute | solution.py:355
  51.6 3.7 %collective-permute-start.3 = (f32[8,32,256]{2,1,0:T(8,128)S(1)}, f32[8,32,256]{2,1,0:T(8,128)S(1)}, u32[]{:S(2)}, u32[]{:S(2)}) collective-permute-start(f32[8,32,256]{2,1,0:T(8,128)S(1)} %all_to_all.11.mine_ref), channel_id=1, source_target_pairs={{0,16},{16,0},{32,48},{48,32},{64,80},{80,64},{96,112},{112,96},{1... | collective-permute-start | bytes 786440 | tf_op jit(solution)/shard_map/ppermute | solution.py:355
  55.9 10.2 %collective-permute-start.5 = (f32[40,1024]{1,0:T(8,128)S(1)}, f32[40,1024]{1,0:T(8,128)S(1)}, u32[]{:S(2)}, u32[]{:S(2)}) collective-permute-start(f32[40,1024]{1,0:T(8,128)S(1)} %get-tuple-element.22), channel_id=1, source_target_pairs={{0,1},{1,2},{2,3},{3,4},{4,5},{5,6},{6,7},{7,8},{8,9},{9,10},{10,1... | collective-permute-start | bytes 491528 | tf_op jit(solution)/shard_map/ppermute | solution.py:370
  56.5 11.8 %collective-permute-start.4 = (f32[40,1024]{1,0:T(8,128)S(1)}, f32[40,1024]{1,0:T(8,128)S(1)}, u32[]{:S(2)}, u32[]{:S(2)}) collective-permute-start(f32[40,1024]{1,0:T(8,128)S(1)} %get-tuple-element.20), channel_id=1, source_target_pairs={{1,0},{2,1},{3,2},{4,3},{5,4},{6,5},{7,6},{8,7},{9,8},{10,9},{11,1... | collective-permute-start | bytes 491528 | tf_op jit(solution)/shard_map/ppermute | solution.py:374

commit v3 on v2

--- a/solution.py
+++ b/solution.py
@@ -185,6 +185,13 @@
     return total
 
 
+def own_and_template_kernel(
+    own_ref, band_ref, coadd_ref, out_ref, template_ref, frame_ref, halves_ref
+):
+    template_ref[...] = coadd_ref[...]
+    own_kernel(own_ref, band_ref, out_ref, frame_ref, halves_ref)
+
+
 def own_kernel(own_ref, band_ref, out_ref, frame_ref, halves_ref):
     clear(frame_ref, ROWS)
     frame_ref[0:ROWS, 0:COLS] = own_ref[...]
@@ -194,8 +201,8 @@
 
 
 def warp_kernel(
-    place_ref,
-    weight_ref,
+    place_source_ref,
+    weight_source_ref,
     own_ref,
     above_ref,
     below_ref,
@@ -208,7 +215,16 @@
     frame_ref,
     halves_ref,
     source_ref,
-):
+    place_ref,
+    weight_ref,
+    sems,
+):
+    fetches = [
+        pltpu.make_async_copy(place_source_ref, place_ref, sems.at[0]),
+        pltpu.make_async_copy(weight_source_ref, weight_ref, sems.at[1]),
+    ]
+    for fetch in fetches:
+        fetch.start()
     clear(frame_ref, 32)
     put_wide(frame_ref, 0, above_ref, 16)
     put_wide(frame_ref, 16, below_ref, 16)
@@ -225,6 +241,8 @@
             own_ref[:, q * CHUNK : (q + 1) * CHUNK] + edges
         )
 
+    for fetch in fetches:
+        fetch.wait()
     offset = place_ref[0]
     first = LEFT - 3 - offset
     aligned = first // 128
@@ -253,7 +271,7 @@
 
 
 def differ_kernel(
-    place_ref,
+    first_core_ref,
     own_ref,
     mine_ref,
     other_ref,
@@ -261,10 +279,11 @@
     up_ref,
     down_ref,
 ):
-    core = place_ref[1]
+    first_core = jnp.broadcast_to(first_core_ref[...], (ROWS, BLOCK)) > 0
     for b in range(16):
         cols = pl.ds(b * BLOCK, BLOCK)
-        coadd = jnp.where(core == b % 2, mine_ref[b // 2], other_ref[b // 2])
+        even, odd = (mine_ref, other_ref) if b % 2 == 0 else (other_ref, mine_ref)
+        coadd = jnp.where(first_core, even[b // 2], odd[b // 2])
         diff_ref[:, cols] = own_ref[:, cols] - coadd
     for q in range(4):
         cols = pl.ds(q * CHUNK, CHUNK)
@@ -311,16 +330,13 @@
 def above_kernel(
     own_ref,
     above_ref,
-    coadd_ref,
     band_ref,
     out_ref,
-    template_ref,
     frame_ref,
     halves_ref,
     done_ref,
     sems,
 ):
-    template_ref[...] = coadd_ref[...]
     clear(frame_ref, 0)
     put_wide(frame_ref, 8, above_ref, 8)
     for extra in range(2):
@@ -396,6 +412,7 @@
     above = to_next(call(down_kernel, sds(72, CHUNK), [VM])(pixels))
     below = to_previous(call(up_kernel, sds(72, CHUNK), [VM])(pixels))
 
+    first_core = jnp.full((1, BLOCK), visit % 2 == 0).astype(jnp.int32)
     kernel = jnp.einsum(
         "b,bij->ij", basis_coeffs[0], basis_kernels, precision=lax.Precision.HIGHEST
     )
@@ -418,8 +435,14 @@
     warped, weighted = call(
         warp_kernel,
         (sds(ROWS, COLS), sds(2, 8, 2 * ROWS, BLOCK)),
-        [SM, SM] + [VM] * 7,
-        frames + [pltpu.VMEM((ROWS, LEFT + COLS + 128), F32)],
+        [ANY, ANY] + [VM] * 7,
+        frames
+        + [
+            pltpu.VMEM((ROWS, LEFT + COLS + 128), F32),
+            pltpu.SMEM((3,), jnp.int32),
+            pltpu.SMEM((1,), F32),
+            pltpu.SemaphoreType.DMA((2,)),
+        ],
     )(
         place,
         visit_weights,
@@ -439,23 +462,21 @@
     difference, up, down = call(
         differ_kernel,
         (sds(ROWS, COLS), sds(40, CHUNK), sds(40, CHUNK)),
-        [SM] + [VM] * 3,
-    )(place, warped, mine, other)
+        [VM] * 4,
+    )(first_core, warped, mine, other)
     above, below = to_next(down), to_previous(up)
-    own_part = call(own_kernel, sds(ROWS, COLS), [VM] * 2, frames)(difference, own_second)
+    own_part, template = call(
+        own_and_template_kernel, (sds(ROWS, COLS), sds(ROWS, BLOCK)), [VM] * 3, frames
+    )(difference, own_second, coadd)
     thin_frames = [
         pltpu.VMEM((THIN, FRAME), F32),
         pltpu.VMEM((256, FRAME), BF16),
         pltpu.VMEM((THIN, COLS), F32),
         pltpu.SemaphoreType.DMA((4,)),
     ]
-    begun, template = call(
-        above_kernel,
-        (sds(ROWS, COLS), sds(ROWS, BLOCK)),
-        [VM] * 4,
-        thin_frames,
-        (ANY, VM),
-    )(own_part, above, coadd, above_second)
+    begun = call(above_kernel, sds(ROWS, COLS), [VM] * 3, thin_frames, ANY)(
+        own_part, above, above_second
+    )
     cleaned = call(
         below_kernel, sds(ROWS, COLS), [VM] * 3 + [ANY], thin_frames, ANY, {3: 0}
     )(own_part, below, below_second, begun)

time: 70.2 us -> 68.8 us (0.980)
  Pallas kernels: 15.2 us -> 14.2 us
    pallas_call x4, Pallas kernels: 9.15 us -> 8.13 us  [the longest x1 4.17 us: on_device(): call(warp_kernel, (sds(ROWS, COLS), sds(2, 8, 2 * ROWS, BLOCK)), [ANY, AN...]
where the time goes in v3:
time: 68.8 us; the launch traced here: 68.4 us
  blocking collectives  22.4 us (33%)
  starting transfers between devices  19.6 us (28%)
  Pallas kernels  14.2 us (21%)
  waiting for transfers between devices  5.37 us (8%)
  local copies, waits for them, and re-layouts  3.93 us (6%)
  between operations  2.28 us (3%)
    all_to_all x2, blocking collectives, over_chips(): lax.all_to_all(blocks, 'visit', split_axis=0, concat_axis=0, axis_index_g...  22.4 us
    ppermute x2, starting transfers between devices, to_previous(): return lax.ppermute(values, 'row', [((i + 1) % 16, i) for i in range(16)])  10.9 us
    ppermute x2, starting transfers between devices, swap(): return lax.ppermute(values, 'visit', [(i, i ^ step) for i in range(16)])  4.45 us
    ppermute x2, starting transfers between devices, to_next(): return lax.ppermute(values, 'row', [(i, (i + 1) % 16) for i in range(16)])  4.24 us
    pallas_call x1, Pallas kernels, on_device(): call(warp_kernel, (sds(ROWS, COLS), sds(2, 8, 2 * ROWS, BLOCK)), [ANY, AN...  4.17 us
    unnamed x21, local copies, waits for them, and re-layouts  3.63 us
    ppermute x2, waiting for transfers between devices, swap(): return lax.ppermute(values, 'visit', [(i, i ^ step) for i in range(16)])  2.7 us
    pallas_call x1, Pallas kernels, on_device(): call(bands_kernel, (bands, bands, bands, thin_bands, thin_bands), [SM] +...  2.65 us
  transfers between devices with their start and end apart: 6, of which 4 were waited for; matrix products, arithmetic and copies ran while one was open for 1% of the time, Pallas kernels for 12%

profile of v3, /device:TPU:1, one launch (start us, length us, event | category | flops | bytes accessed | tf_op | source)
XLA Modules:
  0.0 68.4 jit_solution(14929267130466729700)
XLA Ops:
  0.6 0.0 copy-start
  0.6 0.0 copy-start.1
  0.7 1.1 %copy-done.1 = f32[1,32,4096]{2,1,0:T(8,128)S(1)} copy-done((f32[1,32,4096]{2,1,0:T(8,128)S(1)}, f32[1,32,4096]{2,1,0:T(8,128)}, u32[]{:S(2)}) %copy-start.1) | copy-done | bytes 524312
  1.8 0.0 copy-start.2
  1.8 3.7 %collective-permute-start = (f32[72,1024]{1,0:T(8,128)S(1)}, f32[72,1024]{1,0:T(8,128)S(1)}, u32[]{:S(2)}, u32[]{:S(2)}) collective-permute-start(f32[72,1024]{1,0:T(8,128)S(1)} %shard_map.124), channel_id=1, source_target_pairs={{0,1},{1,2},{2,3},{3,4},{4,5},{5,6},{6,7},{7,8},{8,9},{9,10},{10,1... | collective-permute-start | bytes 884744 | tf_op jit(solution)/shard_map/ppermute | solution.py:386
  5.4 5.4 %collective-permute-start.1 = (f32[72,1024]{1,0:T(8,128)S(1)}, f32[72,1024]{1,0:T(8,128)S(1)}, u32[]{:S(2)}, u32[]{:S(2)}) collective-permute-start(f32[72,1024]{1,0:T(8,128)S(1)} %shard_map.125), channel_id=1, source_target_pairs={{1,0},{2,1},{3,2},{4,3},{5,4},{6,5},{7,6},{8,7},{9,8},{10,9},{11,1... | collective-permute-start | bytes 884744 | tf_op jit(solution)/shard_map/ppermute | solution.py:390
  11.5 0.0 copy-start.9
  11.5 0.6 copy-done.9
  12.2 0.0 copy-done
  12.2 0.6 copy-done.8
  12.8 0.2 fusion
  13.0 0.0 copy-start.6
  13.0 0.1 copy.17
  13.1 0.6 copy-done.6
  13.7 0.1 copy.15
  13.8 0.1 pad.7.k1_ref
  13.9 0.1 pad.8.k2_ref
  14.0 0.1 pad_add_fusion.place_ref.place_source_ref
  14.0 0.1 broadcast_subtract_fusion
  14.1 0.5 copy-done.7
  14.7 0.1 select_reduce_fusion.mix_ref
  14.8 2.6 %shard_map.122 = (bf16[192,512]{1,0:T(8,128)(2,1)S(1)}, bf16[192,512]{1,0:T(8,128)(2,1)S(1)}, bf16[192,512]{1,0:T(8,128)(2,1)S(1)}, bf16[80,256]{1,0:T(8,128)(2,1)S(1)}, bf16[80,256]{1,0:T(8,128)(2,1)S(1)}) custom-call(s32[3]{0:T(128)S(1)} %pad_add_fusion.place_ref.place_source_ref, f32[24,128]{1,0:T(8,128)S(1)} %pad.7.k1_ref, f32[24,128]{1,0:T(8,128)S(1)} %pad.8.k2_ref, ...), custom_call_target="tpu_custom_call" | custom-call | tf_op jit(solution)/shard_map/pallas_call | solution.py:426
  17.4 0.0 copy-done.2
  17.4 0.0 copy-start.3
  17.4 0.0 copy-start.4
  17.5 0.0 copy-start.5
  17.5 1.8 %shard_map.123.own_ref = f32[32,4096]{1,0:T(8,128)S(1)} custom-call(f32[32,4096]{1,0:T(8,128)S(1)} %bitcast.26, bf16[192,512]{1,0:T(8,128)(2,1)S(1)} %get-tuple-element.14.band_ref), custom_call_target="tpu_custom_call" | custom-call | tf_op jit(solution)/shard_map/pallas_call | solution.py:434
  19.9 0.0 collective-permute-done.above_ref
  19.9 1.0 %collective-permute-done.1.below_ref = f32[72,1024]{1,0:T(8,128)S(1)} collective-permute-done((f32[72,1024]{1,0:T(8,128)S(1)}, f32[72,1024]{1,0:T(8,128)S(1)}, u32[]{:S(2)}, u32[]{:S(2)}) %collective-permute-start.1) | collective-permute-done | bytes 294944 | tf_op jit(solution)/shard_map/ppermute | solution.py:390
  20.9 0.0 copy-done.3
  20.9 0.0 copy-done.4
  20.9 0.0 copy-done.5
  20.9 4.2 %shard_map.126 = (f32[32,4096]{1,0:T(8,128)S(1)}, f32[2,8,64,256]{3,2,1,0:T(8,128)S(1)}) custom-call(s32[3]{0:T(128)S(1)} %pad_add_fusion.place_ref.place_source_ref, f32[1]{0:T(128)S(6)} %copy.22.weight_source_ref, f32[32,4096]{1,0:T(8,128)S(1)} %shard_map.123.own_ref, f32[72,1024]{1,0:T(8,128)S(1)} %collective-permute-done.above_ref, ...), custom_call_target="tpu_custom_call" | custom-call | tf_op jit(solution)/shard_map/pallas_call | solution.py:435
  25.1 2.0 %collective-permute-start.2 = (f32[8,64,256]{2,1,0:T(8,128)S(1)}, f32[8,64,256]{2,1,0:T(8,128)S(1)}, u32[]{:S(2)}, u32[]{:S(2)}) collective-permute-start(f32[8,64,256]{2,1,0:T(8,128)S(1)} %slice_bitcast_fusion), channel_id=1, source_target_pairs={{0,16},{16,0},{32,48},{48,32},{64,80},{80,64},{96,112},{112,96},{1... | collective-permute-start | bytes 1572872 | tf_op jit(solution)/shard_map/ppermute | solution.py:371
  27.1 1.5 %collective-permute-done.2 = f32[8,64,256]{2,1,0:T(8,128)S(1)} collective-permute-done((f32[8,64,256]{2,1,0:T(8,128)S(1)}, f32[8,64,256]{2,1,0:T(8,128)S(1)}, u32[]{:S(2)}, u32[]{:S(2)}) %collective-permute-start.2) | collective-permute-done | bytes 524320 | tf_op jit(solution)/shard_map/ppermute | solution.py:371
  28.6 0.1 bitcast_add_fusion
  28.7 13.2 %all_to_all.10 = f32[8,64,256]{2,1,0:T(8,128)S(1)} all-to-all(f32[8,64,256]{2,1,0:T(8,128)S(1)} %bitcast_add_fusion), channel_id=1, replica_groups={{0,32,64,96,128,160,192,224},{16,48,80,112,144,176,208,240},{1,33,65,97..., dimensions={0} | all-to-all | bytes 1048576 | tf_op jit(solution)/shard_map/all_to_all | solution.py:375
  42.0 9.1 %all_to_all.11.mine_ref = f32[8,32,256]{2,1,0:T(8,128)S(1)} all-to-all(f32[8,32,256]{2,1,0:T(8,128)S(1)} %broadcast_in_dim.35), channel_id=1, replica_groups={{0,32,64,96,128,160,192,224},{16,48,80,112,144,176,208,240},{1,33,65,97..., dimensions={0} | all-to-all | bytes 524288 | tf_op jit(solution)/shard_map/all_to_all | solution.py:375
  51.2 2.5 %collective-permute-start.3 = (f32[8,32,256]{2,1,0:T(8,128)S(1)}, f32[8,32,256]{2,1,0:T(8,128)S(1)}, u32[]{:S(2)}, u32[]{:S(2)}) collective-permute-start(f32[8,32,256]{2,1,0:T(8,128)S(1)} %all_to_all.11.mine_ref), channel_id=1, source_target_pairs={{0,16},{16,0},{32,48},{48,32},{64,80},{80,64},{96,112},{112,96},{1... | collective-permute-start | bytes 786440 | tf_op jit(solution)/shard_map/ppermute | solution.py:371
  53.7 1.2 %collective-permute-done.3.other_ref = f32[8,32,256]{2,1,0:T(8,128)S(1)} collective-permute-done((f32[8,32,256]{2,1,0:T(8,128)S(1)}, f32[8,32,256]{2,1,0:T(8,128)S(1)}, u32[]{:S(2)}, u32[]{:S(2)}) %collective-permute-start.3) | collective-permute-done | bytes 262176 | tf_op jit(solution)/shard_map/ppermute | solution.py:371
  54.8 0.1 shard_map.127
  54.9 0.6 collective-permute-start.5
  55.5 5.6 %collective-permute-start.4 = (f32[40,1024]{1,0:T(8,128)S(1)}, f32[40,1024]{1,0:T(8,128)S(1)}, u32[]{:S(2)}, u32[]{:S(2)}) collective-permute-start(f32[40,1024]{1,0:T(8,128)S(1)} %get-tuple-element.21), channel_id=1, source_target_pairs={{1,0},{2,1},{3,2},{4,3},{5,4},{6,5},{7,6},{8,7},{9,8},{10,9},{11,1... | collective-permute-start | bytes 491528 | tf_op jit(solution)/shard_map/ppermute | solution.py:390
  61.1 2.3 %shard_map.128 = (f32[32,4096]{1,0:T(8,128)S(1)}, f32[32,256]{1,0:T(8,128)}) custom-call(f32[32,4096]{1,0:T(8,128)S(1)} %get-tuple-element.18.own_ref, bf16[192,512]{1,0:T(8,128)(2,1)S(1)} %get-tuple-element.19.band_ref, f32[32,256]{1,0:T(8,128)S(1)} %fusion.3.coadd_ref), custom_call_target="tpu_custom_call" | custom-call | tf_op jit(solution)/shard_map/pallas_call | solution.py:468
  63.4 1.7 %collective-permute-done.5.above_ref = f32[40,1024]{1,0:T(8,128)S(1)} collective-permute-done((f32[40,1024]{1,0:T(8,128)S(1)}, f32[40,1024]{1,0:T(8,128)S(1)}, u32[]{:S(2)}, u32[]{:S(2)}) %collective-permute-start.5) | collective-permute-done | bytes 163872 | tf_op jit(solution)/shard_map/ppermute | solution.py:386
  65.1 1.5 %shard_map.129.begun_ref = f32[32,4096]{1,0:T(8,128)} custom-call(f32[32,4096]{1,0:T(8,128)S(1)} %get-tuple-element.20.own_ref, f32[40,1024]{1,0:T(8,128)S(1)} %collective-permute-done.5.above_ref, bf16[80,256]{1,0:T(8,128)(2,1)S(1)} %get-tuple-element.24.band_ref), custom_call_target="tpu_custom_call" | custom-call | tf_op jit(solution)/shard_map/pallas_call | solution.py:477
  66.7 0.0 collective-permute-done.4.below_ref
  66.7 1.5 %shard_map.130 = f32[32,4096]{1,0:T(8,128)} custom-call(f32[32,4096]{1,0:T(8,128)S(1)} %get-tuple-element.20.own_ref, f32[40,1024]{1,0:T(8,128)S(1)} %collective-permute-done.4.below_ref, bf16[80,256]{1,0:T(8,128)(2,1)S(1)} %get-tuple-element.22.band_ref, f32[32,4096]{1,0:T(8,128)} %shard_map.129.begun_ref), custom_call_target="tpu_custom_call", output_to_operand_aliasing={{}: (3, {})} | custom-call | tf_op jit(solution)/shard_map/pallas_call | solution.py:480
  (12 shorter events, 0.2 us)
Async XLA Ops:
  0.6 11.5 %copy-start = (f32[9,21,21]{2,1,0:T(8,128)S(1)}, f32[9,21,21]{2,1,0:T(8,128)}, u32[]{:S(2)}) copy-start(f32[9,21,21]{2,1,0:T(8,128)} %param.12) | copy-start | bytes 47632
  0.6 1.1 %copy-start.1 = (f32[1,32,4096]{2,1,0:T(8,128)S(1)}, f32[1,32,4096]{2,1,0:T(8,128)}, u32[]{:S(2)}) copy-start(f32[1,32,4096]{2,1,0:T(8,128)} %param.11) | copy-start | bytes 1572868
  1.8 15.7 %copy-start.2 = (f32[1,32,4096]{2,1,0:T(8,128)S(1)}, f32[1,32,4096]{2,1,0:T(8,128)}, u32[]{:S(2)}) copy-start(f32[1,32,4096]{2,1,0:T(8,128)} %param.11) | copy-start | bytes 1572868
  1.8 18.2 %collective-permute-start = (f32[72,1024]{1,0:T(8,128)S(1)}, f32[72,1024]{1,0:T(8,128)S(1)}, u32[]{:S(2)}, u32[]{:S(2)}) collective-permute-start(f32[72,1024]{1,0:T(8,128)S(1)} %shard_map.124), channel_id=1, source_target_pairs={{0,1},{1,2},{2,3},{3,4},{4,5},{5,6},{6,7},{7,8},{8,9},{9,10},{10,1... | collective-permute-start | bytes 884744 | tf_op jit(solution)/shard_map/ppermute | solution.py:386
  5.4 15.5 %collective-permute-start.1 = (f32[72,1024]{1,0:T(8,128)S(1)}, f32[72,1024]{1,0:T(8,128)S(1)}, u32[]{:S(2)}, u32[]{:S(2)}) collective-permute-start(f32[72,1024]{1,0:T(8,128)S(1)} %shard_map.125), channel_id=1, source_target_pairs={{1,0},{2,1},{3,2},{4,3},{5,4},{6,5},{7,6},{8,7},{9,8},{10,9},{11,1... | collective-permute-start | bytes 884744 | tf_op jit(solution)/shard_map/ppermute | solution.py:390
  11.5 0.7 copy-start.9
  12.1 0.7 copy-start.8
  13.0 0.7 %copy-start.6 = (f32[1,21,21]{2,0,1:T(1,128)S(1)}, f32[1,21,21]{2,0,1:T(1,128)}, u32[]{:S(2)}) copy-start(f32[1,21,21]{2,0,1:T(1,128)} %param.21) | copy-start | bytes 5296
  14.0 0.7 %copy-start.7 = (f32[1,8,32]{2,1,0:T(8,128)S(1)}, f32[1,8,32]{2,1,0:T(8,128)}, u32[]{:S(2)}) copy-start(f32[1,8,32]{2,1,0:T(8,128)} %param.15) | copy-start | bytes 3076
  17.4 3.5 %copy-start.3 = (s32[1,32,4096]{2,1,0:T(8,128)S(1)}, s32[1,32,4096]{2,1,0:T(8,128)}, u32[]{:S(2)}) copy-start(s32[1,32,4096]{2,1,0:T(8,128)} %param.20) | copy-start | bytes 1572868
  17.4 3.5 %copy-start.4 = (f32[1,8,4096]{2,1,0:T(8,128)S(1)}, f32[1,8,4096]{2,1,0:T(8,128)}, u32[]{:S(2)}) copy-start(f32[1,8,4096]{2,1,0:T(8,128)} %param.18) | copy-start | bytes 393220
  17.5 3.5 %copy-start.5 = (s32[1,4096]{1,0:T(1,128)S(1)}, s32[1,4096]{1,0:T(1,128)}, u32[]{:S(2)}) copy-start(s32[1,4096]{1,0:T(1,128)} %starts_ref.1) | copy-start | bytes 49156
  25.1 3.5 %collective-permute-start.2 = (f32[8,64,256]{2,1,0:T(8,128)S(1)}, f32[8,64,256]{2,1,0:T(8,128)S(1)}, u32[]{:S(2)}, u32[]{:S(2)}) collective-permute-start(f32[8,64,256]{2,1,0:T(8,128)S(1)} %slice_bitcast_fusion), channel_id=1, source_target_pairs={{0,16},{16,0},{32,48},{48,32},{64,80},{80,64},{96,112},{112,96},{1... | collective-permute-start | bytes 1572872 | tf_op jit(solution)/shard_map/ppermute | solution.py:371
  51.2 3.7 %collective-permute-start.3 = (f32[8,32,256]{2,1,0:T(8,128)S(1)}, f32[8,32,256]{2,1,0:T(8,128)S(1)}, u32[]{:S(2)}, u32[]{:S(2)}) collective-permute-start(f32[8,32,256]{2,1,0:T(8,128)S(1)} %all_to_all.11.mine_ref), channel_id=1, source_target_pairs={{0,16},{16,0},{32,48},{48,32},{64,80},{80,64},{96,112},{112,96},{1... | collective-permute-start | bytes 786440 | tf_op jit(solution)/shard_map/ppermute | solution.py:371
  54.9 10.2 %collective-permute-start.5 = (f32[40,1024]{1,0:T(8,128)S(1)}, f32[40,1024]{1,0:T(8,128)S(1)}, u32[]{:S(2)}, u32[]{:S(2)}) collective-permute-start(f32[40,1024]{1,0:T(8,128)S(1)} %get-tuple-element.23), channel_id=1, source_target_pairs={{0,1},{1,2},{2,3},{3,4},{4,5},{5,6},{6,7},{7,8},{8,9},{9,10},{10,1... | collective-permute-start | bytes 491528 | tf_op jit(solution)/shard_map/ppermute | solution.py:386
  55.5 11.1 %collective-permute-start.4 = (f32[40,1024]{1,0:T(8,128)S(1)}, f32[40,1024]{1,0:T(8,128)S(1)}, u32[]{:S(2)}, u32[]{:S(2)}) collective-permute-start(f32[40,1024]{1,0:T(8,128)S(1)} %get-tuple-element.21), channel_id=1, source_target_pairs={{1,0},{2,1},{3,2},{4,3},{5,4},{6,5},{7,6},{8,7},{9,8},{10,9},{11,1... | collective-permute-start | bytes 491528 | tf_op jit(solution)/shard_map/ppermute | solution.py:390

commit v4 on v3

--- a/solution.py
+++ b/solution.py
@@ -115,21 +115,22 @@
     return pltpu.roll(values, shift, 1, stride=1, stride_axis=0)
 
 
-def bands_kernel(
-    place_ref, k1_ref, k2_ref, mix_ref, own1_ref, edge1_ref, own2_ref, above2_ref, below2_ref
-):
+def first_bands_kernel(place_ref, lags_ref, mix_ref, own_ref, edge_ref):
     has_above, has_below = place_ref[2] > 0, place_ref[2] < 15
-    first = jnp.concatenate([skewed(k1_ref, lag, 48, 0) for lag in range(24)], axis=1)
+    values = jnp.concatenate([skewed(lags_ref, lag, 48, 0) for lag in range(24)], axis=1)
     merged = jnp.dot(
-        mix_ref[...], first, precision=lax.Precision.HIGHEST, preferred_element_type=F32
+        mix_ref[...], values, precision=lax.Precision.HIGHEST, preferred_element_type=F32
     )
     slots = [merged[:, SLOT * lag : SLOT * (lag + 1)] for lag in range(24)]
-    put_both(own1_ref, edge1_ref, jnp.concatenate(slots, axis=0), has_above, has_below)
-    slots = [skewed(k2_ref, lag, ROWS, 8) for lag in range(24)]
+    put_both(own_ref, edge_ref, jnp.concatenate(slots, axis=0), has_above, has_below)
+
+
+def second_bands_kernel(place_ref, lags_ref, own_ref, above_ref, below_ref):
+    slots = [skewed(lags_ref, lag, ROWS, 8) for lag in range(24)]
     values = jnp.concatenate(slots, axis=0)
-    put_bands(own2_ref, between(values, BASE, BASE + ROWS, -BASE))
-    put_thin_bands(above2_ref, values, BASE - THIN, 0, has_above)
-    put_thin_bands(below2_ref, values, BASE + ROWS, ROWS - THIN, has_below)
+    put_bands(own_ref, between(values, BASE, BASE + ROWS, -BASE))
+    put_thin_bands(above_ref, values, BASE - THIN, 0, place_ref[2] > 0)
+    put_thin_bands(below_ref, values, BASE + ROWS, ROWS - THIN, place_ref[2] < 15)
 
 
 def coverage(starts, offset, q):
@@ -138,10 +139,20 @@
     return ((actual >= 0) & (actual <= COLS - TAPS)).astype(F32)
 
 
-def put_blocks(ref, values, row, place_ref, q):
-    for j in range(4):
-        at = (j % 2) ^ place_ref[1], 2 * q + j // 2, pl.ds(row, ROWS)
-        ref[at] = values[:, j * BLOCK : (j + 1) * BLOCK]
+def put_blocks(kept_ref, sent_ref, values, core, q):
+    blocks = [values[:, j * BLOCK : (j + 1) * BLOCK] for j in range(4)]
+    for j in range(2):
+        even, odd = blocks[2 * j : 2 * j + 2]
+        kept_ref[2 * q + j] = jnp.where(core == 0, even, odd)
+        sent_ref[2 * q + j] = jnp.where(core == 0, odd, even)
+
+
+def share_kernel(place_ref, weight_ref, mask_ref, starts_ref, kept_ref, sent_ref):
+    for q in range(4):
+        cols = pl.ds(q * CHUNK, CHUNK)
+        covered = coverage(starts_ref[:, cols], place_ref[0], q)
+        share = weight_ref[0] * mask_ref[:, cols].astype(F32) * covered
+        put_blocks(kept_ref, sent_ref, share, place_ref[1], q)
 
 
 def clear(frame_ref, row):
@@ -211,7 +222,8 @@
     taps_ref,
     mask_ref,
     warped_ref,
-    weighted_ref,
+    kept_ref,
+    sent_ref,
     frame_ref,
     halves_ref,
     source_ref,
@@ -252,6 +264,7 @@
         cols = pl.ds(q * CHUNK, CHUNK)
         at = pl.multiple_of((aligned + q * (CHUNK // 128)) * 128, 128)
         moved = pltpu.roll(source_ref[:, pl.ds(at, width)], width - rest, 1)
+        moved = moved[:, : CHUNK + 128]
         starts = starts_ref[:, cols]
         early = starts == -3
         taps = [taps_ref[t : t + 1, cols] for t in range(TAPS)]
@@ -261,13 +274,12 @@
             tap = jnp.where(
                 early, taps[lag] if lag < TAPS else zero, taps[lag - 1] if lag else zero
             )
-            part = moved if lag == 0 else pltpu.roll(moved, width - lag, 1)
+            part = moved if lag == 0 else pltpu.roll(moved, CHUNK + 128 - lag, 1)
             term = tap * part[:, :CHUNK]
             total = term if total is None else total + term
         warped_ref[:, cols] = total
         share = weight_ref[0] * mask_ref[:, cols].astype(F32) * coverage(starts, offset, q)
-        put_blocks(weighted_ref, share * total, 0, place_ref, q)
-        put_blocks(weighted_ref, share, ROWS, place_ref, q)
+        put_blocks(kept_ref, sent_ref, share * total, place_ref[1], q)
 
 
 def differ_kernel(
@@ -423,18 +435,24 @@
     mix = jnp.sum(jnp.where(hits & inside[None], row_taps[0][:, :, None], 0.0), axis=0)
     bands = sds(STEPS * ROWS, GROUP * SLOT, dtype=BF16)
     thin_bands = sds(THIN_STEPS * THIN, 256, dtype=BF16)
-    own_first, edge_first, own_second, above_second, below_second = call(
-        bands_kernel, (bands, bands, bands, thin_bands, thin_bands), [SM] + [VM] * 3
-    )(place, by_lag(kernel), by_lag(decorrelation[0]), mix)
+    own_first, edge_first = call(first_bands_kernel, (bands, bands), [SM] + [VM] * 2)(
+        place, by_lag(kernel), mix
+    )
 
     frames = [
         pltpu.VMEM((SPAN, FRAME), F32),
         pltpu.VMEM((GROUP * SLOT, FRAME), BF16),
     ]
     own_part = call(own_kernel, sds(ROWS, COLS), [VM] * 2, frames)(pixels, own_first)
-    warped, weighted = call(
+    blocks = sds(8, ROWS, BLOCK)
+    kept, sent = call(share_kernel, (blocks, blocks), [SM, SM, VM, VM])(
+        place, visit_weights, clip_masks[0], col_starts
+    )
+    shares = kept + swap(sent, 1)
+    denominator = jnp.maximum(jnp.sum(over_chips(shares), axis=0), 1.0)
+    warped, kept, sent = call(
         warp_kernel,
-        (sds(ROWS, COLS), sds(2, 8, 2 * ROWS, BLOCK)),
+        (sds(ROWS, COLS), blocks, blocks),
         [ANY, ANY] + [VM] * 7,
         frames
         + [
@@ -454,9 +472,14 @@
         col_taps[0],
         clip_masks[0],
     )
-    half = weighted[0] + swap(weighted[1], 1)
-    total = jnp.sum(over_chips(half), axis=0)
-    coadd = total[:ROWS] / jnp.maximum(total[ROWS:], 1.0)
+    sent, denominator = lax.optimization_barrier((sent, denominator))
+    second_lags, kept = lax.optimization_barrier((by_lag(decorrelation[0]), kept))
+    own_second, above_second, below_second = call(
+        second_bands_kernel, (bands, thin_bands, thin_bands), [SM, VM]
+    )(place, second_lags)
+    half = kept + swap(sent, 1)
+    half, own_second = lax.optimization_barrier((half, own_second))
+    coadd = jnp.sum(over_chips(half), axis=0) / denominator
     mine = over_chips(jnp.broadcast_to(coadd[None], (8, ROWS, BLOCK)))
     other = swap(mine, 1)
     difference, up, down = call(

time: 68.8 us -> 68.2 us (level)
  starting transfers between devices: 19.6 us -> 23.6 us
  local copies, waits for them, and re-layouts: 3.93 us -> 1.48 us
  blocking collectives: 22.4 us -> 20.1 us
  waiting for transfers between devices: 5.37 us -> 3.47 us
  Pallas kernels: 14.2 us -> 15.4 us
  other arithmetic: 0.4 us -> 1.1 us
    all_to_all x0 -> x1, starting transfers between devices: none -> 4.35 us  [over_chips(): lax.all_to_all(blocks, 'visit', split_axis=0, concat_axis=0, axis_index_g...]
    unnamed x21, local copies, waits for them, and re-layouts: 3.63 us -> 1.21 us
    all_to_all x2, blocking collectives: 22.4 us -> 20.1 us  [over_chips(): lax.all_to_all(blocks, 'visit', split_axis=0, concat_axis=0, axis_index_g...]
    pallas_call x2 -> x4, Pallas kernels: 6.81 us -> 8.07 us  [the longest x1 4.17 us: on_device(): call(warp_kernel, (sds(ROWS, COLS), blocks, blocks), [ANY, ANY] + [VM] *...]
    ppermute x2, waiting for transfers between devices: 0.97 us -> 0.01 us  [to_previous(): return lax.ppermute(values, 'row', [((i + 1) % 16, i) for i in range(16)])]
    ppermute x2 -> x3, waiting for transfers between devices: 2.7 us -> 1.83 us  [swap(): return lax.ppermute(values, 'visit', [(i, i ^ step) for i in range(16)])]
    ppermute x2 -> x3, starting transfers between devices: 4.45 us -> 4.92 us  [swap(): return lax.ppermute(values, 'visit', [(i, i ^ step) for i in range(16)])]
  transfers between devices with their start and end apart: 6 -> 8, of which waited for: 4 -> 3; matrix products, arithmetic and copies ran while one was open for 1% -> 2% of each run, Pallas kernels for 12% -> 20%
where the time goes in v4:
time: 68.2 us; the launch traced here: 67.8 us
  starting transfers between devices  23.6 us (35%)
  blocking collectives  20.1 us (29%)
  Pallas kernels  15.4 us (23%)
  waiting for transfers between devices  3.47 us (5%)
  between operations  2.37 us (3%)
  local copies, waits for them, and re-layouts  1.48 us (2%)
  other arithmetic  1.1 us (2%)
    all_to_all x2, blocking collectives, over_chips(): lax.all_to_all(blocks, 'visit', split_axis=0, concat_axis=0, axis_index_g...  20.1 us
    ppermute x2, starting transfers between devices, to_previous(): return lax.ppermute(values, 'row', [((i + 1) % 16, i) for i in range(16)])  10.5 us
    ppermute x3, starting transfers between devices, swap(): return lax.ppermute(values, 'visit', [(i, i ^ step) for i in range(16)])  4.92 us
    all_to_all x1, starting transfers between devices, over_chips(): lax.all_to_all(blocks, 'visit', split_axis=0, concat_axis=0, axis_index_g...  4.35 us
    pallas_call x1, Pallas kernels, on_device(): call(warp_kernel, (sds(ROWS, COLS), blocks, blocks), [ANY, ANY] + [VM] *...  4.17 us
    ppermute x2, starting transfers between devices, to_next(): return lax.ppermute(values, 'row', [(i, (i + 1) % 16) for i in range(16)])  3.91 us
    pallas_call x1, Pallas kernels, on_device(): call(own_and_template_kernel, (sds(ROWS, COLS), sds(ROWS, BLOCK)), [VM] *...  2.37 us
    ppermute x3, waiting for transfers between devices, swap(): return lax.ppermute(values, 'visit', [(i, i ^ step) for i in range(16)])  1.83 us
  transfers between devices with their start and end apart: 8, of which 3 were waited for; matrix products, arithmetic and copies ran while one was open for 2% of the time, Pallas kernels for 20%

profile of v4, /device:TPU:1, one launch (start us, length us, event | category | flops | bytes accessed | tf_op | source)
XLA Modules:
  0.0 67.8 jit_solution(2454717341607699909)
XLA Ops:
  0.6 0.0 copy-start
  0.6 0.0 copy-start.1
  0.7 1.1 %copy-done.1 = f32[1,32,4096]{2,1,0:T(8,128)S(1)} copy-done((f32[1,32,4096]{2,1,0:T(8,128)S(1)}, f32[1,32,4096]{2,1,0:T(8,128)}, u32[]{:S(2)}) %copy-start.1) | copy-done | bytes 524312
  1.8 0.0 copy-start.3
  1.8 3.7 %collective-permute-start = (f32[72,1024]{1,0:T(8,128)S(1)}, f32[72,1024]{1,0:T(8,128)S(1)}, u32[]{:S(2)}, u32[]{:S(2)}) collective-permute-start(f32[72,1024]{1,0:T(8,128)S(1)} %shard_map.124), channel_id=1, source_target_pairs={{0,1},{1,2},{2,3},{3,4},{4,5},{5,6},{6,7},{7,8},{8,9},{9,10},{10,1... | collective-permute-start | bytes 884744 | tf_op jit(solution)/shard_map/ppermute | solution.py:398
  5.4 5.4 %collective-permute-start.1 = (f32[72,1024]{1,0:T(8,128)S(1)}, f32[72,1024]{1,0:T(8,128)S(1)}, u32[]{:S(2)}, u32[]{:S(2)}) collective-permute-start(f32[72,1024]{1,0:T(8,128)S(1)} %shard_map.125), channel_id=1, source_target_pairs={{1,0},{2,1},{3,2},{4,3},{5,4},{6,5},{7,6},{8,7},{9,8},{10,9},{11,1... | collective-permute-start | bytes 884744 | tf_op jit(solution)/shard_map/ppermute | solution.py:402
  12.1 0.1 pad_add_fusion.place_ref.place_source_ref
  12.2 0.0 copy-done.3
  12.2 0.6 shard_map.127
  12.9 0.0 copy-start.9
  12.9 0.0 copy-start.8
  12.9 1.0 %collective-permute-start.2 = (f32[8,32,256]{2,1,0:T(8,128)S(1)}, f32[8,32,256]{2,1,0:T(8,128)S(1)}, u32[]{:S(2)}, u32[]{:S(2)}) collective-permute-start(f32[8,32,256]{2,1,0:T(8,128)S(1)} %get-tuple-element.30), channel_id=1, source_target_pairs={{0,16},{16,0},{32,48},{48,32},{64,80},{80,64},{96,112},{112,96},{1... | collective-permute-start | bytes 786440 | tf_op jit(solution)/shard_map/ppermute | solution.py:383
  14.0 0.0 copy-done
  14.0 0.0 copy-done.8
  14.0 0.2 fusion
  14.2 0.1 broadcast_subtract_fusion
  14.3 0.1 copy.17
  14.4 0.1 pad.7.lags_ref
  14.4 0.7 collective-permute-done.2
  15.1 0.7 %add.51 = f32[8,32,256]{2,1,0:T(8,128)} add(f32[8,32,256]{2,1,0:T(8,128)S(1)} %get-tuple-element.29, f32[8,32,256]{2,1,0:T(8,128)S(1)} %collective-permute-done.2) | non-fusion elementwise | flops 65536 | bytes 786432 | tf_op jit(solution)/shard_map/add | solution.py:451
  15.9 4.4 %all-to-all-start = ((f32[8,32,256]{2,1,0:T(8,128)}), f32[8,32,256]{2,1,0:T(8,128)S(1)}, u32[]{:S(2)}, u32[]{:S(2)}) async-start(f32[8,32,256]{2,1,0:T(8,128)} %add.51), calls=%async_computation | async-start | bytes 524288 | tf_op jit(solution)/shard_map/all_to_all | solution.py:387
  20.2 0.1 select_reduce_fusion.mix_ref
  20.3 1.7 %shard_map.122 = (bf16[192,512]{1,0:T(8,128)(2,1)S(1)}, bf16[192,512]{1,0:T(8,128)(2,1)S(1)}) custom-call(s32[3]{0:T(128)S(1)} %pad_add_fusion.place_ref.place_source_ref, f32[24,128]{1,0:T(8,128)S(1)} %pad.7.lags_ref, f32[32,48]{1,0:T(8,128)S(1)} %select_reduce_fusion.mix_ref), custom_call_target="tpu_custom_call" | custom-call | tf_op jit(solution)/shard_map/pallas_call | solution.py:438
  22.1 0.0 copy-start.4
  22.1 1.8 %shard_map.123.own_ref = f32[32,4096]{1,0:T(8,128)S(1)} custom-call(f32[32,4096]{1,0:T(8,128)S(1)} %bitcast.22, bf16[192,512]{1,0:T(8,128)(2,1)S(1)} %get-tuple-element.23.band_ref), custom_call_target="tpu_custom_call" | custom-call | tf_op jit(solution)/shard_map/pallas_call | solution.py:446
  23.9 0.0 collective-permute-done.above_ref
  23.9 0.0 collective-permute-done.1.below_ref
  23.9 4.2 %shard_map.126 = (f32[32,4096]{1,0:T(8,128)S(1)}, f32[8,32,256]{2,1,0:T(8,128)S(1)}, f32[8,32,256]{2,1,0:T(8,128)S(1)}) custom-call(s32[3]{0:T(128)S(1)} %pad_add_fusion.place_ref.place_source_ref, f32[1]{0:T(128)S(6)} %copy.22.weight_source_ref.weight_ref, f32[32,4096]{1,0:T(8,128)S(1)} %shard_map.123.own_ref, ...), custom_call_target="tpu_custom_call" | custom-call | tf_op jit(solution)/shard_map/pallas_call | solution.py:453
  28.1 0.0 all-to-all-done
  28.1 0.0 copy-start.6
  28.2 0.7 %collective-permute-start.3 = (f32[8,32,256]{2,1,0:T(8,128)S(1)}, f32[8,32,256]{2,1,0:T(8,128)S(1)}, u32[]{:S(2)}, u32[]{:S(2)}) collective-permute-start(f32[8,32,256]{2,1,0:T(8,128)S(1)} %get-tuple-element.31), channel_id=1, source_target_pairs={{0,16},{16,0},{32,48},{48,32},{64,80},{80,64},{96,112},{112,96},{1... | collective-permute-start | bytes 786440 | tf_op jit(solution)/shard_map/ppermute | solution.py:383
  28.9 0.0 copy-done.6
  28.9 0.1 copy.15
  29.0 0.1 pad.8.lags_ref
  29.1 1.5 %shard_map.128 = (bf16[192,512]{1,0:T(8,128)(2,1)S(1)}, bf16[80,256]{1,0:T(8,128)(2,1)S(1)}, bf16[80,256]{1,0:T(8,128)(2,1)S(1)}) custom-call(s32[3]{0:T(128)S(1)} %pad_add_fusion.place_ref.place_source_ref, f32[24,128]{1,0:T(8,128)S(1)} %pad.8.lags_ref), custom_call_target="tpu_custom_call" | custom-call | tf_op jit(solution)/shard_map/pallas_call | solution.py:477
  30.6 0.0 collective-permute-done.3
  30.7 11.4 %all_to_all.15 = f32[8,32,256]{2,1,0:T(8,128)S(1)} all-to-all(f32[8,32,256]{2,1,0:T(8,128)S(1)} %add.52), channel_id=1, replica_groups={{0,32,64,96,128,160,192,224},{16,48,80,112,144,176,208,240},{1,33,65,97..., dimensions={0} | all-to-all | bytes 524288 | tf_op jit(solution)/shard_map/all_to_all | solution.py:387
  42.1 8.7 %all_to_all.16.mine_ref = f32[8,32,256]{2,1,0:T(8,128)S(1)} all-to-all(f32[8,32,256]{2,1,0:T(8,128)S(1)} %broadcast_in_dim.35), channel_id=1, replica_groups={{0,32,64,96,128,160,192,224},{16,48,80,112,144,176,208,240},{1,33,65,97..., dimensions={0} | all-to-all | bytes 524288 | tf_op jit(solution)/shard_map/all_to_all | solution.py:387
  50.9 3.1 %collective-permute-start.4 = (f32[8,32,256]{2,1,0:T(8,128)S(1)}, f32[8,32,256]{2,1,0:T(8,128)S(1)}, u32[]{:S(2)}, u32[]{:S(2)}) collective-permute-start(f32[8,32,256]{2,1,0:T(8,128)S(1)} %all_to_all.16.mine_ref), channel_id=1, source_target_pairs={{0,16},{16,0},{32,48},{48,32},{64,80},{80,64},{96,112},{112,96},{1... | collective-permute-start | bytes 786440 | tf_op jit(solution)/shard_map/ppermute | solution.py:383
  54.0 1.2 %collective-permute-done.4.other_ref = f32[8,32,256]{2,1,0:T(8,128)S(1)} collective-permute-done((f32[8,32,256]{2,1,0:T(8,128)S(1)}, f32[8,32,256]{2,1,0:T(8,128)S(1)}, u32[]{:S(2)}, u32[]{:S(2)}) %collective-permute-start.4) | collective-permute-done | bytes 262176 | tf_op jit(solution)/shard_map/ppermute | solution.py:383
  55.2 0.1 shard_map.129
  55.3 0.3 collective-permute-start.6
  55.5 5.1 %collective-permute-start.5 = (f32[40,1024]{1,0:T(8,128)S(1)}, f32[40,1024]{1,0:T(8,128)S(1)}, u32[]{:S(2)}, u32[]{:S(2)}) collective-permute-start(f32[40,1024]{1,0:T(8,128)S(1)} %get-tuple-element.39), channel_id=1, source_target_pairs={{1,0},{2,1},{3,2},{4,3},{5,4},{6,5},{7,6},{8,7},{9,8},{10,9},{11,1... | collective-permute-start | bytes 491528 | tf_op jit(solution)/shard_map/ppermute | solution.py:402
  60.6 2.4 %shard_map.130 = (f32[32,4096]{1,0:T(8,128)S(1)}, f32[32,256]{1,0:T(8,128)}) custom-call(f32[32,4096]{1,0:T(8,128)S(1)} %get-tuple-element.36.own_ref, bf16[192,512]{1,0:T(8,128)(2,1)S(1)} %get-tuple-element.37.band_ref, f32[32,256]{1,0:T(8,128)S(1)} %div.3.coadd_ref), custom_call_target="tpu_custom_call" | custom-call | tf_op jit(solution)/shard_map/pallas_call | solution.py:491
  63.0 1.6 %collective-permute-done.6.above_ref = f32[40,1024]{1,0:T(8,128)S(1)} collective-permute-done((f32[40,1024]{1,0:T(8,128)S(1)}, f32[40,1024]{1,0:T(8,128)S(1)}, u32[]{:S(2)}, u32[]{:S(2)}) %collective-permute-start.6) | collective-permute-done | bytes 163872 | tf_op jit(solution)/shard_map/ppermute | solution.py:398
  64.6 1.5 %shard_map.131.begun_ref = f32[32,4096]{1,0:T(8,128)} custom-call(f32[32,4096]{1,0:T(8,128)S(1)} %get-tuple-element.38.own_ref, f32[40,1024]{1,0:T(8,128)S(1)} %collective-permute-done.6.above_ref, bf16[80,256]{1,0:T(8,128)(2,1)S(1)} %get-tuple-element.42.band_ref), custom_call_target="tpu_custom_call" | custom-call | tf_op jit(solution)/shard_map/pallas_call | solution.py:500
  66.1 0.0 collective-permute-done.5.below_ref
  66.1 1.5 %shard_map.132 = f32[32,4096]{1,0:T(8,128)} custom-call(f32[32,4096]{1,0:T(8,128)S(1)} %get-tuple-element.38.own_ref, f32[40,1024]{1,0:T(8,128)S(1)} %collective-permute-done.5.below_ref, bf16[80,256]{1,0:T(8,128)(2,1)S(1)} %get-tuple-element.40.band_ref, f32[32,4096]{1,0:T(8,128)} %shard_map.131.begun_ref), custom_call_target="tpu_custom_call", output_to_operand_aliasing={{}: (3, {})} | custom-call | tf_op jit(solution)/shard_map/pallas_call | solution.py:503
  (20 shorter events, 0.2 us)
Async XLA Ops:
  0.6 13.3 %copy-start = (f32[9,21,21]{2,1,0:T(8,128)S(1)}, f32[9,21,21]{2,1,0:T(8,128)}, u32[]{:S(2)}) copy-start(f32[9,21,21]{2,1,0:T(8,128)} %param.12) | copy-start | bytes 47632
  0.6 1.1 %copy-start.1 = (f32[1,32,4096]{2,1,0:T(8,128)S(1)}, f32[1,32,4096]{2,1,0:T(8,128)}, u32[]{:S(2)}) copy-start(f32[1,32,4096]{2,1,0:T(8,128)} %param.11) | copy-start | bytes 1572868
  1.8 10.5 %copy-start.3 = (s32[1,32,4096]{2,1,0:T(8,128)S(1)}, s32[1,32,4096]{2,1,0:T(8,128)}, u32[]{:S(2)}) copy-start(s32[1,32,4096]{2,1,0:T(8,128)} %param.20) | copy-start | bytes 1572868
  1.8 22.1 %collective-permute-start = (f32[72,1024]{1,0:T(8,128)S(1)}, f32[72,1024]{1,0:T(8,128)S(1)}, u32[]{:S(2)}, u32[]{:S(2)}) collective-permute-start(f32[72,1024]{1,0:T(8,128)S(1)} %shard_map.124), channel_id=1, source_target_pairs={{0,1},{1,2},{2,3},{3,4},{4,5},{5,6},{6,7},{7,8},{8,9},{9,10},{10,1... | collective-permute-start | bytes 884744 | tf_op jit(solution)/shard_map/ppermute | solution.py:398
  5.4 18.5 %collective-permute-start.1 = (f32[72,1024]{1,0:T(8,128)S(1)}, f32[72,1024]{1,0:T(8,128)S(1)}, u32[]{:S(2)}, u32[]{:S(2)}) collective-permute-start(f32[72,1024]{1,0:T(8,128)S(1)} %shard_map.125), channel_id=1, source_target_pairs={{1,0},{2,1},{3,2},{4,3},{5,4},{6,5},{7,6},{8,7},{9,8},{10,9},{11,1... | collective-permute-start | bytes 884744 | tf_op jit(solution)/shard_map/ppermute | solution.py:402
  10.8 1.4 %copy-start.5 = (s32[1,4096]{1,0:T(1,128)S(1)}, s32[1,4096]{1,0:T(1,128)}, u32[]{:S(2)}) copy-start(s32[1,4096]{1,0:T(1,128)} %starts_ref.3) | copy-start | bytes 49156
  12.9 1.1 %copy-start.9 = (s32[1,32]{1,0:T(1,128)S(1)}, s32[1,32]{1,0:T(1,128)}, u32[]{:S(2)}) copy-start(s32[1,32]{1,0:T(1,128)} %param.14) | copy-start | bytes 388
  12.9 1.1 %copy-start.8 = (f32[1,9]{1,0:T(1,128)S(1)}, f32[1,9]{1,0:T(1,128)}, u32[]{:S(2)}) copy-start(f32[1,9]{1,0:T(1,128)} %param.13) | copy-start | bytes 112
  12.9 2.2 %collective-permute-start.2 = (f32[8,32,256]{2,1,0:T(8,128)S(1)}, f32[8,32,256]{2,1,0:T(8,128)S(1)}, u32[]{:S(2)}, u32[]{:S(2)}) collective-permute-start(f32[8,32,256]{2,1,0:T(8,128)S(1)} %get-tuple-element.30), channel_id=1, source_target_pairs={{0,16},{16,0},{32,48},{48,32},{64,80},{80,64},{96,112},{112,96},{1... | collective-permute-start | bytes 786440 | tf_op jit(solution)/shard_map/ppermute | solution.py:383
  15.1 7.0 %copy-start.2 = (f32[1,32,4096]{2,1,0:T(8,128)S(1)}, f32[1,32,4096]{2,1,0:T(8,128)}, u32[]{:S(2)}) copy-start(f32[1,32,4096]{2,1,0:T(8,128)} %param.11) | copy-start | bytes 1572868
  15.9 4.4 %copy-start.7 = (f32[1,8,32]{2,1,0:T(8,128)S(1)}, f32[1,8,32]{2,1,0:T(8,128)}, u32[]{:S(2)}) copy-start(f32[1,8,32]{2,1,0:T(8,128)} %param.15) | copy-start | bytes 3076
  15.9 12.3 %all-to-all-start = ((f32[8,32,256]{2,1,0:T(8,128)}), f32[8,32,256]{2,1,0:T(8,128)S(1)}, u32[]{:S(2)}, u32[]{:S(2)}) async-start(f32[8,32,256]{2,1,0:T(8,128)} %add.51), calls=%async_computation | async-start | bytes 524288 | tf_op jit(solution)/shard_map/all_to_all | solution.py:387
  22.1 1.9 %copy-start.4 = (f32[1,8,4096]{2,1,0:T(8,128)S(1)}, f32[1,8,4096]{2,1,0:T(8,128)}, u32[]{:S(2)}) copy-start(f32[1,8,4096]{2,1,0:T(8,128)} %param.18) | copy-start | bytes 393220
  28.1 0.8 %copy-start.6 = (f32[1,21,21]{2,0,1:T(1,128)S(1)}, f32[1,21,21]{2,0,1:T(1,128)}, u32[]{:S(2)}) copy-start(f32[1,21,21]{2,0,1:T(1,128)} %param.21) | copy-start | bytes 5296
  28.2 2.4 %collective-permute-start.3 = (f32[8,32,256]{2,1,0:T(8,128)S(1)}, f32[8,32,256]{2,1,0:T(8,128)S(1)}, u32[]{:S(2)}, u32[]{:S(2)}) collective-permute-start(f32[8,32,256]{2,1,0:T(8,128)S(1)} %get-tuple-element.31), channel_id=1, source_target_pairs={{0,16},{16,0},{32,48},{48,32},{64,80},{80,64},{96,112},{112,96},{1... | collective-permute-start | bytes 786440 | tf_op jit(solution)/shard_map/ppermute | solution.py:383
  50.9 4.3 %collective-permute-start.4 = (f32[8,32,256]{2,1,0:T(8,128)S(1)}, f32[8,32,256]{2,1,0:T(8,128)S(1)}, u32[]{:S(2)}, u32[]{:S(2)}) collective-permute-start(f32[8,32,256]{2,1,0:T(8,128)S(1)} %all_to_all.16.mine_ref), channel_id=1, source_target_pairs={{0,16},{16,0},{32,48},{48,32},{64,80},{80,64},{96,112},{112,96},{1... | collective-permute-start | bytes 786440 | tf_op jit(solution)/shard_map/ppermute | solution.py:383
  55.3 9.3 %collective-permute-start.6 = (f32[40,1024]{1,0:T(8,128)S(1)}, f32[40,1024]{1,0:T(8,128)S(1)}, u32[]{:S(2)}, u32[]{:S(2)}) collective-permute-start(f32[40,1024]{1,0:T(8,128)S(1)} %get-tuple-element.41), channel_id=1, source_target_pairs={{0,1},{1,2},{2,3},{3,4},{4,5},{5,6},{6,7},{7,8},{8,9},{9,10},{10,1... | collective-permute-start | bytes 491528 | tf_op jit(solution)/shard_map/ppermute | solution.py:398
  55.5 10.6 %collective-permute-start.5 = (f32[40,1024]{1,0:T(8,128)S(1)}, f32[40,1024]{1,0:T(8,128)S(1)}, u32[]{:S(2)}, u32[]{:S(2)}) collective-permute-start(f32[40,1024]{1,0:T(8,128)S(1)} %get-tuple-element.39), channel_id=1, source_target_pairs={{1,0},{2,1},{3,2},{4,3},{5,4},{6,5},{7,6},{8,7},{9,8},{10,9},{11,1... | collective-permute-start | bytes 491528 | tf_op jit(solution)/shard_map/ppermute | solution.py:402

commit v5 on v4

--- a/solution.py
+++ b/solution.py
@@ -115,8 +115,10 @@
     return pltpu.roll(values, shift, 1, stride=1, stride_axis=0)
 
 
-def first_bands_kernel(place_ref, lags_ref, mix_ref, own_ref, edge_ref):
-    has_above, has_below = place_ref[2] > 0, place_ref[2] < 15
+def first_bands_kernel(valid_ref, lags_ref, mix_ref, own_ref, edge_ref):
+    shape = (ROWS * GROUP * STEPS, SLOT)
+    has_above = jnp.broadcast_to(valid_ref[0:1, :], shape) > 0
+    has_below = jnp.broadcast_to(valid_ref[1:2, :], shape) > 0
     values = jnp.concatenate([skewed(lags_ref, lag, 48, 0) for lag in range(24)], axis=1)
     merged = jnp.dot(
         mix_ref[...], values, precision=lax.Precision.HIGHEST, preferred_element_type=F32
@@ -125,12 +127,14 @@
     put_both(own_ref, edge_ref, jnp.concatenate(slots, axis=0), has_above, has_below)
 
 
-def second_bands_kernel(place_ref, lags_ref, own_ref, above_ref, below_ref):
+def second_bands_kernel(valid_ref, lags_ref, own_ref, above_ref, below_ref):
     slots = [skewed(lags_ref, lag, ROWS, 8) for lag in range(24)]
     values = jnp.concatenate(slots, axis=0)
     put_bands(own_ref, between(values, BASE, BASE + ROWS, -BASE))
-    put_thin_bands(above_ref, values, BASE - THIN, 0, place_ref[2] > 0)
-    put_thin_bands(below_ref, values, BASE + ROWS, ROWS - THIN, place_ref[2] < 15)
+    has_above = jnp.broadcast_to(valid_ref[0:1, :], values.shape) > 0
+    has_below = jnp.broadcast_to(valid_ref[1:2, :], values.shape) > 0
+    put_thin_bands(above_ref, values, BASE - THIN, 0, has_above)
+    put_thin_bands(below_ref, values, BASE + ROWS, ROWS - THIN, has_below)
 
 
 def coverage(starts, offset, q):
@@ -424,6 +428,8 @@
     above = to_next(call(down_kernel, sds(72, CHUNK), [VM])(pixels))
     below = to_previous(call(up_kernel, sds(72, CHUNK), [VM])(pixels))
 
+    valid = jnp.stack([band > 0, band < 15]).astype(jnp.int32)
+    valid = jnp.broadcast_to(valid[:, None], (2, SLOT))
     first_core = jnp.full((1, BLOCK), visit % 2 == 0).astype(jnp.int32)
     kernel = jnp.einsum(
         "b,bij->ij", basis_coeffs[0], basis_kernels, precision=lax.Precision.HIGHEST
@@ -435,8 +441,8 @@
     mix = jnp.sum(jnp.where(hits & inside[None], row_taps[0][:, :, None], 0.0), axis=0)
     bands = sds(STEPS * ROWS, GROUP * SLOT, dtype=BF16)
     thin_bands = sds(THIN_STEPS * THIN, 256, dtype=BF16)
-    own_first, edge_first = call(first_bands_kernel, (bands, bands), [SM] + [VM] * 2)(
-        place, by_lag(kernel), mix
+    own_first, edge_first = call(first_bands_kernel, (bands, bands), [VM] * 3)(
+        valid, by_lag(kernel), mix
     )
 
     frames = [
@@ -475,8 +481,8 @@
     sent, denominator = lax.optimization_barrier((sent, denominator))
     second_lags, kept = lax.optimization_barrier((by_lag(decorrelation[0]), kept))
     own_second, above_second, below_second = call(
-        second_bands_kernel, (bands, thin_bands, thin_bands), [SM, VM]
-    )(place, second_lags)
+        second_bands_kernel, (bands, thin_bands, thin_bands), [VM] * 2
+    )(valid, second_lags)
     half = kept + swap(sent, 1)
     half, own_second = lax.optimization_barrier((half, own_second))
     coadd = jnp.sum(over_chips(half), axis=0) / denominator

time: 68.2 us -> 68.1 us (level)
  local copies, waits for them, and re-layouts: 1.48 us -> 3.73 us
  Pallas kernels: 15.4 us -> 14.3 us
    unnamed x21, local copies, waits for them, and re-layouts: 1.21 us -> 3.39 us
    pallas_call x2, Pallas kernels: 3.25 us -> 2.17 us  [the longest x1 1.18 us: on_device(): call(first_bands_kernel, (bands, bands), [VM] * 3)]
  transfers between devices with their start and end apart: 8 -> 8, of which waited for: 3 -> 2; matrix products, arithmetic and copies ran while one was open for 2% -> 3% of each run, Pallas kernels for 20% -> 19%
where the time goes in v5:
time: 68.1 us; the launch traced here: 67.6 us
  starting transfers between devices  23.2 us (34%)
  blocking collectives  19.8 us (29%)
  Pallas kernels  14.3 us (21%)
  local copies, waits for them, and re-layouts  3.73 us (5%)
  waiting for transfers between devices  2.8 us (4%)
  between operations  2.34 us (3%)
  other arithmetic  1.18 us (2%)
    all_to_all x2, blocking collectives, over_chips(): lax.all_to_all(blocks, 'visit', split_axis=0, concat_axis=0, axis_index_g...  19.8 us
    ppermute x2, starting transfers between devices, to_previous(): return lax.ppermute(values, 'row', [((i + 1) % 16, i) for i in range(16)])  10.5 us
    ppermute x3, starting transfers between devices, swap(): return lax.ppermute(values, 'visit', [(i, i ^ step) for i in range(16)])  4.59 us
    all_to_all x1, starting transfers between devices, over_chips(): lax.all_to_all(blocks, 'visit', split_axis=0, concat_axis=0, axis_index_g...  4.22 us
    pallas_call x1, Pallas kernels, on_device(): call(warp_kernel, (sds(ROWS, COLS), blocks, blocks), [ANY, ANY] + [VM] *...  4.15 us
    ppermute x2, starting transfers between devices, to_next(): return lax.ppermute(values, 'row', [(i, (i + 1) % 16) for i in range(16)])  3.91 us
    unnamed x21, local copies, waits for them, and re-layouts  3.39 us
    pallas_call x1, Pallas kernels, on_device(): call(own_and_template_kernel, (sds(ROWS, COLS), sds(ROWS, BLOCK)), [VM] *...  2.37 us
  transfers between devices with their start and end apart: 8, of which 2 were waited for; matrix products, arithmetic and copies ran while one was open for 3% of the time, Pallas kernels for 19%

profile of v5, /device:TPU:1, one launch (start us, length us, event | category | flops | bytes accessed | tf_op | source)
XLA Modules:
  0.0 67.6 jit_solution(18352809381587052352)
XLA Ops:
  0.6 0.0 copy-start
  0.6 0.0 copy-start.1
  0.7 1.1 %copy-done.1 = f32[1,32,4096]{2,1,0:T(8,128)S(1)} copy-done((f32[1,32,4096]{2,1,0:T(8,128)S(1)}, f32[1,32,4096]{2,1,0:T(8,128)}, u32[]{:S(2)}) %copy-start.1) | copy-done | bytes 524312
  1.8 0.0 copy-start.3
  1.8 3.7 %collective-permute-start = (f32[72,1024]{1,0:T(8,128)S(1)}, f32[72,1024]{1,0:T(8,128)S(1)}, u32[]{:S(2)}, u32[]{:S(2)}) collective-permute-start(f32[72,1024]{1,0:T(8,128)S(1)} %shard_map.124), channel_id=1, source_target_pairs={{0,1},{1,2},{2,3},{3,4},{4,5},{5,6},{6,7},{7,8},{8,9},{9,10},{10,1... | collective-permute-start | bytes 884744 | tf_op jit(solution)/shard_map/ppermute | solution.py:402
  5.4 5.4 %collective-permute-start.1 = (f32[72,1024]{1,0:T(8,128)S(1)}, f32[72,1024]{1,0:T(8,128)S(1)}, u32[]{:S(2)}, u32[]{:S(2)}) collective-permute-start(f32[72,1024]{1,0:T(8,128)S(1)} %shard_map.125), channel_id=1, source_target_pairs={{1,0},{2,1},{3,2},{4,3},{5,4},{6,5},{7,6},{8,7},{9,8},{10,9},{11,1... | collective-permute-start | bytes 884744 | tf_op jit(solution)/shard_map/ppermute | solution.py:406
  12.1 0.1 pad_add_fusion.place_source_ref.place_ref
  12.2 0.6 shard_map.127
  12.9 1.0 %collective-permute-start.2 = (f32[8,32,256]{2,1,0:T(8,128)S(1)}, f32[8,32,256]{2,1,0:T(8,128)S(1)}, u32[]{:S(2)}, u32[]{:S(2)}) collective-permute-start(f32[8,32,256]{2,1,0:T(8,128)S(1)} %get-tuple-element.30), channel_id=1, source_target_pairs={{0,16},{16,0},{32,48},{48,32},{64,80},{80,64},{96,112},{112,96},{1... | collective-permute-start | bytes 786440 | tf_op jit(solution)/shard_map/ppermute | solution.py:387
  13.9 0.7 copy-done.9
  14.6 0.6 copy-done.8
  15.2 0.2 fusion
  15.5 0.1 copy.17
  15.5 0.1 pad.7.lags_ref
  15.6 0.1 broadcast_subtract_fusion
  15.7 0.0 collective-permute-done.2
  15.7 0.0 copy-start.2
  15.7 0.7 %add.51 = f32[8,32,256]{2,1,0:T(8,128)} add(f32[8,32,256]{2,1,0:T(8,128)S(1)} %get-tuple-element.29, f32[8,32,256]{2,1,0:T(8,128)S(1)} %collective-permute-done.2) | non-fusion elementwise | flops 65536 | bytes 786432 | tf_op jit(solution)/shard_map/add | solution.py:457
  16.5 4.2 %all-to-all-start = ((f32[8,32,256]{2,1,0:T(8,128)}), f32[8,32,256]{2,1,0:T(8,128)S(1)}, u32[]{:S(2)}, u32[]{:S(2)}) async-start(f32[8,32,256]{2,1,0:T(8,128)} %add.51), calls=%async_computation | async-start | bytes 524288 | tf_op jit(solution)/shard_map/all_to_all | solution.py:391
  20.7 0.1 add_convert_fusion
  20.8 0.6 copy-done.7
  21.4 0.1 select_reduce_fusion.mix_ref
  21.5 0.1 broadcast_in_dim.38.valid_ref
  21.6 1.2 %shard_map.122 = (bf16[192,512]{1,0:T(8,128)(2,1)S(1)}, bf16[192,512]{1,0:T(8,128)(2,1)S(1)}) custom-call(s32[2,128]{1,0:T(2,128)S(1)} %broadcast_in_dim.38.valid_ref, f32[24,128]{1,0:T(8,128)S(1)} %pad.7.lags_ref, f32[32,48]{1,0:T(8,128)S(1)} %select_reduce_fusion.mix_ref), custom_call_target="tpu_custom_call" | custom-call | tf_op jit(solution)/shard_map/pallas_call | solution.py:444
  22.8 0.0 copy-start.4
  22.8 1.8 %shard_map.123.own_ref = f32[32,4096]{1,0:T(8,128)S(1)} custom-call(f32[32,4096]{1,0:T(8,128)S(1)} %bitcast.24, bf16[192,512]{1,0:T(8,128)(2,1)S(1)} %get-tuple-element.23.band_ref), custom_call_target="tpu_custom_call" | custom-call | tf_op jit(solution)/shard_map/pallas_call | solution.py:452
  24.6 0.0 collective-permute-done.above_ref
  24.6 0.0 collective-permute-done.1.below_ref
  24.6 4.2 %shard_map.126 = (f32[32,4096]{1,0:T(8,128)S(1)}, f32[8,32,256]{2,1,0:T(8,128)S(1)}, f32[8,32,256]{2,1,0:T(8,128)S(1)}) custom-call(s32[3]{0:T(128)S(1)} %pad_add_fusion.place_source_ref.place_ref, f32[1]{0:T(128)S(6)} %copy.22.weight_source_ref.weight_ref, f32[32,4096]{1,0:T(8,128)S(1)} %shard_map.123.own_ref, ...), custom_call_target="tpu_custom_call" | custom-call | tf_op jit(solution)/shard_map/pallas_call | solution.py:459
  28.8 0.0 all-to-all-done
  28.8 0.0 copy-start.6
  28.8 0.4 collective-permute-start.3
  29.2 0.3 copy-done.6
  29.5 0.1 copy.15
  29.6 0.1 pad.8.lags_ref
  29.7 1.0 %shard_map.128 = (bf16[192,512]{1,0:T(8,128)(2,1)S(1)}, bf16[80,256]{1,0:T(8,128)(2,1)S(1)}, bf16[80,256]{1,0:T(8,128)(2,1)S(1)}) custom-call(s32[2,128]{1,0:T(2,128)S(1)} %broadcast_in_dim.38.valid_ref, f32[24,128]{1,0:T(8,128)S(1)} %pad.8.lags_ref), custom_call_target="tpu_custom_call" | custom-call | tf_op jit(solution)/shard_map/pallas_call | solution.py:483
  30.7 0.0 collective-permute-done.3
  30.7 11.1 %all_to_all.15 = f32[8,32,256]{2,1,0:T(8,128)S(1)} all-to-all(f32[8,32,256]{2,1,0:T(8,128)S(1)} %add.52), channel_id=1, replica_groups={{0,32,64,96,128,160,192,224},{16,48,80,112,144,176,208,240},{1,33,65,97..., dimensions={0} | all-to-all | bytes 524288 | tf_op jit(solution)/shard_map/all_to_all | solution.py:391
  41.9 8.7 %all_to_all.16.mine_ref = f32[8,32,256]{2,1,0:T(8,128)S(1)} all-to-all(f32[8,32,256]{2,1,0:T(8,128)S(1)} %broadcast_in_dim.42), channel_id=1, replica_groups={{0,32,64,96,128,160,192,224},{16,48,80,112,144,176,208,240},{1,33,65,97..., dimensions={0} | all-to-all | bytes 524288 | tf_op jit(solution)/shard_map/all_to_all | solution.py:391
  50.6 3.1 %collective-permute-start.4 = (f32[8,32,256]{2,1,0:T(8,128)S(1)}, f32[8,32,256]{2,1,0:T(8,128)S(1)}, u32[]{:S(2)}, u32[]{:S(2)}) collective-permute-start(f32[8,32,256]{2,1,0:T(8,128)S(1)} %all_to_all.16.mine_ref), channel_id=1, source_target_pairs={{0,16},{16,0},{32,48},{48,32},{64,80},{80,64},{96,112},{112,96},{1... | collective-permute-start | bytes 786440 | tf_op jit(solution)/shard_map/ppermute | solution.py:387
  53.8 1.2 %collective-permute-done.4.other_ref = f32[8,32,256]{2,1,0:T(8,128)S(1)} collective-permute-done((f32[8,32,256]{2,1,0:T(8,128)S(1)}, f32[8,32,256]{2,1,0:T(8,128)S(1)}, u32[]{:S(2)}, u32[]{:S(2)}) %collective-permute-start.4) | collective-permute-done | bytes 262176 | tf_op jit(solution)/shard_map/ppermute | solution.py:387
  55.0 0.1 shard_map.129
  55.0 0.3 collective-permute-start.6
  55.3 5.1 %collective-permute-start.5 = (f32[40,1024]{1,0:T(8,128)S(1)}, f32[40,1024]{1,0:T(8,128)S(1)}, u32[]{:S(2)}, u32[]{:S(2)}) collective-permute-start(f32[40,1024]{1,0:T(8,128)S(1)} %get-tuple-element.39), channel_id=1, source_target_pairs={{1,0},{2,1},{3,2},{4,3},{5,4},{6,5},{7,6},{8,7},{9,8},{10,9},{11,1... | collective-permute-start | bytes 491528 | tf_op jit(solution)/shard_map/ppermute | solution.py:406
  60.4 2.4 %shard_map.130 = (f32[32,4096]{1,0:T(8,128)S(1)}, f32[32,256]{1,0:T(8,128)}) custom-call(f32[32,4096]{1,0:T(8,128)S(1)} %get-tuple-element.36.own_ref, bf16[192,512]{1,0:T(8,128)(2,1)S(1)} %get-tuple-element.37.band_ref, f32[32,256]{1,0:T(8,128)S(1)} %div.3.coadd_ref), custom_call_target="tpu_custom_call" | custom-call | tf_op jit(solution)/shard_map/pallas_call | solution.py:497
  62.8 1.6 %collective-permute-done.6.above_ref = f32[40,1024]{1,0:T(8,128)S(1)} collective-permute-done((f32[40,1024]{1,0:T(8,128)S(1)}, f32[40,1024]{1,0:T(8,128)S(1)}, u32[]{:S(2)}, u32[]{:S(2)}) %collective-permute-start.6) | collective-permute-done | bytes 163872 | tf_op jit(solution)/shard_map/ppermute | solution.py:402
  64.4 1.5 %shard_map.131.begun_ref = f32[32,4096]{1,0:T(8,128)} custom-call(f32[32,4096]{1,0:T(8,128)S(1)} %get-tuple-element.38.own_ref, f32[40,1024]{1,0:T(8,128)S(1)} %collective-permute-done.6.above_ref, bf16[80,256]{1,0:T(8,128)(2,1)S(1)} %get-tuple-element.42.band_ref), custom_call_target="tpu_custom_call" | custom-call | tf_op jit(solution)/shard_map/pallas_call | solution.py:506
  65.9 1.5 %shard_map.132 = f32[32,4096]{1,0:T(8,128)} custom-call(f32[32,4096]{1,0:T(8,128)S(1)} %get-tuple-element.38.own_ref, f32[40,1024]{1,0:T(8,128)S(1)} %collective-permute-done.5.below_ref, bf16[80,256]{1,0:T(8,128)(2,1)S(1)} %get-tuple-element.40.band_ref, f32[32,4096]{1,0:T(8,128)} %shard_map.131.begun_ref), custom_call_target="tpu_custom_call", output_to_operand_aliasing={{}: (3, {})} | custom-call | tf_op jit(solution)/shard_map/pallas_call | solution.py:509
  (22 shorter events, 0.2 us)
Async XLA Ops:
  0.6 14.0 %copy-start = (f32[9,21,21]{2,1,0:T(8,128)S(1)}, f32[9,21,21]{2,1,0:T(8,128)}, u32[]{:S(2)}) copy-start(f32[9,21,21]{2,1,0:T(8,128)} %param.12) | copy-start | bytes 47632
  0.6 1.1 %copy-start.1 = (f32[1,32,4096]{2,1,0:T(8,128)S(1)}, f32[1,32,4096]{2,1,0:T(8,128)}, u32[]{:S(2)}) copy-start(f32[1,32,4096]{2,1,0:T(8,128)} %param.11) | copy-start | bytes 1572868
  1.8 10.5 %copy-start.3 = (s32[1,32,4096]{2,1,0:T(8,128)S(1)}, s32[1,32,4096]{2,1,0:T(8,128)}, u32[]{:S(2)}) copy-start(s32[1,32,4096]{2,1,0:T(8,128)} %param.20) | copy-start | bytes 1572868
  1.8 22.8 %collective-permute-start = (f32[72,1024]{1,0:T(8,128)S(1)}, f32[72,1024]{1,0:T(8,128)S(1)}, u32[]{:S(2)}, u32[]{:S(2)}) collective-permute-start(f32[72,1024]{1,0:T(8,128)S(1)} %shard_map.124), channel_id=1, source_target_pairs={{0,1},{1,2},{2,3},{3,4},{4,5},{5,6},{6,7},{7,8},{8,9},{9,10},{10,1... | collective-permute-start | bytes 884744 | tf_op jit(solution)/shard_map/ppermute | solution.py:402
  5.4 19.1 %collective-permute-start.1 = (f32[72,1024]{1,0:T(8,128)S(1)}, f32[72,1024]{1,0:T(8,128)S(1)}, u32[]{:S(2)}, u32[]{:S(2)}) collective-permute-start(f32[72,1024]{1,0:T(8,128)S(1)} %shard_map.125), channel_id=1, source_target_pairs={{1,0},{2,1},{3,2},{4,3},{5,4},{6,5},{7,6},{8,7},{9,8},{10,9},{11,1... | collective-permute-start | bytes 884744 | tf_op jit(solution)/shard_map/ppermute | solution.py:406
  10.8 1.4 %copy-start.5 = (s32[1,4096]{1,0:T(1,128)S(1)}, s32[1,4096]{1,0:T(1,128)}, u32[]{:S(2)}) copy-start(s32[1,4096]{1,0:T(1,128)} %starts_ref.3) | copy-start | bytes 49156
  12.9 2.8 %collective-permute-start.2 = (f32[8,32,256]{2,1,0:T(8,128)S(1)}, f32[8,32,256]{2,1,0:T(8,128)S(1)}, u32[]{:S(2)}, u32[]{:S(2)}) collective-permute-start(f32[8,32,256]{2,1,0:T(8,128)S(1)} %get-tuple-element.30), channel_id=1, source_target_pairs={{0,16},{16,0},{32,48},{48,32},{64,80},{80,64},{96,112},{112,96},{1... | collective-permute-start | bytes 786440 | tf_op jit(solution)/shard_map/ppermute | solution.py:387
  13.9 0.7 copy-start.9
  14.6 0.7 copy-start.8
  15.7 7.0 %copy-start.2 = (f32[1,32,4096]{2,1,0:T(8,128)S(1)}, f32[1,32,4096]{2,1,0:T(8,128)}, u32[]{:S(2)}) copy-start(f32[1,32,4096]{2,1,0:T(8,128)} %param.11) | copy-start | bytes 1572868
  16.5 12.3 %all-to-all-start = ((f32[8,32,256]{2,1,0:T(8,128)}), f32[8,32,256]{2,1,0:T(8,128)S(1)}, u32[]{:S(2)}, u32[]{:S(2)}) async-start(f32[8,32,256]{2,1,0:T(8,128)} %add.51), calls=%async_computation | async-start | bytes 524288 | tf_op jit(solution)/shard_map/all_to_all | solution.py:391
  20.7 0.7 %copy-start.7 = (f32[1,8,32]{2,1,0:T(8,128)S(1)}, f32[1,8,32]{2,1,0:T(8,128)}, u32[]{:S(2)}) copy-start(f32[1,8,32]{2,1,0:T(8,128)} %param.15) | copy-start | bytes 3076
  22.8 1.8 %copy-start.4 = (f32[1,8,4096]{2,1,0:T(8,128)S(1)}, f32[1,8,4096]{2,1,0:T(8,128)}, u32[]{:S(2)}) copy-start(f32[1,8,4096]{2,1,0:T(8,128)} %param.18) | copy-start | bytes 393220
  28.8 0.7 %copy-start.6 = (f32[1,21,21]{2,0,1:T(1,128)S(1)}, f32[1,21,21]{2,0,1:T(1,128)}, u32[]{:S(2)}) copy-start(f32[1,21,21]{2,0,1:T(1,128)} %param.21) | copy-start | bytes 5296
  28.8 1.9 %collective-permute-start.3 = (f32[8,32,256]{2,1,0:T(8,128)S(1)}, f32[8,32,256]{2,1,0:T(8,128)S(1)}, u32[]{:S(2)}, u32[]{:S(2)}) collective-permute-start(f32[8,32,256]{2,1,0:T(8,128)S(1)} %get-tuple-element.31), channel_id=1, source_target_pairs={{0,16},{16,0},{32,48},{48,32},{64,80},{80,64},{96,112},{112,96},{1... | collective-permute-start | bytes 786440 | tf_op jit(solution)/shard_map/ppermute | solution.py:387
  50.6 4.3 %collective-permute-start.4 = (f32[8,32,256]{2,1,0:T(8,128)S(1)}, f32[8,32,256]{2,1,0:T(8,128)S(1)}, u32[]{:S(2)}, u32[]{:S(2)}) collective-permute-start(f32[8,32,256]{2,1,0:T(8,128)S(1)} %all_to_all.16.mine_ref), channel_id=1, source_target_pairs={{0,16},{16,0},{32,48},{48,32},{64,80},{80,64},{96,112},{112,96},{1... | collective-permute-start | bytes 786440 | tf_op jit(solution)/shard_map/ppermute | solution.py:387
  55.0 9.3 %collective-permute-start.6 = (f32[40,1024]{1,0:T(8,128)S(1)}, f32[40,1024]{1,0:T(8,128)S(1)}, u32[]{:S(2)}, u32[]{:S(2)}) collective-permute-start(f32[40,1024]{1,0:T(8,128)S(1)} %get-tuple-element.41), channel_id=1, source_target_pairs={{0,1},{1,2},{2,3},{3,4},{4,5},{5,6},{6,7},{7,8},{8,9},{9,10},{10,1... | collective-permute-start | bytes 491528 | tf_op jit(solution)/shard_map/ppermute | solution.py:402
  55.3 10.6 %collective-permute-start.5 = (f32[40,1024]{1,0:T(8,128)S(1)}, f32[40,1024]{1,0:T(8,128)S(1)}, u32[]{:S(2)}, u32[]{:S(2)}) collective-permute-start(f32[40,1024]{1,0:T(8,128)S(1)} %get-tuple-element.39), channel_id=1, source_target_pairs={{1,0},{2,1},{3,2},{4,3},{5,4},{6,5},{7,6},{8,7},{9,8},{10,9},{11,1... | collective-permute-start | bytes 491528 | tf_op jit(solution)/shard_map/ppermute | solution.py:406

commit v6 on v5

--- a/solution.py
+++ b/solution.py
@@ -143,20 +143,23 @@
     return ((actual >= 0) & (actual <= COLS - TAPS)).astype(F32)
 
 
-def put_blocks(kept_ref, sent_ref, values, core, q):
+def put_blocks(kept_ref, sent_ref, values, first_core, q):
     blocks = [values[:, j * BLOCK : (j + 1) * BLOCK] for j in range(4)]
     for j in range(2):
         even, odd = blocks[2 * j : 2 * j + 2]
-        kept_ref[2 * q + j] = jnp.where(core == 0, even, odd)
-        sent_ref[2 * q + j] = jnp.where(core == 0, odd, even)
-
-
-def share_kernel(place_ref, weight_ref, mask_ref, starts_ref, kept_ref, sent_ref):
-    for q in range(4):
-        cols = pl.ds(q * CHUNK, CHUNK)
-        covered = coverage(starts_ref[:, cols], place_ref[0], q)
-        share = weight_ref[0] * mask_ref[:, cols].astype(F32) * covered
-        put_blocks(kept_ref, sent_ref, share, place_ref[1], q)
+        kept_ref[2 * q + j] = jnp.where(first_core, even, odd)
+        sent_ref[2 * q + j] = jnp.where(first_core, odd, even)
+
+
+def share_kernel(
+    offset_ref, weight_ref, first_core_ref, mask_ref, starts_ref, kept_ref, sent_ref
+):
+    first_core = jnp.broadcast_to(first_core_ref[...], (ROWS, BLOCK)) > 0
+    for q in range(4):
+        cols = pl.ds(q * CHUNK, CHUNK)
+        covered = coverage(starts_ref[:, cols], offset_ref[...], q)
+        share = weight_ref[...] * mask_ref[:, cols].astype(F32) * covered
+        put_blocks(kept_ref, sent_ref, share, first_core, q)
 
 
 def clear(frame_ref, row):
@@ -283,7 +286,7 @@
             total = term if total is None else total + term
         warped_ref[:, cols] = total
         share = weight_ref[0] * mask_ref[:, cols].astype(F32) * coverage(starts, offset, q)
-        put_blocks(kept_ref, sent_ref, share * total, place_ref[1], q)
+        put_blocks(kept_ref, sent_ref, share * total, place_ref[1] == 0, q)
 
 
 def differ_kernel(
@@ -451,8 +454,8 @@
     ]
     own_part = call(own_kernel, sds(ROWS, COLS), [VM] * 2, frames)(pixels, own_first)
     blocks = sds(8, ROWS, BLOCK)
-    kept, sent = call(share_kernel, (blocks, blocks), [SM, SM, VM, VM])(
-        place, visit_weights, clip_masks[0], col_starts
+    kept, sent = call(share_kernel, (blocks, blocks), [VM] * 5)(
+        col_offsets[None], visit_weights[None], first_core, clip_masks[0], col_starts
     )
     shares = kept + swap(sent, 1)
     denominator = jnp.maximum(jnp.sum(over_chips(shares), axis=0), 1.0)

time: 68.1 us -> 67 us (0.984)
  local copies, waits for them, and re-layouts: 3.73 us -> 2.19 us
  starting transfers between devices: 23.2 us -> 24.1 us
    unnamed x21, local copies, waits for them, and re-layouts: 3.39 us -> 1.85 us
    ppermute x3, starting transfers between devices: 4.59 us -> 5.4 us  [swap(): return lax.ppermute(values, 'visit', [(i, i ^ step) for i in range(16)])]
  transfers between devices with their start and end apart: 8 -> 8, of which waited for: 2 -> 2; matrix products, arithmetic and copies ran while one was open for 3% -> 3% of each run, Pallas kernels for 19% -> 18%
where the time goes in v6:
time: 67 us; the launch traced here: 66.6 us
  starting transfers between devices  24.1 us (36%)
  blocking collectives  19.8 us (30%)
  Pallas kernels  13.9 us (21%)
  waiting for transfers between devices  2.8 us (4%)
  between operations  2.35 us (4%)
  local copies, waits for them, and re-layouts  2.19 us (3%)
  other arithmetic  1.18 us (2%)
    all_to_all x2, blocking collectives, over_chips(): lax.all_to_all(blocks, 'visit', split_axis=0, concat_axis=0, axis_index_g...  19.8 us
    ppermute x2, starting transfers between devices, to_previous(): return lax.ppermute(values, 'row', [((i + 1) % 16, i) for i in range(16)])  10.5 us
    ppermute x3, starting transfers between devices, swap(): return lax.ppermute(values, 'visit', [(i, i ^ step) for i in range(16)])  5.4 us
    all_to_all x1, starting transfers between devices, over_chips(): lax.all_to_all(blocks, 'visit', split_axis=0, concat_axis=0, axis_index_g...  4.35 us
    pallas_call x1, Pallas kernels, on_device(): call(warp_kernel, (sds(ROWS, COLS), blocks, blocks), [ANY, ANY] + [VM] *...  4.18 us
    ppermute x2, starting transfers between devices, to_next(): return lax.ppermute(values, 'row', [(i, (i + 1) % 16) for i in range(16)])  3.91 us
    pallas_call x1, Pallas kernels, on_device(): call(own_and_template_kernel, (sds(ROWS, COLS), sds(ROWS, BLOCK)), [VM] *...  2.37 us
    unnamed x21, local copies, waits for them, and re-layouts  1.85 us
  transfers between devices with their start and end apart: 8, of which 2 were waited for; matrix products, arithmetic and copies ran while one was open for 3% of the time, Pallas kernels for 18%

profile of v6, /device:TPU:1, one launch (start us, length us, event | category | flops | bytes accessed | tf_op | source)
XLA Modules:
  0.0 66.6 jit_solution(10478949595527765220)
XLA Ops:
  0.6 0.0 copy-start
  0.6 0.0 copy-start.1
  0.7 1.1 %copy-done.1 = f32[1,32,4096]{2,1,0:T(8,128)S(1)} copy-done((f32[1,32,4096]{2,1,0:T(8,128)S(1)}, f32[1,32,4096]{2,1,0:T(8,128)}, u32[]{:S(2)}) %copy-start.1) | copy-done | bytes 524312
  1.8 0.0 copy-start.3
  1.8 3.7 %collective-permute-start = (f32[72,1024]{1,0:T(8,128)S(1)}, f32[72,1024]{1,0:T(8,128)S(1)}, u32[]{:S(2)}, u32[]{:S(2)}) collective-permute-start(f32[72,1024]{1,0:T(8,128)S(1)} %shard_map.124), channel_id=1, source_target_pairs={{0,1},{1,2},{2,3},{3,4},{4,5},{5,6},{6,7},{7,8},{8,9},{9,10},{10,1... | collective-permute-start | bytes 884744 | tf_op jit(solution)/shard_map/ppermute | solution.py:405
  5.4 5.4 %collective-permute-start.1 = (f32[72,1024]{1,0:T(8,128)S(1)}, f32[72,1024]{1,0:T(8,128)S(1)}, u32[]{:S(2)}, u32[]{:S(2)}) collective-permute-start(f32[72,1024]{1,0:T(8,128)S(1)} %shard_map.125), channel_id=1, source_target_pairs={{1,0},{2,1},{3,2},{4,3},{5,4},{6,5},{7,6},{8,7},{9,8},{10,9},{11,1... | collective-permute-start | bytes 884744 | tf_op jit(solution)/shard_map/ppermute | solution.py:409
  12.2 0.0 copy-done.3
  12.2 0.0 copy-done.5
  12.2 0.2 shard_map.127
  12.4 0.0 copy-start.9
  12.4 1.0 %collective-permute-start.2 = (f32[8,32,256]{2,1,0:T(8,128)S(1)}, f32[8,32,256]{2,1,0:T(8,128)S(1)}, u32[]{:S(2)}, u32[]{:S(2)}) collective-permute-start(f32[8,32,256]{2,1,0:T(8,128)S(1)} %get-tuple-element.30), channel_id=1, source_target_pairs={{0,16},{16,0},{32,48},{48,32},{64,80},{80,64},{96,112},{112,96},{1... | collective-permute-start | bytes 786440 | tf_op jit(solution)/shard_map/ppermute | solution.py:390
  13.4 0.6 copy-done.8
  14.1 0.2 fusion
  14.3 0.1 broadcast_subtract_fusion
  14.4 0.1 copy.17
  14.5 0.1 pad.7.lags_ref
  14.5 0.1 add_convert_fusion
  14.6 0.0 collective-permute-done.2
  14.6 0.7 %add.51 = f32[8,32,256]{2,1,0:T(8,128)} add(f32[8,32,256]{2,1,0:T(8,128)S(1)} %get-tuple-element.29, f32[8,32,256]{2,1,0:T(8,128)S(1)} %collective-permute-done.2) | non-fusion elementwise | flops 65536 | bytes 786432 | tf_op jit(solution)/shard_map/add | solution.py:460
  15.4 4.3 %all-to-all-start = ((f32[8,32,256]{2,1,0:T(8,128)}), f32[8,32,256]{2,1,0:T(8,128)S(1)}, u32[]{:S(2)}, u32[]{:S(2)}) async-start(f32[8,32,256]{2,1,0:T(8,128)} %add.51), calls=%async_computation | async-start | bytes 524288 | tf_op jit(solution)/shard_map/all_to_all | solution.py:394
  19.7 0.1 select_reduce_fusion.mix_ref
  19.8 0.1 broadcast_in_dim.44.valid_ref
  19.9 1.2 %shard_map.122 = (bf16[192,512]{1,0:T(8,128)(2,1)S(1)}, bf16[192,512]{1,0:T(8,128)(2,1)S(1)}) custom-call(s32[2,128]{1,0:T(2,128)S(1)} %broadcast_in_dim.44.valid_ref, f32[24,128]{1,0:T(8,128)S(1)} %pad.7.lags_ref, f32[32,48]{1,0:T(8,128)S(1)} %select_reduce_fusion.mix_ref), custom_call_target="tpu_custom_call" | custom-call | tf_op jit(solution)/shard_map/pallas_call | solution.py:447
  21.1 0.0 copy-start.4
  21.1 1.8 %shard_map.123.own_ref = f32[32,4096]{1,0:T(8,128)S(1)} custom-call(f32[32,4096]{1,0:T(8,128)S(1)} %bitcast.28, bf16[192,512]{1,0:T(8,128)(2,1)S(1)} %get-tuple-element.23.band_ref), custom_call_target="tpu_custom_call" | custom-call | tf_op jit(solution)/shard_map/pallas_call | solution.py:455
  22.9 0.1 pad_add_fusion.place_source_ref
  23.0 0.0 collective-permute-done.above_ref
  23.0 0.0 collective-permute-done.1.below_ref
  23.0 4.2 %shard_map.126 = (f32[32,4096]{1,0:T(8,128)S(1)}, f32[8,32,256]{2,1,0:T(8,128)S(1)}, f32[8,32,256]{2,1,0:T(8,128)S(1)}) custom-call(s32[3]{0:T(128)S(1)} %pad_add_fusion.place_source_ref, f32[1]{0:T(128)} %copy.22.weight_source_ref, f32[32,4096]{1,0:T(8,128)S(1)} %shard_map.123.own_ref, f32[72,1024]{1,0:T(8,128)S(1)} %collective-permute-done.above_ref, ...), custom_call_target="tpu_custom_call" | custom-call | tf_op jit(solution)/shard_map/pallas_call | solution.py:462
  27.2 0.0 all-to-all-done
  27.2 0.0 copy-start.6
  27.3 1.2 %collective-permute-start.3 = (f32[8,32,256]{2,1,0:T(8,128)S(1)}, f32[8,32,256]{2,1,0:T(8,128)S(1)}, u32[]{:S(2)}, u32[]{:S(2)}) collective-permute-start(f32[8,32,256]{2,1,0:T(8,128)S(1)} %get-tuple-element.31), channel_id=1, source_target_pairs={{0,16},{16,0},{32,48},{48,32},{64,80},{80,64},{96,112},{112,96},{1... | collective-permute-start | bytes 786440 | tf_op jit(solution)/shard_map/ppermute | solution.py:390
  28.5 0.1 copy.15
  28.6 0.1 pad.8.lags_ref
  28.7 1.0 %shard_map.128 = (bf16[192,512]{1,0:T(8,128)(2,1)S(1)}, bf16[80,256]{1,0:T(8,128)(2,1)S(1)}, bf16[80,256]{1,0:T(8,128)(2,1)S(1)}) custom-call(s32[2,128]{1,0:T(2,128)S(1)} %broadcast_in_dim.44.valid_ref, f32[24,128]{1,0:T(8,128)S(1)} %pad.8.lags_ref), custom_call_target="tpu_custom_call" | custom-call | tf_op jit(solution)/shard_map/pallas_call | solution.py:486
  29.7 0.0 collective-permute-done.3
  29.7 11.1 %all_to_all.15 = f32[8,32,256]{2,1,0:T(8,128)S(1)} all-to-all(f32[8,32,256]{2,1,0:T(8,128)S(1)} %add.52), channel_id=1, replica_groups={{0,32,64,96,128,160,192,224},{16,48,80,112,144,176,208,240},{1,33,65,97..., dimensions={0} | all-to-all | bytes 524288 | tf_op jit(solution)/shard_map/all_to_all | solution.py:394
  40.9 8.7 %all_to_all.16.mine_ref = f32[8,32,256]{2,1,0:T(8,128)S(1)} all-to-all(f32[8,32,256]{2,1,0:T(8,128)S(1)} %broadcast_in_dim.50), channel_id=1, replica_groups={{0,32,64,96,128,160,192,224},{16,48,80,112,144,176,208,240},{1,33,65,97..., dimensions={0} | all-to-all | bytes 524288 | tf_op jit(solution)/shard_map/all_to_all | solution.py:394
  49.6 3.1 %collective-permute-start.4 = (f32[8,32,256]{2,1,0:T(8,128)S(1)}, f32[8,32,256]{2,1,0:T(8,128)S(1)}, u32[]{:S(2)}, u32[]{:S(2)}) collective-permute-start(f32[8,32,256]{2,1,0:T(8,128)S(1)} %all_to_all.16.mine_ref), channel_id=1, source_target_pairs={{0,16},{16,0},{32,48},{48,32},{64,80},{80,64},{96,112},{112,96},{1... | collective-permute-start | bytes 786440 | tf_op jit(solution)/shard_map/ppermute | solution.py:390
  52.7 1.2 %collective-permute-done.4.other_ref = f32[8,32,256]{2,1,0:T(8,128)S(1)} collective-permute-done((f32[8,32,256]{2,1,0:T(8,128)S(1)}, f32[8,32,256]{2,1,0:T(8,128)S(1)}, u32[]{:S(2)}, u32[]{:S(2)}) %collective-permute-start.4) | collective-permute-done | bytes 262176 | tf_op jit(solution)/shard_map/ppermute | solution.py:390
  53.9 0.1 shard_map.129
  54.0 0.3 collective-permute-start.6
  54.3 5.1 %collective-permute-start.5 = (f32[40,1024]{1,0:T(8,128)S(1)}, f32[40,1024]{1,0:T(8,128)S(1)}, u32[]{:S(2)}, u32[]{:S(2)}) collective-permute-start(f32[40,1024]{1,0:T(8,128)S(1)} %get-tuple-element.39), channel_id=1, source_target_pairs={{1,0},{2,1},{3,2},{4,3},{5,4},{6,5},{7,6},{8,7},{9,8},{10,9},{11,1... | collective-permute-start | bytes 491528 | tf_op jit(solution)/shard_map/ppermute | solution.py:409
  59.3 2.4 %shard_map.130 = (f32[32,4096]{1,0:T(8,128)S(1)}, f32[32,256]{1,0:T(8,128)}) custom-call(f32[32,4096]{1,0:T(8,128)S(1)} %get-tuple-element.36.own_ref, bf16[192,512]{1,0:T(8,128)(2,1)S(1)} %get-tuple-element.37.band_ref, f32[32,256]{1,0:T(8,128)S(1)} %div.3.coadd_ref), custom_call_target="tpu_custom_call" | custom-call | tf_op jit(solution)/shard_map/pallas_call | solution.py:500
  61.7 1.6 %collective-permute-done.6.above_ref = f32[40,1024]{1,0:T(8,128)S(1)} collective-permute-done((f32[40,1024]{1,0:T(8,128)S(1)}, f32[40,1024]{1,0:T(8,128)S(1)}, u32[]{:S(2)}, u32[]{:S(2)}) %collective-permute-start.6) | collective-permute-done | bytes 163872 | tf_op jit(solution)/shard_map/ppermute | solution.py:405
  63.3 1.5 %shard_map.131.begun_ref = f32[32,4096]{1,0:T(8,128)} custom-call(f32[32,4096]{1,0:T(8,128)S(1)} %get-tuple-element.38.own_ref, f32[40,1024]{1,0:T(8,128)S(1)} %collective-permute-done.6.above_ref, bf16[80,256]{1,0:T(8,128)(2,1)S(1)} %get-tuple-element.42.band_ref), custom_call_target="tpu_custom_call" | custom-call | tf_op jit(solution)/shard_map/pallas_call | solution.py:509
  64.9 0.0 collective-permute-done.5.below_ref
  64.9 1.5 %shard_map.132 = f32[32,4096]{1,0:T(8,128)} custom-call(f32[32,4096]{1,0:T(8,128)S(1)} %get-tuple-element.38.own_ref, f32[40,1024]{1,0:T(8,128)S(1)} %collective-permute-done.5.below_ref, bf16[80,256]{1,0:T(8,128)(2,1)S(1)} %get-tuple-element.40.band_ref, f32[32,4096]{1,0:T(8,128)} %shard_map.131.begun_ref), custom_call_target="tpu_custom_call", output_to_operand_aliasing={{}: (3, {})} | custom-call | tf_op jit(solution)/shard_map/pallas_call | solution.py:512
  (22 shorter events, 0.2 us)
Async XLA Ops:
  0.6 12.8 %copy-start = (f32[9,21,21]{2,1,0:T(8,128)S(1)}, f32[9,21,21]{2,1,0:T(8,128)}, u32[]{:S(2)}) copy-start(f32[9,21,21]{2,1,0:T(8,128)} %param.12) | copy-start | bytes 47632
  0.6 1.1 %copy-start.1 = (f32[1,32,4096]{2,1,0:T(8,128)S(1)}, f32[1,32,4096]{2,1,0:T(8,128)}, u32[]{:S(2)}) copy-start(f32[1,32,4096]{2,1,0:T(8,128)} %param.11) | copy-start | bytes 1572868
  1.8 10.4 %copy-start.3 = (s32[1,32,4096]{2,1,0:T(8,128)S(1)}, s32[1,32,4096]{2,1,0:T(8,128)}, u32[]{:S(2)}) copy-start(s32[1,32,4096]{2,1,0:T(8,128)} %param.20) | copy-start | bytes 1572868
  1.8 21.2 %collective-permute-start = (f32[72,1024]{1,0:T(8,128)S(1)}, f32[72,1024]{1,0:T(8,128)S(1)}, u32[]{:S(2)}, u32[]{:S(2)}) collective-permute-start(f32[72,1024]{1,0:T(8,128)S(1)} %shard_map.124), channel_id=1, source_target_pairs={{0,1},{1,2},{2,3},{3,4},{4,5},{5,6},{6,7},{7,8},{8,9},{9,10},{10,1... | collective-permute-start | bytes 884744 | tf_op jit(solution)/shard_map/ppermute | solution.py:405
  5.4 17.6 %collective-permute-start.1 = (f32[72,1024]{1,0:T(8,128)S(1)}, f32[72,1024]{1,0:T(8,128)S(1)}, u32[]{:S(2)}, u32[]{:S(2)}) collective-permute-start(f32[72,1024]{1,0:T(8,128)S(1)} %shard_map.125), channel_id=1, source_target_pairs={{1,0},{2,1},{3,2},{4,3},{5,4},{6,5},{7,6},{8,7},{9,8},{10,9},{11,1... | collective-permute-start | bytes 884744 | tf_op jit(solution)/shard_map/ppermute | solution.py:409
  10.8 1.3 %copy-start.5 = (s32[1,4096]{1,0:T(1,128)S(1)}, s32[1,4096]{1,0:T(1,128)}, u32[]{:S(2)}) copy-start(s32[1,4096]{1,0:T(1,128)} %starts_ref.3) | copy-start | bytes 49156
  12.4 1.1 %copy-start.9 = (s32[1,32]{1,0:T(1,128)S(1)}, s32[1,32]{1,0:T(1,128)}, u32[]{:S(2)}) copy-start(s32[1,32]{1,0:T(1,128)} %param.14) | copy-start | bytes 388
  12.4 2.3 %collective-permute-start.2 = (f32[8,32,256]{2,1,0:T(8,128)S(1)}, f32[8,32,256]{2,1,0:T(8,128)S(1)}, u32[]{:S(2)}, u32[]{:S(2)}) collective-permute-start(f32[8,32,256]{2,1,0:T(8,128)S(1)} %get-tuple-element.30), channel_id=1, source_target_pairs={{0,16},{16,0},{32,48},{48,32},{64,80},{80,64},{96,112},{112,96},{1... | collective-permute-start | bytes 786440 | tf_op jit(solution)/shard_map/ppermute | solution.py:390
  13.4 0.7 copy-start.8
  14.6 6.5 %copy-start.2 = (f32[1,32,4096]{2,1,0:T(8,128)S(1)}, f32[1,32,4096]{2,1,0:T(8,128)}, u32[]{:S(2)}) copy-start(f32[1,32,4096]{2,1,0:T(8,128)} %param.11) | copy-start | bytes 1572868
  15.4 4.4 %copy-start.7 = (f32[1,8,32]{2,1,0:T(8,128)S(1)}, f32[1,8,32]{2,1,0:T(8,128)}, u32[]{:S(2)}) copy-start(f32[1,8,32]{2,1,0:T(8,128)} %param.15) | copy-start | bytes 3076
  15.4 11.8 %all-to-all-start = ((f32[8,32,256]{2,1,0:T(8,128)}), f32[8,32,256]{2,1,0:T(8,128)S(1)}, u32[]{:S(2)}, u32[]{:S(2)}) async-start(f32[8,32,256]{2,1,0:T(8,128)} %add.51), calls=%async_computation | async-start | bytes 524288 | tf_op jit(solution)/shard_map/all_to_all | solution.py:394
  21.1 1.9 %copy-start.4 = (f32[1,8,4096]{2,1,0:T(8,128)S(1)}, f32[1,8,4096]{2,1,0:T(8,128)}, u32[]{:S(2)}) copy-start(f32[1,8,4096]{2,1,0:T(8,128)} %param.18) | copy-start | bytes 393220
  27.2 1.2 %copy-start.6 = (f32[1,21,21]{2,0,1:T(1,128)S(1)}, f32[1,21,21]{2,0,1:T(1,128)}, u32[]{:S(2)}) copy-start(f32[1,21,21]{2,0,1:T(1,128)} %param.21) | copy-start | bytes 5296
  27.3 2.4 %collective-permute-start.3 = (f32[8,32,256]{2,1,0:T(8,128)S(1)}, f32[8,32,256]{2,1,0:T(8,128)S(1)}, u32[]{:S(2)}, u32[]{:S(2)}) collective-permute-start(f32[8,32,256]{2,1,0:T(8,128)S(1)} %get-tuple-element.31), channel_id=1, source_target_pairs={{0,16},{16,0},{32,48},{48,32},{64,80},{80,64},{96,112},{112,96},{1... | collective-permute-start | bytes 786440 | tf_op jit(solution)/shard_map/ppermute | solution.py:390
  49.6 4.3 %collective-permute-start.4 = (f32[8,32,256]{2,1,0:T(8,128)S(1)}, f32[8,32,256]{2,1,0:T(8,128)S(1)}, u32[]{:S(2)}, u32[]{:S(2)}) collective-permute-start(f32[8,32,256]{2,1,0:T(8,128)S(1)} %all_to_all.16.mine_ref), channel_id=1, source_target_pairs={{0,16},{16,0},{32,48},{48,32},{64,80},{80,64},{96,112},{112,96},{1... | collective-permute-start | bytes 786440 | tf_op jit(solution)/shard_map/ppermute | solution.py:390
  54.0 9.3 %collective-permute-start.6 = (f32[40,1024]{1,0:T(8,128)S(1)}, f32[40,1024]{1,0:T(8,128)S(1)}, u32[]{:S(2)}, u32[]{:S(2)}) collective-permute-start(f32[40,1024]{1,0:T(8,128)S(1)} %get-tuple-element.41), channel_id=1, source_target_pairs={{0,1},{1,2},{2,3},{3,4},{4,5},{5,6},{6,7},{7,8},{8,9},{9,10},{10,1... | collective-permute-start | bytes 491528 | tf_op jit(solution)/shard_map/ppermute | solution.py:405
  54.3 10.6 %collective-permute-start.5 = (f32[40,1024]{1,0:T(8,128)S(1)}, f32[40,1024]{1,0:T(8,128)S(1)}, u32[]{:S(2)}, u32[]{:S(2)}) collective-permute-start(f32[40,1024]{1,0:T(8,128)S(1)} %get-tuple-element.39), channel_id=1, source_target_pairs={{1,0},{2,1},{3,2},{4,3},{5,4},{6,5},{7,6},{8,7},{9,8},{10,9},{11,1... | collective-permute-start | bytes 491528 | tf_op jit(solution)/shard_map/ppermute | solution.py:409
